TPU v7x, 128 devices: a whole 4x4x4 slice. The times are simulated.
128 devices in a mesh: ep: 32 (over x, y, core), ex: 4 (over z).
Axes of the slice: x: 4, y: 4, z: 4, core: 2. Of those that a mesh axis runs over, the one named last changes fastest.
Arguments:
- latent: bfloat16 [16384, 1024], P(('ep', 'ex')), may hold values from -6 to 6
- picks: int32 [16384, 4], P(('ep', 'ex')), may hold values from 0 to 63, all different within a row; in each aligned block of 128 rows (0 to 127, 128 to 255, ...) at most 10 rows name the same one
- gates: float32 [16384, 4], P(('ep', 'ex')), may hold values from 0.1 to 1
- gate_w: bfloat16 [128, 1024, 1024], P(('ep', 'ex')), may hold values from -0.1875 to 0.1875
- up_w: bfloat16 [128, 1024, 1024], P(('ep', 'ex')), may hold values from -0.1875 to 0.1875
- down_w: bfloat16 [128, 1024, 1024], P(('ep', 'ex')), may hold values from -0.125 to 0.125
- cotangent: bfloat16 [16384, 1024], P(('ep', 'ex')), may hold values from -6 to 6
Outputs:
- moe_out: bfloat16 [16384, 1024], P(('ep', 'ex'))
- d_latent: bfloat16 [16384, 1024], P(('ep', 'ex'))
- gate_grad: float32 [16384, 4], P(('ep', 'ex'))
- grad_gate_w: bfloat16 [128, 1024, 1024], P(('ep', 'ex'))
- grad_up_w: bfloat16 [128, 1024, 1024], P(('ep', 'ex'))
- grad_down_w: bfloat16 [128, 1024, 1024], P(('ep', 'ex'))
Inputs may be any that keep to these rules, and one draw needn't show every extreme that they name: Each token names 4 different experts. Within the rows of one device no expert is named by more than 10 picks, a bound that some block reaches.
All inputs are finite; a program needn't handle non-finite values.
Results may differ from a plain program's by a relative error of at most 0.0065.
Values may be sent and summed in bfloat16 or wider, within the bound.
No kernel may reach another device: no remote copies, remote signals or barrier semaphores. Data moves between devices by JAX's collectives and lax.ppermute only.
A program may use at most 128 MiB of HBM per device.

v0:
```python
import jax
import jax.numpy as jnp
from jax import lax
from jax.sharding import PartitionSpec as P


def slots_of(pick_rows, count_experts):
    flat_ids = pick_rows.reshape(-1)
    onehot = (flat_ids[:, None] == jnp.arange(count_experts, dtype=jnp.int32)[None, :]).astype(
        jnp.int32
    )
    before = jnp.cumsum(onehot, axis=0) - onehot
    return jnp.sum(before * onehot, axis=1).reshape(pick_rows.shape)


def silu_parts(pre_gate):
    sigma = jax.nn.sigmoid(pre_gate)
    return (pre_gate * sigma, sigma * (1.0 + pre_gate * (1.0 - sigma)))


def to_experts(blocks):
    return lax.all_to_all(blocks, ("ep", "ex"), split_axis=0, concat_axis=0, tiled=True)


def to_sources(blocks):
    return lax.all_to_all(blocks, ("ep", "ex"), split_axis=0, concat_axis=0, tiled=True)


def join_halves(returned, experts, capacity, width):
    paired = returned.reshape(experts, 2, capacity, width)
    return (paired[:, 0] + paired[:, 1]).astype(jnp.bfloat16).reshape(experts * capacity, width)


def shards(latent, picks, gates, gate_w, up_w, down_w, cotangent):
    tok_rows, width = latent.shape
    top_count = picks.shape[1]
    devices = lax.axis_size("ep") * lax.axis_size("ex")
    experts = devices // 2
    capacity = max(2, (5 * tok_rows * top_count + 4 * experts - 1) // (4 * experts))
    slot_ids = slots_of(picks, experts)
    target = picks * capacity + slot_ids
    positions = jnp.arange(experts * capacity, dtype=jnp.int32)
    hits = target.reshape(-1)[None, :] == positions[:, None]
    pick_table = hits.astype(jnp.bfloat16)
    token_table = jnp.any(hits.reshape(experts * capacity, tok_rows, top_count), axis=2).astype(
        jnp.bfloat16
    )
    w_gate = gate_w[0]
    w_up = up_w[0]
    w_down = down_w[0]
    sent = jnp.dot(token_table, latent, preferred_element_type=jnp.float32).astype(jnp.bfloat16)
    weighted = (gates[..., None] * cotangent[:, None, :].astype(jnp.float32)).astype(jnp.bfloat16)
    d_sent = jnp.dot(
        pick_table, weighted.reshape(-1, width), preferred_element_type=jnp.float32
    ).astype(jnp.bfloat16)
    joined = jnp.concatenate([sent, d_sent], axis=1).reshape(experts, 1, capacity, 2 * width)
    doubled = jnp.broadcast_to(joined, (experts, 2, capacity, 2 * width)).reshape(
        devices, capacity, 2 * width
    )
    moved = to_experts(doubled)
    arrived = moved[:, :, :width].reshape(-1, width)
    d_arrived = moved[:, :, width:].reshape(-1, width)
    pre_gate = jnp.dot(arrived, w_gate, preferred_element_type=jnp.float32)
    pre_up = jnp.dot(arrived, w_up, preferred_element_type=jnp.float32)
    active, slope = silu_parts(pre_gate)
    hidden = (active * pre_up).astype(jnp.bfloat16)
    partial_out = jnp.dot(hidden, w_down, preferred_element_type=jnp.float32)
    returned = to_sources(partial_out.reshape(devices, capacity, width))
    expert_rows = join_halves(returned, experts, capacity, width)
    picked = expert_rows[target].astype(jnp.float32)
    moe_out = jnp.sum(gates[..., None] * picked, axis=1).astype(jnp.bfloat16)
    gate_grad = jnp.sum(cotangent[:, None, :].astype(jnp.float32) * picked, axis=-1)
    d_hidden = jnp.dot(d_arrived, w_down.T, preferred_element_type=jnp.float32)
    grad_down = jnp.dot(hidden.T, d_arrived, preferred_element_type=jnp.float32).astype(
        jnp.bfloat16
    )
    d_pre_gate = (d_hidden * pre_up * slope).astype(jnp.bfloat16)
    d_pre_up = (d_hidden * active).astype(jnp.bfloat16)
    grad_gate = jnp.dot(arrived.T, d_pre_gate, preferred_element_type=jnp.float32).astype(
        jnp.bfloat16
    )
    grad_up = jnp.dot(arrived.T, d_pre_up, preferred_element_type=jnp.float32).astype(jnp.bfloat16)
    partial_rows = jnp.dot(d_pre_gate, w_gate.T, preferred_element_type=jnp.float32) + jnp.dot(
        d_pre_up, w_up.T, preferred_element_type=jnp.float32
    )
    d_back = to_sources(partial_rows.reshape(devices, capacity, width))
    d_rows = join_halves(d_back, experts, capacity, width)
    d_latent = jnp.sum(d_rows[target].astype(jnp.float32), axis=1).astype(jnp.bfloat16)
    return (moe_out, d_latent, gate_grad, grad_gate[None], grad_up[None], grad_down[None])


def solution(mesh):
    return jax.shard_map(
        shards,
        mesh=mesh,
        in_specs=(
            P(("ep", "ex"), None),
            P(("ep", "ex"), None),
            P(("ep", "ex"), None),
            P(("ep", "ex"), None, None),
            P(("ep", "ex"), None, None),
            P(("ep", "ex"), None, None),
            P(("ep", "ex"), None),
        ),
        out_specs=(
            P(("ep", "ex"), None),
            P(("ep", "ex"), None),
            P(("ep", "ex"), None),
            P(("ep", "ex"), None, None),
            P(("ep", "ex"), None, None),
            P(("ep", "ex"), None, None),
        ),
        check_vma=False,
    )
```

profile of v0, /device:TPU:0, one launch (start us, length us, event | category | flops | bytes accessed | tf_op | source)
XLA Modules:
  0.0 434.3 jit_solution(1550022511957409347)
XLA Ops:
  0.6 0.0 copy-start
  0.6 0.9 copy.61
  1.6 0.1 eq.51
  1.7 0.1 eq.47
  1.8 1.2 reduce-window.6
  3.0 0.2 slice_reduce_fusion
  3.3 0.1 fusion.22
  3.4 0.1 reshape.81
  3.5 0.1 copy.64
  3.6 0.7 compare_select_fusion
  4.3 0.1 copy.65
  4.4 0.2 fusion.17
  4.6 0.8 copy.60
  5.4 0.1 mul.66
  5.5 0.1 eq.58
  5.6 2.8 mul.68
  8.4 3.0 mul.69
  11.4 0.0 copy-done.6
  11.4 0.5 convolution_convert_fusion.1
  11.9 2.5 convolution_convert_fusion
  14.4 1.8 pad_maximum_fusion
  16.2 5.4 %broadcast_in_dim.12 = bf16[64,10,2048]{2,1,0:T(8,128)(2,1)} reshape(bf16[640,2048]{1,0:T(8,128)(2,1)} %pad_maximum_fusion) | data formatting | bytes 5242880 | tf_op jit(solution)/shard_map/broadcast_in_dim | solution.py:57
  21.5 6.8 %broadcast_in_dim.13 = bf16[64,2,10,2048]{3,2,1,0:T(8,128)(2,1)} broadcast(bf16[64,10,2048]{2,1,0:T(8,128)(2,1)} %broadcast_in_dim.12), dimensions={0,2,3} | broadcast | bytes 7864320 | tf_op jit(solution)/shard_map/broadcast_in_dim | solution.py:57
  28.3 109.1 %all_to_all.15 = bf16[128,10,2048]{2,1,0:T(8,128)(2,1)S(1)} all-to-all(bf16[128,10,2048]{2,1,0:T(8,128)(2,1)} %bitcast.83), channel_id=1, replica_groups=mesh['ep'=32,'ex'=4] {'ep','ex'}, dimensions={0} | all-to-all | bytes 10485760 | tf_op jit(solution)/shard_map/all_to_all | solution.py:22
  137.4 3.7 fusion.24
  141.0 6.1 %reshape.85 = bf16[1280,1024]{1,0:T(8,128)(2,1)} reshape(bf16[128,10,1024]{2,1,0:T(8,128)(2,1)} %get-tuple-element.31) | data formatting | bytes 5242880 | tf_op jit(solution)/shard_map/reshape | solution.py:62
  147.2 6.1 %reshape.83 = bf16[1280,1024]{1,0:T(8,128)(2,1)} reshape(bf16[128,10,1024]{2,1,0:T(8,128)(2,1)} %get-tuple-element.32) | data formatting | bytes 5242880 | tf_op jit(solution)/shard_map/reshape | solution.py:61
  153.3 5.4 %fusion.11 = f32[1280,1024]{1,0:T(8,128)S(1)} fusion(bf16[1280,1024]{1,0:T(8,128)(2,1)} %reshape.83, bf16[1,1024,1024]{2,1,0:T(8,128)(2,1)} %param.11), kind=kOutput, calls=%fused_computation.23 | convolution fusion | flops 2684354560 | bytes 9961472 | tf_op jit(solution)/shard_map/dot_general | solution.py:64
  158.8 0.0 copy-done.2
  158.8 0.0 copy-done.7
  158.8 0.0 copy-start.4
  158.8 2.9 fusion.15
  161.7 0.0 copy-done
  161.7 0.0 copy-done.4
  161.8 6.6 %multiply_convert_fusion = (bf16[1280,1024]{1,0:T(8,128)(2,1)S(1)}, bf16[1280,1024]{1,0:T(8,128)(2,1)S(1)}, bf16[1280,1024]{1,0:T(8,128)(2,1)}) fusion(f32[1280,1024]{1,0:T(8,128)S(1)} %fusion.15, f32[1280,1024]{1,0:T(8,128)S(1)} %fusion.11, bf16[1280,1024]{1,0:T(8,128)(2,1)S(1)} %copy-done.4, bf16[1,1024,1024]{2,1,0:T(8,128)(2,1)S(1)} %copy-done), kind=kOutput, calls=%fused_computation.2 | convolution fusion | flops 2704015360 | bytes 23068672 | tf_op jit(solution)/shard_map/dot_general | solution.py:73
  168.4 2.9 fusion.13
  171.3 0.0 copy-done.11
  171.3 0.2 copy-done.8
  171.5 5.3 %convolution_add_fusion = f32[1280,1024]{1,0:T(8,128)} fusion(f32[1280,1024]{1,0:T(8,128)S(1)} %fusion.13, bf16[1280,1024]{1,0:T(8,128)(2,1)S(1)} %get-tuple-element.28, bf16[1,1024,1024]{2,1,0:T(8,128)(2,1)S(1)} %copy-done.8), kind=kOutput, calls=%fused_computation.7 | convolution fusion | flops 2685665280 | bytes 15204352 | tf_op jit(solution)/shard_map/dot_general | solution.py:83
  176.8 7.3 %reshape.86 = f32[128,10,1024]{2,1,0:T(8,128)} reshape(f32[1280,1024]{1,0:T(8,128)} %convolution_add_fusion) | data formatting | bytes 10485760 | tf_op jit(solution)/shard_map/reshape | solution.py:86
  184.1 5.9 %all-to-all-start.2 = ((f32[128,10,1024]{2,1,0:T(8,128)}), f32[128,10,1024]{2,1,0:T(8,128)}, u32[]{:S(2)}, u32[]{:S(2)}) async-start(f32[128,10,1024]{2,1,0:T(8,128)} %reshape.86), calls=%async_computation.2 | async-start | bytes 16777216 | tf_op jit(solution)/shard_map/all_to_all | solution.py:26
  190.0 6.0 %dot_general.39 = bf16[128,10,1024]{2,1,0:T(8,128)(2,1)} reshape(bf16[1280,1024]{1,0:T(8,128)(2,1)} %get-tuple-element.30) | data formatting | bytes 5242880 | tf_op jit(solution)/shard_map/dot_general | solution.py:67
  196.1 5.7 %fusion.5 = f32[128,10,1024]{2,0,1:T(8,128)S(1)} fusion(bf16[128,10,1024]{2,1,0:T(8,128)(2,1)} %dot_general.39, bf16[1,1024,1024]{2,1,0:T(8,128)(2,1)S(1)} %copy-done), kind=kOutput, calls=%fused_computation.17 | convolution fusion | flops 2684354560 | bytes 9961472 | tf_op jit(solution)/shard_map/dot_general | solution.py:67
  201.8 6.4 %copy.68 = f32[128,10,1024]{2,1,0:T(8,128)} copy(f32[128,10,1024]{2,0,1:T(8,128)S(1)} %fusion.5) | data formatting | bytes 10485760 | tf_op jit(solution)/shard_map/dot_general | solution.py:67
  208.2 89.9 %all-to-all-done.2 = f32[128,10,1024]{2,1,0:T(8,128)} async-done(((f32[128,10,1024]{2,1,0:T(8,128)}), f32[128,10,1024]{2,1,0:T(8,128)}, u32[]{:S(2)}, u32[]{:S(2)}) %all-to-all-start.2) | async-done | bytes 5242912 | tf_op jit(solution)/shard_map/all_to_all | solution.py:26
  298.1 7.2 %all-to-all-start.1 = ((f32[128,10,1024]{2,1,0:T(8,128)}), f32[128,10,1024]{2,1,0:T(8,128)}, u32[]{:S(2)}, u32[]{:S(2)}) async-start(f32[128,10,1024]{2,1,0:T(8,128)} %copy.68), calls=%async_computation.1 | async-start | bytes 16777216 | tf_op jit(solution)/shard_map/all_to_all | solution.py:26
  305.4 0.9 convert_element_type.67
  306.2 0.1 copy.71
  306.3 0.1 reshape.90
  306.5 6.9 %convert_bitcast_fusion = bf16[1,1024,1024]{2,1,0:T(8,128)(2,1)} fusion(bf16[1280,1024]{1,0:T(8,128)(2,1)} %get-tuple-element.30, bf16[1280,1024]{1,0:T(8,128)(2,1)} %reshape.85), kind=kOutput, calls=%fused_computation.29 | convolution fusion | flops 2685403136 | bytes 7340032 | tf_op jit(solution)/shard_map/dot_general | solution.py:74
  313.4 4.1 convert_bitcast_fusion.1
  317.5 4.1 convert_bitcast_fusion.2
  321.6 5.6 %fusion.2 = bf16[64,1,10,1024]{3,2,0,1:T(8,128)(2,1)} fusion(f32[64,2,10,1024]{3,2,1,0:T(8,128)} %bitcast.7), kind=kLoop, calls=%fused_computation.10 | loop fusion | flops 1310720 | bytes 6553600 | tf_op jit(solution)/shard_map/convert_element_type | solution.py:31
  327.3 2.6 convert_element_type.78
  329.8 2.8 gather_fusion.1
  332.6 2.3 reshape.101
  334.9 78.2 %all-to-all-done.1 = f32[128,10,1024]{2,1,0:T(8,128)} async-done(((f32[128,10,1024]{2,1,0:T(8,128)}), f32[128,10,1024]{2,1,0:T(8,128)}, u32[]{:S(2)}, u32[]{:S(2)}) %all-to-all-start.1) | async-done | bytes 5242912 | tf_op jit(solution)/shard_map/all_to_all | solution.py:26
  413.1 5.6 %fusion.4 = bf16[64,1,10,1024]{3,2,0,1:T(8,128)(2,1)} fusion(f32[64,2,10,1024]{3,2,1,0:T(8,128)} %bitcast.6), kind=kLoop, calls=%fused_computation.14 | loop fusion | flops 1310720 | bytes 6553600 | tf_op jit(solution)/shard_map/convert_element_type | solution.py:31
  418.7 2.6 convert_element_type.72
  421.2 2.8 gather_fusion
  424.0 3.0 reshape.108
  427.1 4.2 multiply_reduce_fusion
  431.3 0.7 copy.74
  432.0 2.1 reduce_sum.41
  (21 shorter events, 0.1 us)
Async XLA Ops:
  0.6 161.1 %copy-start = (bf16[1,1024,1024]{2,1,0:T(8,128)(2,1)S(1)}, bf16[1,1024,1024]{2,1,0:T(8,128)(2,1)}, u32[]{:S(2)}) copy-start(bf16[1,1024,1024]{2,1,0:T(8,128)(2,1)} %param.12) | copy-start | bytes 6291460
  8.4 3.0 copy-start.6
  153.3 5.5 %copy-start.2 = (bf16[1280,1024]{1,0:T(8,128)(2,1)S(1)}, bf16[1280,1024]{1,0:T(8,128)(2,1)}, u32[]{:S(2)}) copy-start(bf16[1280,1024]{1,0:T(8,128)(2,1)} %reshape.83) | copy-start | bytes 7864324
  153.3 5.5 %copy-start.7 = (bf16[1,1024,1024]{2,1,0:T(8,128)(2,1)S(1)}, bf16[1,1024,1024]{2,1,0:T(8,128)(2,1)}, u32[]{:S(2)}) copy-start(bf16[1,1024,1024]{2,1,0:T(8,128)(2,1)} %param.10) | copy-start | bytes 6291460
  158.8 3.0 copy-start.4
  168.4 3.0 copy-start.11
  168.4 3.0 copy-start.9
  168.4 3.1 copy-start.8
  184.1 114.0 %all-to-all-start.2 = ((f32[128,10,1024]{2,1,0:T(8,128)}), f32[128,10,1024]{2,1,0:T(8,128)}, u32[]{:S(2)}, u32[]{:S(2)}) async-start(f32[128,10,1024]{2,1,0:T(8,128)} %reshape.86), calls=%async_computation.2 | async-start | bytes 16777216 | tf_op jit(solution)/shard_map/all_to_all | solution.py:26
  208.2 97.2 %copy-start.5 = (bf16[128,1024]{1,0:T(8,128)(2,1)S(1)}, bf16[128,1024]{1,0:T(8,128)(2,1)}, u32[]{:S(2)}) copy-start(bf16[128,1024]{1,0:T(8,128)(2,1)} %param.13) | copy-start | bytes 786436
  298.1 114.9 %all-to-all-start.1 = ((f32[128,10,1024]{2,1,0:T(8,128)}), f32[128,10,1024]{2,1,0:T(8,128)}, u32[]{:S(2)}, u32[]{:S(2)}) async-start(f32[128,10,1024]{2,1,0:T(8,128)} %copy.68), calls=%async_computation.1 | async-start | bytes 16777216 | tf_op jit(solution)/shard_map/all_to_all | solution.py:26
  306.5 7.0 %copy-start.3 = (bf16[1280,1024]{1,0:T(8,128)(2,1)S(1)}, bf16[1280,1024]{1,0:T(8,128)(2,1)}, u32[]{:S(2)}) copy-start(bf16[1280,1024]{1,0:T(8,128)(2,1)} %reshape.83) | copy-start | bytes 7864324
  306.5 7.0 %copy-start.10 = (bf16[1280,1024]{1,0:T(8,128)(2,1)S(1)}, bf16[1280,1024]{1,0:T(8,128)(2,1)}, u32[]{:S(2)}) copy-start(bf16[1280,1024]{1,0:T(8,128)(2,1)} %copy-done.9) | copy-start | bytes 7864324
  313.4 4.1 copy-start.12
  424.0 7.9 %copy-start.1 = (bf16[128,4,1024]{2,1,0:T(4,128)(2,1)S(1)}, bf16[128,4,1024]{2,1,0:T(4,128)(2,1)}, u32[]{:S(2)}) copy-start(bf16[128,4,1024]{2,1,0:T(4,128)(2,1)} %reshape.101) | copy-start | bytes 3145732
where the time goes:
time: 439 us; the launch traced here: 434 us
  waiting for transfers between devices  168 us (38%)
  blocking collectives  109 us (25%)
  local copies, waits for them, and re-layouts  73.3 us (17%)
  matrix products  47.1 us (11%)
  other arithmetic  22.4 us (5%)
  starting transfers between devices  13.2 us (3%)
    all_to_all x2, waiting for transfers between devices, to_sources(): lax.all_to_all(blocks, ('ep', 'ex'), split_axis=0, concat_axis=0, tiled=T...  168 us
    all_to_all x1, blocking collectives, to_experts(): lax.all_to_all(blocks, ('ep', 'ex'), split_axis=0, concat_axis=0, tiled=T...  109 us
    all_to_all x2, starting transfers between devices, to_sources(): lax.all_to_all(blocks, ('ep', 'ex'), split_axis=0, concat_axis=0, tiled=T...  13.2 us
    dot_general x2, local copies, waits for them, and re-layouts, shards(): partial_out = jnp.dot(hidden, w_down, preferred_element_type=jnp.float32)  12.4 us
    broadcast_in_dim x2, local copies, waits for them, and re-layouts, shards(): jnp.broadcast_to(joined, (experts, 2, capacity, 2 * width))  12.1 us
    convert_element_type x2, other arithmetic, join_halves(): (paired[:, 0] + paired[:, 1]).astype(jnp.bfloat16)  11.2 us
  transfers between devices with their start and end apart: 2, of which 2 were waited for; matrix products, arithmetic and copies ran while one was open for 11% of the time, Pallas kernels for 0%

commit v1 on v0

v1 whole, which is shorter than its diff:
```python
import functools

import jax
import jax.numpy as jnp
import numpy as np
from jax import lax
from jax.experimental import pallas as pl
from jax.experimental.pallas import tpu as pltpu
from jax.sharding import PartitionSpec as P

BF16 = jnp.bfloat16
F32 = jnp.float32
AXES = ("ep", "ex")
TOPK = 4
CAP = 10
PIECES = 4
GROUP = 8
VMEM_LIMIT = 48 * 1024 * 1024
STEPS = 4


def dot(a, b, ca=1, cb=0):
    return lax.dot_general(a, b, (((ca,), (cb,)), ((), ())), preferred_element_type=F32)


def one_hot(mask):
    return jnp.where(mask, 1.0, 0.0).astype(BF16)


def returned_codes(experts):
    slots = np.arange(experts * CAP, dtype=np.int32).reshape(experts, 1, CAP)
    return np.broadcast_to(slots, (experts, 2, CAP)).reshape(STEPS, 1, experts * 2 * CAP // STEPS)


def unpack_table():
    size = GROUP * PIECES * CAP
    table = np.zeros((size, size), np.float32)
    for block in range(GROUP):
        for piece in range(PIECES):
            for slot in range(CAP):
                table[(piece * GROUP + block) * CAP + slot, (block * PIECES + piece) * CAP + slot] = 1
    return table


def double_table():
    table = unpack_table().T.reshape(GROUP, 1, PIECES * CAP, -1)
    return np.broadcast_to(table, (GROUP, 2) + table.shape[2:]).reshape(-1, table.shape[-1])


def call(kernel, grid, in_specs, out_specs, out_shape, scratch=(), flops=0, moved=0):
    return pl.pallas_call(
        kernel,
        grid=grid,
        in_specs=in_specs,
        out_specs=out_specs,
        out_shape=out_shape,
        scratch_shapes=list(scratch),
        compiler_params=pltpu.CompilerParams(vmem_limit_bytes=VMEM_LIMIT),
        cost_estimate=pl.CostEstimate(flops=flops, bytes_accessed=moved, transcendentals=0),
    )


def fixed(shape):
    return pl.BlockSpec(shape, lambda i: (0,) * len(shape))


def rows_of(count, width):
    return pl.BlockSpec((count, width), lambda i: (i, 0))


def pieces(rows):
    width = rows.shape[1] // PIECES
    return jnp.concatenate([rows[:, p * width : (p + 1) * width] for p in range(PIECES)], axis=0)


def send(rows, table, sent_ref):
    inner = GROUP * CAP
    size = table.shape[0]
    for group in range(rows.shape[0] // inner):
        part = dot(table[...], pieces(rows[group * inner : (group + 1) * inner, :]))
        sent_ref[group * size : (group + 1) * size, :] = part.astype(BF16)


def repack(rows, table, back_ref):
    inner = GROUP * CAP
    size = table.shape[0]
    for group in range(rows.shape[0] // inner):
        part = dot(table[...], pieces(rows[group * inner : (group + 1) * inner, :]))
        back_ref[group * size : (group + 1) * size, :] = part.astype(BF16)


def unpack(back_ref, table):
    size = table.shape[0]
    inner = GROUP * CAP
    groups = []
    for group in range(back_ref.shape[0] // size):
        mixed = dot(table[...], back_ref[group * size : (group + 1) * size, :]).astype(BF16)
        groups.append(jnp.concatenate([mixed[p * inner : (p + 1) * inner, :] for p in range(PIECES)], axis=1))
    return jnp.concatenate(groups, axis=0)


def route_kernel(picks_ref, latent_ref, table, target_ref, sent_ref):
    picks = picks_ref[...]
    tokens = picks.shape[0]
    lane = lax.broadcasted_iota(jnp.int32, (tokens, 128), 1)
    named = [picks[:, k : k + 1] == lane for k in range(TOPK)]
    some = functools.reduce(jnp.logical_or, named)
    now = lax.broadcasted_iota(jnp.int32, (tokens, tokens), 0)
    other = lax.broadcasted_iota(jnp.int32, (tokens, tokens), 1)
    before = dot(one_hot(other < now), one_hot(some))
    slots = sent_ref.shape[0] // (2 * PIECES)
    codes = lax.broadcasted_iota(jnp.int32, (1, slots), 1)
    hit = None
    for k in range(TOPK):
        slot = jnp.sum(jnp.where(named[k], before, 0.0), axis=1, keepdims=True)
        target = picks[:, k : k + 1] * CAP + slot.astype(jnp.int32)
        target_ref[:, k : k + 1] = target
        here = target == codes
        hit = here if hit is None else hit | here
    send(dot(one_hot(hit), latent_ref[...], 0, 0).astype(BF16), table, sent_ref)


def pack_kernel(target_ref, gates_ref, cotangent_ref, table, sent_ref):
    cotangent = cotangent_ref[...].astype(F32)
    weighted = jnp.concatenate([(gates_ref[:, k : k + 1] * cotangent).astype(BF16) for k in range(TOPK)], axis=0)
    slots = sent_ref.shape[0] // (2 * PIECES)
    codes = lax.broadcasted_iota(jnp.int32, (1, slots), 1)
    hits = jnp.concatenate([one_hot(target_ref[:, k : k + 1] == codes) for k in range(TOPK)], axis=0)
    send(dot(hits, weighted, 0, 0).astype(BF16), table, sent_ref)


def forward_kernel(moved_ref, w_gate, w_up, w_down, apart, together, rows_ref, active_ref, slope_ref, hidden_ref, back_ref):
    rows = unpack(moved_ref, apart)
    rows_ref[...] = rows
    pre_gate = dot(rows, w_gate[...])
    pre_up = dot(rows, w_up[...])
    sigma = jax.nn.sigmoid(pre_gate)
    active = pre_gate * sigma
    hidden = (active * pre_up).astype(BF16)
    active_ref[...] = active
    slope_ref[...] = pre_up * (sigma * (1.0 + pre_gate * (1.0 - sigma)))
    hidden_ref[...] = hidden
    repack(dot(hidden, w_down[...]).astype(BF16), together, back_ref)


def backward_kernel(moved_ref, active_ref, slope_ref, w_gate, w_up, w_down, apart, together, rows_ref, d_gate_ref, d_up_ref, back_ref):
    rows = unpack(moved_ref, apart)
    rows_ref[...] = rows
    d_hidden = dot(rows, w_down[...], 1, 1)
    d_gate = (d_hidden * slope_ref[...]).astype(BF16)
    d_up = (d_hidden * active_ref[...]).astype(BF16)
    d_gate_ref[...] = d_gate
    d_up_ref[...] = d_up
    d_rows = dot(d_gate, w_gate[...], 1, 1) + dot(d_up, w_up[...], 1, 1)
    repack(d_rows.astype(BF16), together, back_ref)


def moe_kernel(back_ref, codes_ref, target_ref, gates_ref, cotangent_ref, table, moe_ref, gate_grad_ref, picked):
    step = pl.program_id(0)
    tokens = target_ref.shape[0]
    codes = codes_ref[0]
    hits = jnp.concatenate([one_hot(target_ref[:, k : k + 1] == codes) for k in range(TOPK)], axis=0)
    part = dot(hits, unpack(back_ref, table))

    @pl.when(step == 0)
    def _():
        picked[...] = part

    @pl.when(step > 0)
    def _():
        picked[...] += part

    @pl.when(step == pl.num_programs(0) - 1)
    def _():
        cotangent = cotangent_ref[...].astype(F32)
        total = None
        for k in range(TOPK):
            mine = picked[k * tokens : (k + 1) * tokens, :]
            gate_grad_ref[:, k : k + 1] = jnp.sum(cotangent * mine, axis=1, keepdims=True)
            term = gates_ref[:, k : k + 1] * mine
            total = term if total is None else total + term
        moe_ref[...] = total.astype(BF16)


def latent_kernel(back_ref, codes_ref, target_ref, table, out_ref, total):
    step = pl.program_id(0)
    codes = codes_ref[0]
    hit = functools.reduce(jnp.logical_or, [target_ref[:, k : k + 1] == codes for k in range(TOPK)])
    part = dot(one_hot(hit), unpack(back_ref, table))

    @pl.when(step == 0)
    def _():
        total[...] = part

    @pl.when(step > 0)
    def _():
        total[...] += part

    @pl.when(step == pl.num_programs(0) - 1)
    def _():
        out_ref[...] = total[...].astype(BF16)


def exchange(blocks, devices):
    shape = blocks.shape
    blocks = blocks.reshape(devices, shape[0] // devices, shape[1])
    moved = lax.all_to_all(blocks, AXES, split_axis=0, concat_axis=0, tiled=True).reshape(shape)
    return pltpu.with_memory_space_constraint(moved, pltpu.HBM)


def shards(latent, picks, gates, gate_w, up_w, down_w, cotangent):
    tokens, width = latent.shape
    devices = lax.axis_size("ep") * lax.axis_size("ex")
    experts = devices // 2
    w_gate, w_up, w_down = gate_w[0], up_w[0], down_w[0]
    hidden_width = w_gate.shape[1]
    total_rows, back_rows = devices * CAP, devices * CAP * PIECES
    piece = width // PIECES
    back_shape = pltpu.HBM((back_rows, piece), BF16)
    apart, together, doubled = [jnp.asarray(t, BF16) for t in (unpack_table(), unpack_table().T, double_table())]
    codes = jnp.asarray(returned_codes(experts))

    target, sent = call(
        route_kernel,
        (1,),
        [fixed(picks.shape), fixed(latent.shape), fixed(doubled.shape)],
        [fixed(picks.shape), fixed(back_shape.shape)],
        [jax.ShapeDtypeStruct(picks.shape, jnp.int32), back_shape],
        flops=2 * total_rows * tokens * width,
        moved=2 * (total_rows + tokens) * width,
    )(picks, latent, doubled)
    moved = exchange(sent, devices)
    d_sent = call(
        pack_kernel,
        (1,),
        [fixed(picks.shape), fixed(gates.shape), fixed(cotangent.shape), fixed(doubled.shape)],
        fixed(back_shape.shape),
        back_shape,
        flops=2 * total_rows * tokens * TOPK * width,
        moved=2 * (total_rows + tokens) * width,
    )(target, gates, cotangent, doubled)
    d_moved = exchange(d_sent, devices)

    block = total_rows // STEPS
    weights = [fixed(w_gate.shape), fixed(w_up.shape), fixed(w_down.shape), fixed(apart.shape), fixed(apart.shape)]
    row_spec, hidden_spec = rows_of(block, width), rows_of(block, hidden_width)
    back_spec = rows_of(back_rows // STEPS, piece)
    row_shape = jax.ShapeDtypeStruct((total_rows, width), BF16)
    hidden_shape = jax.ShapeDtypeStruct((total_rows, hidden_width), BF16)
    wide_shape = jax.ShapeDtypeStruct((total_rows, hidden_width), F32)
    rows, active, slope, hidden, back = call(
        forward_kernel,
        (STEPS,),
        [back_spec] + weights,
        [row_spec, hidden_spec, hidden_spec, hidden_spec, back_spec],
        [row_shape, wide_shape, wide_shape, hidden_shape, back_shape],
        flops=6 * total_rows * width * hidden_width,
        moved=6 * width * hidden_width + 18 * total_rows * width,
    )(moved, w_gate, w_up, w_down, apart, together)
    returned = exchange(back, devices)
    d_rows, d_gate, d_up, d_back = call(
        backward_kernel,
        (STEPS,),
        [back_spec, hidden_spec, hidden_spec] + weights,
        [row_spec, hidden_spec, hidden_spec, back_spec],
        [row_shape, hidden_shape, hidden_shape, back_shape],
        flops=6 * total_rows * width * hidden_width,
        moved=6 * width * hidden_width + 18 * total_rows * width,
    )(d_moved, active, slope, w_gate, w_up, w_down, apart, together)
    d_returned = exchange(d_back, devices)

    grad_gate = jnp.dot(rows.T, d_gate, preferred_element_type=F32).astype(BF16)
    grad_up = jnp.dot(rows.T, d_up, preferred_element_type=F32).astype(BF16)
    grad_down = jnp.dot(hidden.T, d_rows, preferred_element_type=F32).astype(BF16)

    codes_spec = pl.BlockSpec((1,) + codes.shape[1:], lambda i: (i, 0, 0))
    moe_out, gate_grad = call(
        moe_kernel,
        (STEPS,),
        [back_spec, codes_spec, fixed(picks.shape), fixed(gates.shape), fixed(cotangent.shape), fixed(apart.shape)],
        [fixed(latent.shape), fixed(gates.shape)],
        [jax.ShapeDtypeStruct(latent.shape, BF16), jax.ShapeDtypeStruct(gates.shape, F32)],
        [pltpu.VMEM((TOPK * tokens, width), F32)],
        flops=2 * total_rows * tokens * TOPK * width,
        moved=2 * back_rows * piece,
    )(returned, codes, target, gates, cotangent, apart)
    d_latent = call(
        latent_kernel,
        (STEPS,),
        [back_spec, codes_spec, fixed(picks.shape), fixed(apart.shape)],
        fixed(latent.shape),
        jax.ShapeDtypeStruct(latent.shape, BF16),
        [pltpu.VMEM((tokens, width), F32)],
        flops=2 * total_rows * tokens * width,
        moved=2 * back_rows * piece,
    )(d_returned, codes, target, apart)
    return (moe_out, d_latent, gate_grad, grad_gate[None], grad_up[None], grad_down[None])


def solution(mesh):
    rows, blocks = P(AXES, None), P(AXES, None, None)
    return jax.shard_map(
        shards,
        mesh=mesh,
        in_specs=(rows, rows, rows, blocks, blocks, blocks, rows),
        out_specs=(rows, rows, rows, blocks, blocks, blocks),
        check_vma=False,
    )
```

time: 439 us -> 185 us (0.42)
  blocking collectives: 109 us -> 0 us
  waiting for transfers between devices: 168 us -> 80.3 us
  local copies, waits for them, and re-layouts: 73.3 us -> 6.75 us
  Pallas kernels: 0 us -> 52 us
  matrix products: 47.1 us -> 14.2 us
  other arithmetic: 22.4 us -> 0 us
  starting transfers between devices: 13.2 us -> 29.3 us
    all_to_all x1 -> x0, blocking collectives: 109 us -> none  [to_experts(): lax.all_to_all(blocks, ('ep', 'ex'), split_axis=0, concat_axis=0, tiled=T...]
    all_to_all x2 -> x4, waiting for transfers between devices: 168 us -> 80.3 us  [exchange(): lax.all_to_all(blocks, AXES, split_axis=0, concat_axis=0, tiled=True)]
    pallas_call x0 -> x6, Pallas kernels: none -> 52 us  [the longest x1 16 us: shards(): call(backward_kernel, (STEPS,), [back_spec, hidden_spec, hidden_spec] + w...]
    dot_general x11 -> x3, matrix products: 47.1 us -> 14.2 us  [the longest x1 6.02 us: shards(): grad_gate = jnp.dot(rows.T, d_gate, preferred_element_type=F32).astype(BF16)]
    reshape x5 -> x0, local copies, waits for them, and re-layouts: 19.7 us -> none  [the longest x1 7.3 us: shards(): d_back = to_sources(partial_rows.reshape(devices, capacity, width))]
    all_to_all x2 -> x4, starting transfers between devices: 13.2 us -> 29.3 us  [exchange(): lax.all_to_all(blocks, AXES, split_axis=0, concat_axis=0, tiled=True)]
    dot_general x2 -> x0, local copies, waits for them, and re-layouts: 12.4 us -> none  [shards(): partial_out = jnp.dot(hidden, w_down, preferred_element_type=jnp.float32)]
    broadcast_in_dim x3 -> x0, local copies, waits for them, and re-layouts: 12.2 us -> none  [the longest x2 12.1 us: shards(): jnp.broadcast_to(joined, (experts, 2, capacity, 2 * width))]
  transfers between devices with their start and end apart: 2 -> 4, of which waited for: 2 -> 4; matrix products, arithmetic and copies ran while one was open for 11% -> 8% of each run, Pallas kernels for 0% -> 23%
where the time goes in v1:
time: 185 us; the launch traced here: 183 us
  waiting for transfers between devices  80.3 us (43%)
  Pallas kernels  52 us (28%)
  starting transfers between devices  29.3 us (16%)
  matrix products  14.2 us (8%)
  local copies, waits for them, and re-layouts  6.75 us (4%)
    all_to_all x4, waiting for transfers between devices, exchange(): lax.all_to_all(blocks, AXES, split_axis=0, concat_axis=0, tiled=True)  80.3 us
    all_to_all x4, starting transfers between devices, exchange(): lax.all_to_all(blocks, AXES, split_axis=0, concat_axis=0, tiled=True)  29.3 us
    pallas_call x1, Pallas kernels, shards(): call(backward_kernel, (STEPS,), [back_spec, hidden_spec, hidden_spec] + w...  16 us
    pallas_call x1, Pallas kernels, shards(): call(forward_kernel, (STEPS,), [back_spec] + weights, [row_spec, hidden_s...  15.3 us
    pallas_call x1, Pallas kernels, shards(): call(moe_kernel, (STEPS,), [back_spec, codes_spec, fixed(picks.shape), fi...  7.49 us
    unnamed x35, local copies, waits for them, and re-layouts  6.75 us
    dot_general x1, matrix products, shards(): grad_gate = jnp.dot(rows.T, d_gate, preferred_element_type=F32).astype(BF16)  6.02 us
    pallas_call x1, Pallas kernels, shards(): call(latent_kernel, (STEPS,), [back_spec, codes_spec, fixed(picks.shape),...  5.29 us
  transfers between devices with their start and end apart: 4, of which 4 were waited for; matrix products, arithmetic and copies ran while one was open for 8% of the time, Pallas kernels for 23%

profile of v1, /device:TPU:0, one launch (start us, length us, event | category | flops | bytes accessed | tf_op | source)
XLA Modules:
  0.0 183.4 jit_solution(6928830216622661301)
XLA Ops:
  0.6 0.8 copy.17.picks_ref
  1.4 0.0 copy-start.5
  1.4 0.9 copy-done.5
  2.4 0.0 copy-start.7
  2.4 1.0 copy-done.7
  3.4 3.9 %shard_map.154 = (s32[128,4]{1,0:T(8,128)S(1)}, bf16[5120,256]{1,0:T(8,128)(2,1)}) custom-call(s32[128,4]{1,0:T(8,128)S(1)} %copy.17.picks_ref, bf16[128,1024]{1,0:T(8,128)(2,1)S(1)} %copy-done.5, bf16[640,320]{1,0:T(8,128)(2,1)S(1)} %copy-done.7), custom_call_target="tpu_custom_call" | custom-call | flops 335544320 | bytes 2883584 | tf_op jit(solution)/shard_map/pallas_call | solution.py:223
  7.3 0.0 copy-start.10
  7.3 0.0 copy-start.6
  7.3 0.0 copy-start.8
  7.3 11.6 %all-to-all-start = ((bf16[128,40,256]{2,1,0:T(8,128)(2,1)}), bf16[128,40,256]{2,1,0:T(8,128)(2,1)}, u32[]{:S(2)}, u32[]{:S(2)}) async-start(bf16[128,40,256]{2,1,0:T(8,128)(2,1)} %bitcast.30), calls=%async_computation | async-start | bytes 5242880 | tf_op jit(solution)/shard_map/all_to_all | solution.py:207
  18.9 0.0 copy-done.10
  18.9 0.1 copy.18.gates_ref
  19.0 0.0 copy-done.6
  19.1 0.0 copy-done.8
  19.1 4.0 %shard_map.157 = bf16[5120,256]{1,0:T(8,128)(2,1)} custom-call(s32[128,4]{1,0:T(8,128)S(1)} %get-tuple-element.21.target_ref, f32[128,4]{1,0:T(8,128)S(1)} %copy.18.gates_ref, bf16[128,1024]{1,0:T(8,128)(2,1)S(1)} %copy-done.6, bf16[640,320]{1,0:T(8,128)(2,1)S(1)} %copy-done.8), custom_call_target="tpu_custom_call" | custom-call | flops 1342177280 | bytes 2883584 | tf_op jit(solution)/shard_map/pallas_call | solution.py:233
  23.1 31.3 %all-to-all-done = bf16[128,40,256]{2,1,0:T(8,128)(2,1)} async-done(((bf16[128,40,256]{2,1,0:T(8,128)(2,1)}), bf16[128,40,256]{2,1,0:T(8,128)(2,1)}, u32[]{:S(2)}, u32[]{:S(2)}) %all-to-all-start) | async-done | bytes 2621472 | tf_op jit(solution)/shard_map/all_to_all | solution.py:207
  54.3 0.0 copy-start
  54.3 0.0 copy-start.2
  54.3 0.0 copy-start.9
  54.3 5.9 %all-to-all-start.2 = ((bf16[128,40,256]{2,1,0:T(8,128)(2,1)}), bf16[128,40,256]{2,1,0:T(8,128)(2,1)}, u32[]{:S(2)}, u32[]{:S(2)}) async-start(bf16[128,40,256]{2,1,0:T(8,128)(2,1)} %bitcast.29), calls=%async_computation.2 | async-start | bytes 5242880 | tf_op jit(solution)/shard_map/all_to_all | solution.py:207
  60.3 0.0 copy-done
  60.3 0.0 copy-done.2
  60.3 0.0 copy-done.9
  60.3 0.0 copy-start.3
  60.3 1.6 copy-done.3
  61.9 15.3 %shard_map.155 = (bf16[1280,1024]{1,0:T(8,128)(2,1)}, f32[1280,1024]{1,0:T(8,128)}, f32[1280,1024]{1,0:T(8,128)}, bf16[1280,1024]{1,0:T(8,128)(2,1)}, bf16[5120,256]{1,0:T(8,128)(2,1)}) custom-call(bf16[5120,256]{1,0:T(8,128)(2,1)} %bitcast.1.moved_ref, bf16[1024,1024]{1,0:T(8,128)(2,1)S(1)} %bitcast.23, bf16[1024,1024]{1,0:T(8,128)(2,1)S(1)} %bitcast.25, ...), custom_call_target="tpu_custom_call" | custom-call | flops 8053063680 | bytes 29884416 | tf_op jit(solution)/shard_map/pallas_call | solution.py:251
  77.2 18.5 %all-to-all-done.2 = bf16[128,40,256]{2,1,0:T(8,128)(2,1)} async-done(((bf16[128,40,256]{2,1,0:T(8,128)(2,1)}), bf16[128,40,256]{2,1,0:T(8,128)(2,1)}, u32[]{:S(2)}, u32[]{:S(2)}) %all-to-all-start.2) | async-done | bytes 2621472 | tf_op jit(solution)/shard_map/all_to_all | solution.py:207
  95.7 5.7 %all-to-all-start.1 = ((bf16[128,40,256]{2,1,0:T(8,128)(2,1)}), bf16[128,40,256]{2,1,0:T(8,128)(2,1)}, u32[]{:S(2)}, u32[]{:S(2)}) async-start(bf16[128,40,256]{2,1,0:T(8,128)(2,1)} %bitcast.28), calls=%async_computation.1 | async-start | bytes 5242880 | tf_op jit(solution)/shard_map/all_to_all | solution.py:207
  101.4 0.0 copy-start.4
  101.4 1.6 copy-done.4
  103.0 16.0 %shard_map.158 = (bf16[1280,1024]{1,0:T(8,128)(2,1)}, bf16[1280,1024]{1,0:T(8,128)(2,1)}, bf16[1280,1024]{1,0:T(8,128)(2,1)}, bf16[5120,256]{1,0:T(8,128)(2,1)}) custom-call(bf16[5120,256]{1,0:T(8,128)(2,1)} %bitcast.8.moved_ref, f32[1280,1024]{1,0:T(8,128)} %get-tuple-element.23.active_ref, f32[1280,1024]{1,0:T(8,128)} %get-tuple-element.24.slope_ref, ...), custom_call_target="tpu_custom_call" | custom-call | flops 8053063680 | bytes 29884416 | tf_op jit(solution)/shard_map/pallas_call | solution.py:261
  119.1 17.8 %all-to-all-done.1 = bf16[128,40,256]{2,1,0:T(8,128)(2,1)} async-done(((bf16[128,40,256]{2,1,0:T(8,128)(2,1)}), bf16[128,40,256]{2,1,0:T(8,128)(2,1)}, u32[]{:S(2)}, u32[]{:S(2)}) %all-to-all-start.1) | async-done | bytes 2621472 | tf_op jit(solution)/shard_map/all_to_all | solution.py:207
  136.8 0.0 copy-start.13
  136.8 6.1 %all-to-all-start.3 = ((bf16[128,40,256]{2,1,0:T(8,128)(2,1)}), bf16[128,40,256]{2,1,0:T(8,128)(2,1)}, u32[]{:S(2)}, u32[]{:S(2)}) async-start(bf16[128,40,256]{2,1,0:T(8,128)(2,1)} %bitcast.27), calls=%async_computation.3 | async-start | bytes 5242880 | tf_op jit(solution)/shard_map/all_to_all | solution.py:207
  142.9 0.0 copy-done.13
  142.9 0.0 copy-start.12
  142.9 0.0 copy-start.15
  142.9 6.0 %convert_bitcast_fusion.2 = bf16[1,1024,1024]{2,1,0:T(8,128)(2,1)} fusion(bf16[1280,1024]{1,0:T(8,128)(2,1)} %get-tuple-element.27, bf16[1280,1024]{1,0:T(8,128)(2,1)S(1)} %copy-done.13), kind=kOutput, calls=%fused_computation.2 | convolution fusion | flops 2685403136 | bytes 7340032 | tf_op jit(solution)/shard_map/dot_general | solution.py:272
  149.0 0.0 copy-done.12
  149.0 0.0 copy-done.15
  149.0 0.0 copy-start.11
  149.0 0.0 copy-start.14
  149.0 4.1 %convert_bitcast_fusion.1 = bf16[1,1024,1024]{2,1,0:T(8,128)(2,1)} fusion(bf16[1280,1024]{1,0:T(8,128)(2,1)S(1)} %copy-done.15, bf16[1280,1024]{1,0:T(8,128)(2,1)S(1)} %copy-done.12), kind=kOutput, calls=%fused_computation.1 | convolution fusion | flops 2685403136 | bytes 7340032 | tf_op jit(solution)/shard_map/dot_general | solution.py:273
  153.1 0.0 copy-done.11
  153.1 0.0 copy-done.14
  153.1 0.0 copy-start.1
  153.1 4.1 %convert_bitcast_fusion = bf16[1,1024,1024]{2,1,0:T(8,128)(2,1)} fusion(bf16[1280,1024]{1,0:T(8,128)(2,1)S(1)} %copy-done.14, bf16[1280,1024]{1,0:T(8,128)(2,1)S(1)} %copy-done.11), kind=kOutput, calls=%fused_computation | convolution fusion | flops 2685403136 | bytes 7340032 | tf_op jit(solution)/shard_map/dot_general | solution.py:274
  157.2 0.0 copy-done.1
  157.2 7.5 %shard_map.156 = (bf16[128,1024]{1,0:T(8,128)(2,1)}, f32[128,4]{1,0:T(8,128)S(1)}) custom-call(bf16[5120,256]{1,0:T(8,128)(2,1)} %bitcast.6.back_ref, s32[4,1,320]{2,1,0:T(1,128)S(1)} %copy-done.1, s32[128,4]{1,0:T(8,128)S(1)} %get-tuple-element.21.target_ref, f32[128,4]{1,0:T(8,128)S(1)} %copy.18.gates_ref, bf16[128,1024]{1,0:T(8,128)(2,1)S(1)} %copy-done.6, ...), custom_call_target="tpu_custom_call" | custom-call | flops 1342177280 | bytes 2621440 | tf_op jit(solution)/shard_map/pallas_call | solution.py:277
  164.7 0.7 copy.20
  165.4 12.8 %all-to-all-done.3 = bf16[128,40,256]{2,1,0:T(8,128)(2,1)} async-done(((bf16[128,40,256]{2,1,0:T(8,128)(2,1)}), bf16[128,40,256]{2,1,0:T(8,128)(2,1)}, u32[]{:S(2)}, u32[]{:S(2)}) %all-to-all-start.3) | async-done | bytes 2621472 | tf_op jit(solution)/shard_map/all_to_all | solution.py:207
  178.2 5.3 %shard_map.159 = bf16[128,1024]{1,0:T(8,128)(2,1)} custom-call(bf16[5120,256]{1,0:T(8,128)(2,1)} %bitcast.10.back_ref, s32[4,1,320]{2,1,0:T(1,128)S(1)} %copy-done.1, s32[128,4]{1,0:T(8,128)S(1)} %get-tuple-element.21.target_ref, bf16[320,320]{1,0:T(8,128)(2,1)S(1)} %copy-done), custom_call_target="tpu_custom_call" | custom-call | flops 335544320 | bytes 2621440 | tf_op jit(solution)/shard_map/pallas_call | solution.py:287
Async XLA Ops:
  1.4 0.9 copy-start.5
  2.4 1.0 copy-start.7
  7.3 11.6 %copy-start.10 = (f32[128,4]{0,1:T(4,128)S(1)}, f32[128,4]{0,1:T(4,128)}, u32[]{:S(2)}) copy-start(f32[128,4]{0,1:T(4,128)} %param.13) | copy-start | bytes 6148
  7.3 11.7 %copy-start.6 = (bf16[128,1024]{1,0:T(8,128)(2,1)S(1)}, bf16[128,1024]{1,0:T(8,128)(2,1)}, u32[]{:S(2)}) copy-start(bf16[128,1024]{1,0:T(8,128)(2,1)} %cotangent_ref.3) | copy-start | bytes 786436
  7.3 11.8 %copy-start.8 = (bf16[640,320]{1,0:T(8,128)(2,1)S(1)}, bf16[640,320]{1,0:T(8,128)(2,1)}, u32[]{:S(2)}) copy-start(bf16[640,320]{1,0:T(8,128)(2,1)} %constant.10.clone.table) | copy-start | bytes 1228804
  7.3 47.0 %all-to-all-start = ((bf16[128,40,256]{2,1,0:T(8,128)(2,1)}), bf16[128,40,256]{2,1,0:T(8,128)(2,1)}, u32[]{:S(2)}, u32[]{:S(2)}) async-start(bf16[128,40,256]{2,1,0:T(8,128)(2,1)} %bitcast.30), calls=%async_computation | async-start | bytes 5242880 | tf_op jit(solution)/shard_map/all_to_all | solution.py:207
  54.3 5.9 %copy-start = (bf16[320,320]{1,0:T(8,128)(2,1)S(1)}, bf16[320,320]{1,0:T(8,128)(2,1)}, u32[]{:S(2)}) copy-start(bf16[320,320]{1,0:T(8,128)(2,1)} %constant.8.clone.apart.table) | copy-start | bytes 614404
  54.3 5.9 %copy-start.2 = (bf16[1,1024,1024]{2,1,0:T(8,128)(2,1)S(1)}, bf16[1,1024,1024]{2,1,0:T(8,128)(2,1)}, u32[]{:S(2)}) copy-start(bf16[1,1024,1024]{2,1,0:T(8,128)(2,1)} %param.14) | copy-start | bytes 6291460
  54.3 5.9 %copy-start.9 = (bf16[320,320]{1,0:T(8,128)(2,1)S(1)}, bf16[320,320]{1,0:T(8,128)(2,1)}, u32[]{:S(2)}) copy-start(bf16[320,320]{1,0:T(8,128)(2,1)} %constant.9.clone.together) | copy-start | bytes 614404
  54.3 41.3 %all-to-all-start.2 = ((bf16[128,40,256]{2,1,0:T(8,128)(2,1)}), bf16[128,40,256]{2,1,0:T(8,128)(2,1)}, u32[]{:S(2)}, u32[]{:S(2)}) async-start(bf16[128,40,256]{2,1,0:T(8,128)(2,1)} %bitcast.29), calls=%async_computation.2 | async-start | bytes 5242880 | tf_op jit(solution)/shard_map/all_to_all | solution.py:207
  60.3 1.6 copy-start.3
  95.7 41.2 %all-to-all-start.1 = ((bf16[128,40,256]{2,1,0:T(8,128)(2,1)}), bf16[128,40,256]{2,1,0:T(8,128)(2,1)}, u32[]{:S(2)}, u32[]{:S(2)}) async-start(bf16[128,40,256]{2,1,0:T(8,128)(2,1)} %bitcast.28), calls=%async_computation.1 | async-start | bytes 5242880 | tf_op jit(solution)/shard_map/all_to_all | solution.py:207
  101.4 1.6 copy-start.4
  136.8 6.1 %copy-start.13 = (bf16[1280,1024]{1,0:T(8,128)(2,1)S(1)}, bf16[1280,1024]{1,0:T(8,128)(2,1)}, u32[]{:S(2)}) copy-start(bf16[1280,1024]{1,0:T(8,128)(2,1)} %get-tuple-element.28) | copy-start | bytes 7864324
  136.8 41.3 %all-to-all-start.3 = ((bf16[128,40,256]{2,1,0:T(8,128)(2,1)}), bf16[128,40,256]{2,1,0:T(8,128)(2,1)}, u32[]{:S(2)}, u32[]{:S(2)}) async-start(bf16[128,40,256]{2,1,0:T(8,128)(2,1)} %bitcast.27), calls=%async_computation.3 | async-start | bytes 5242880 | tf_op jit(solution)/shard_map/all_to_all | solution.py:207
  142.9 6.0 %copy-start.12 = (bf16[1280,1024]{1,0:T(8,128)(2,1)S(1)}, bf16[1280,1024]{1,0:T(8,128)(2,1)}, u32[]{:S(2)}) copy-start(bf16[1280,1024]{1,0:T(8,128)(2,1)} %get-tuple-element.29) | copy-start | bytes 7864324
  142.9 6.0 %copy-start.15 = (bf16[1280,1024]{1,0:T(8,128)(2,1)S(1)}, bf16[1280,1024]{1,0:T(8,128)(2,1)}, u32[]{:S(2)}) copy-start(bf16[1280,1024]{1,0:T(8,128)(2,1)} %get-tuple-element.27) | copy-start | bytes 7864324
  149.0 4.1 %copy-start.11 = (bf16[1280,1024]{1,0:T(8,128)(2,1)S(1)}, bf16[1280,1024]{1,0:T(8,128)(2,1)}, u32[]{:S(2)}) copy-start(bf16[1280,1024]{1,0:T(8,128)(2,1)} %get-tuple-element.31) | copy-start | bytes 7864324
  149.0 4.1 %copy-start.14 = (bf16[1280,1024]{1,0:T(8,128)(2,1)S(1)}, bf16[1280,1024]{1,0:T(8,128)(2,1)}, u32[]{:S(2)}) copy-start(bf16[1280,1024]{1,0:T(8,128)(2,1)} %get-tuple-element.30) | copy-start | bytes 7864324
  153.1 4.1 %copy-start.1 = (s32[4,1,320]{2,1,0:T(1,128)S(1)}, s32[4,1,320]{2,1,0:T(1,128)}, u32[]{:S(2)}) copy-start(s32[4,1,320]{2,1,0:T(1,128)} %constant.11.clone.codes_ref) | copy-start | bytes 15364

commit v2 on v1

--- a/solution.py
+++ b/solution.py
@@ -29,7 +29,7 @@
 
 def returned_codes(experts):
     slots = np.arange(experts * CAP, dtype=np.int32).reshape(experts, 1, CAP)
-    return np.broadcast_to(slots, (experts, 2, CAP)).reshape(STEPS, 1, experts * 2 * CAP // STEPS)
+    return np.broadcast_to(slots, (experts, 2, CAP)).reshape(-1, 1)
 
 
 def unpack_table():
@@ -73,12 +73,18 @@
     return jnp.concatenate([rows[:, p * width : (p + 1) * width] for p in range(PIECES)], axis=0)
 
 
-def send(rows, table, sent_ref):
+def send(rows, table, sent_ref, ready, sems):
     inner = GROUP * CAP
     size = table.shape[0]
+    copies = []
     for group in range(rows.shape[0] // inner):
         part = dot(table[...], pieces(rows[group * inner : (group + 1) * inner, :]))
-        sent_ref[group * size : (group + 1) * size, :] = part.astype(BF16)
+        ready[group] = part.astype(BF16)
+        place = sent_ref.at[group * size : (group + 1) * size, :]
+        copies.append(pltpu.make_async_copy(ready.at[group], place, sems.at[group]))
+        copies[-1].start()
+    for copy in copies:
+        copy.wait()
 
 
 def repack(rows, table, back_ref):
@@ -99,34 +105,51 @@
     return jnp.concatenate(groups, axis=0)
 
 
-def route_kernel(picks_ref, latent_ref, table, target_ref, sent_ref):
+def column(row):
+    count = row.shape[1]
+    here = lax.broadcasted_iota(jnp.int32, (count, count), 0) == lax.broadcasted_iota(jnp.int32, (count, count), 1)
+    return jnp.sum(jnp.where(here, row, 0), axis=1, keepdims=True)
+
+
+def row_of(values):
+    count = values.shape[0]
+    here = lax.broadcasted_iota(jnp.int32, (count, count), 0) == lax.broadcasted_iota(jnp.int32, (count, count), 1)
+    return jnp.sum(jnp.where(here, values, 0), axis=0, keepdims=True)
+
+
+def route_kernel(picks_ref, latent_ref, table, target_ref, sent_ref, ready, sems):
     picks = picks_ref[...]
-    tokens = picks.shape[0]
-    lane = lax.broadcasted_iota(jnp.int32, (tokens, 128), 1)
-    named = [picks[:, k : k + 1] == lane for k in range(TOPK)]
+    tokens = picks.shape[1]
+    slots = sent_ref.shape[0] // (2 * PIECES)
+    names = lax.broadcasted_iota(jnp.int32, (slots // CAP, tokens), 0)
+    named = [picks[k : k + 1, :] == names for k in range(TOPK)]
     some = functools.reduce(jnp.logical_or, named)
-    now = lax.broadcasted_iota(jnp.int32, (tokens, tokens), 0)
-    other = lax.broadcasted_iota(jnp.int32, (tokens, tokens), 1)
-    before = dot(one_hot(other < now), one_hot(some))
-    slots = sent_ref.shape[0] // (2 * PIECES)
-    codes = lax.broadcasted_iota(jnp.int32, (1, slots), 1)
+    other = lax.broadcasted_iota(jnp.int32, (tokens, tokens), 0)
+    now = lax.broadcasted_iota(jnp.int32, (tokens, tokens), 1)
+    before = dot(one_hot(some), one_hot(other < now))
+    codes = lax.broadcasted_iota(jnp.int32, (slots, tokens), 0)
     hit = None
     for k in range(TOPK):
-        slot = jnp.sum(jnp.where(named[k], before, 0.0), axis=1, keepdims=True)
-        target = picks[:, k : k + 1] * CAP + slot.astype(jnp.int32)
-        target_ref[:, k : k + 1] = target
-        here = target == codes
+        slot = jnp.sum(jnp.where(named[k], before, 0.0), axis=0, keepdims=True)
+        target = picks[k : k + 1, :] * CAP + slot.astype(jnp.int32)
+        target_ref[k : k + 1, :] = target
+        here = codes == target
         hit = here if hit is None else hit | here
-    send(dot(one_hot(hit), latent_ref[...], 0, 0).astype(BF16), table, sent_ref)
-
-
-def pack_kernel(target_ref, gates_ref, cotangent_ref, table, sent_ref):
+    rows = dot(one_hot(hit), latent_ref[...]).astype(BF16)
+    send(rows, table, sent_ref, ready, sems)
+
+
+def pack_kernel(target_ref, gates_ref, cotangent_ref, table, sent_ref, ready, sems):
     cotangent = cotangent_ref[...].astype(F32)
-    weighted = jnp.concatenate([(gates_ref[:, k : k + 1] * cotangent).astype(BF16) for k in range(TOPK)], axis=0)
+    tokens = cotangent.shape[0]
     slots = sent_ref.shape[0] // (2 * PIECES)
-    codes = lax.broadcasted_iota(jnp.int32, (1, slots), 1)
-    hits = jnp.concatenate([one_hot(target_ref[:, k : k + 1] == codes) for k in range(TOPK)], axis=0)
-    send(dot(hits, weighted, 0, 0).astype(BF16), table, sent_ref)
+    codes = lax.broadcasted_iota(jnp.int32, (slots, tokens), 0)
+    hits, weighted = [], []
+    for k in range(TOPK):
+        hits.append(one_hot(codes == target_ref[k : k + 1, :]))
+        weighted.append((column(gates_ref[k : k + 1, :]) * cotangent).astype(BF16))
+    rows = dot(jnp.concatenate(hits, axis=1), jnp.concatenate(weighted, axis=0)).astype(BF16)
+    send(rows, table, sent_ref, ready, sems)
 
 
 def forward_kernel(moved_ref, w_gate, w_up, w_down, apart, together, rows_ref, active_ref, slope_ref, hidden_ref, back_ref):
@@ -157,10 +180,10 @@
 
 def moe_kernel(back_ref, codes_ref, target_ref, gates_ref, cotangent_ref, table, moe_ref, gate_grad_ref, picked):
     step = pl.program_id(0)
-    tokens = target_ref.shape[0]
-    codes = codes_ref[0]
-    hits = jnp.concatenate([one_hot(target_ref[:, k : k + 1] == codes) for k in range(TOPK)], axis=0)
-    part = dot(hits, unpack(back_ref, table))
+    tokens = target_ref.shape[1]
+    codes = codes_ref[...]
+    hits = jnp.concatenate([one_hot(codes == target_ref[k : k + 1, :]) for k in range(TOPK)], axis=1)
+    part = dot(hits, unpack(back_ref, table), 0, 0)
 
     @pl.when(step == 0)
     def _():
@@ -176,36 +199,26 @@
         total = None
         for k in range(TOPK):
             mine = picked[k * tokens : (k + 1) * tokens, :]
-            gate_grad_ref[:, k : k + 1] = jnp.sum(cotangent * mine, axis=1, keepdims=True)
-            term = gates_ref[:, k : k + 1] * mine
+            gate_grad_ref[k : k + 1, :] = row_of(jnp.sum(cotangent * mine, axis=1, keepdims=True))
+            term = column(gates_ref[k : k + 1, :]) * mine
             total = term if total is None else total + term
         moe_ref[...] = total.astype(BF16)
 
 
-def latent_kernel(back_ref, codes_ref, target_ref, table, out_ref, total):
-    step = pl.program_id(0)
-    codes = codes_ref[0]
-    hit = functools.reduce(jnp.logical_or, [target_ref[:, k : k + 1] == codes for k in range(TOPK)])
-    part = dot(one_hot(hit), unpack(back_ref, table))
-
-    @pl.when(step == 0)
-    def _():
-        total[...] = part
-
-    @pl.when(step > 0)
-    def _():
-        total[...] += part
-
-    @pl.when(step == pl.num_programs(0) - 1)
-    def _():
-        out_ref[...] = total[...].astype(BF16)
+def latent_kernel(back_ref, codes_ref, target_ref, table, out_ref):
+    codes = codes_ref[...]
+    hit = functools.reduce(jnp.logical_or, [codes == target_ref[k : k + 1, :] for k in range(TOPK)])
+    out_ref[...] = dot(one_hot(hit), unpack(back_ref, table), 0, 0).astype(BF16)
 
 
 def exchange(blocks, devices):
     shape = blocks.shape
     blocks = blocks.reshape(devices, shape[0] // devices, shape[1])
-    moved = lax.all_to_all(blocks, AXES, split_axis=0, concat_axis=0, tiled=True).reshape(shape)
-    return pltpu.with_memory_space_constraint(moved, pltpu.HBM)
+    return lax.all_to_all(blocks, AXES, split_axis=0, concat_axis=0, tiled=True).reshape(shape)
+
+
+def in_hbm(value):
+    return pltpu.with_memory_space_constraint(value, pltpu.HBM)
 
 
 def shards(latent, picks, gates, gate_w, up_w, down_w, cotangent):
@@ -220,26 +233,32 @@
     apart, together, doubled = [jnp.asarray(t, BF16) for t in (unpack_table(), unpack_table().T, double_table())]
     codes = jnp.asarray(returned_codes(experts))
 
+    picks, gates = picks.T, gates.T
+    groups = experts // GROUP
+    sending = [pltpu.VMEM((groups, doubled.shape[0], piece), BF16), pltpu.SemaphoreType.DMA((groups,))]
+    sent_spec = pl.BlockSpec(memory_space=pltpu.HBM)
     target, sent = call(
         route_kernel,
         (1,),
         [fixed(picks.shape), fixed(latent.shape), fixed(doubled.shape)],
-        [fixed(picks.shape), fixed(back_shape.shape)],
+        [fixed(picks.shape), sent_spec],
         [jax.ShapeDtypeStruct(picks.shape, jnp.int32), back_shape],
+        sending,
         flops=2 * total_rows * tokens * width,
         moved=2 * (total_rows + tokens) * width,
-    )(picks, latent, doubled)
-    moved = exchange(sent, devices)
+    )(in_hbm(picks), in_hbm(latent), in_hbm(doubled))
+    moved = in_hbm(exchange(sent, devices))
     d_sent = call(
         pack_kernel,
         (1,),
         [fixed(picks.shape), fixed(gates.shape), fixed(cotangent.shape), fixed(doubled.shape)],
-        fixed(back_shape.shape),
+        sent_spec,
         back_shape,
+        sending,
         flops=2 * total_rows * tokens * TOPK * width,
         moved=2 * (total_rows + tokens) * width,
     )(target, gates, cotangent, doubled)
-    d_moved = exchange(d_sent, devices)
+    d_moved = in_hbm(exchange(d_sent, devices))
 
     block = total_rows // STEPS
     weights = [fixed(w_gate.shape), fixed(w_up.shape), fixed(w_down.shape), fixed(apart.shape), fixed(apart.shape)]
@@ -257,7 +276,7 @@
         flops=6 * total_rows * width * hidden_width,
         moved=6 * width * hidden_width + 18 * total_rows * width,
     )(moved, w_gate, w_up, w_down, apart, together)
-    returned = exchange(back, devices)
+    returned = in_hbm(exchange(back, devices))
     d_rows, d_gate, d_up, d_back = call(
         backward_kernel,
         (STEPS,),
@@ -273,7 +292,7 @@
     grad_up = jnp.dot(rows.T, d_up, preferred_element_type=F32).astype(BF16)
     grad_down = jnp.dot(hidden.T, d_rows, preferred_element_type=F32).astype(BF16)
 
-    codes_spec = pl.BlockSpec((1,) + codes.shape[1:], lambda i: (i, 0, 0))
+    codes_spec = rows_of(total_rows // STEPS, 1)
     moe_out, gate_grad = call(
         moe_kernel,
         (STEPS,),
@@ -284,17 +303,17 @@
         flops=2 * total_rows * tokens * TOPK * width,
         moved=2 * back_rows * piece,
     )(returned, codes, target, gates, cotangent, apart)
+    whole = pl.BlockSpec(memory_space=pltpu.VMEM)
     d_latent = call(
         latent_kernel,
-        (STEPS,),
-        [back_spec, codes_spec, fixed(picks.shape), fixed(apart.shape)],
-        fixed(latent.shape),
+        (),
+        [whole, whole, whole, whole],
+        whole,
         jax.ShapeDtypeStruct(latent.shape, BF16),
-        [pltpu.VMEM((tokens, width), F32)],
         flops=2 * total_rows * tokens * width,
         moved=2 * back_rows * piece,
     )(d_returned, codes, target, apart)
-    return (moe_out, d_latent, gate_grad, grad_gate[None], grad_up[None], grad_down[None])
+    return (moe_out, d_latent, gate_grad.T, grad_gate[None], grad_up[None], grad_down[None])
 
 
 def solution(mesh):

time: 185 us -> 180 us (0.973)
  Pallas kernels: 52 us -> 49.3 us
  local copies, waits for them, and re-layouts: 6.75 us -> 4.8 us
    pallas_call x1, Pallas kernels: 5.29 us -> 2.61 us  [shards(): call(latent_kernel, (), [whole, whole, whole, whole], whole, jax.ShapeDty...]
    unnamed x35 -> x30, local copies, waits for them, and re-layouts: 6.75 us -> 4.8 us
  transfers between devices with their start and end apart: 4 -> 4, of which waited for: 4 -> 4; matrix products, arithmetic and copies ran while one was open for 8% -> 8% of each run, Pallas kernels for 23% -> 24%
where the time goes in v2:
time: 180 us; the launch traced here: 179 us
  waiting for transfers between devices  81.2 us (45%)
  Pallas kernels  49.3 us (27%)
  starting transfers between devices  27.6 us (15%)
  matrix products  15.2 us (8%)
  local copies, waits for them, and re-layouts  4.8 us (3%)
    all_to_all x4, waiting for transfers between devices, exchange(): lax.all_to_all(blocks, AXES, split_axis=0, concat_axis=0, tiled=True)  81.2 us
    all_to_all x4, starting transfers between devices, exchange(): lax.all_to_all(blocks, AXES, split_axis=0, concat_axis=0, tiled=True)  27.6 us
    pallas_call x1, Pallas kernels, shards(): call(backward_kernel, (STEPS,), [back_spec, hidden_spec, hidden_spec] + w...  16.1 us
    pallas_call x1, Pallas kernels, shards(): call(forward_kernel, (STEPS,), [back_spec] + weights, [row_spec, hidden_s...  15.5 us
    pallas_call x1, Pallas kernels, shards(): call(moe_kernel, (STEPS,), [back_spec, codes_spec, fixed(picks.shape), fi...  7.49 us
    dot_general x1, matrix products, shards(): grad_gate = jnp.dot(rows.T, d_gate, preferred_element_type=F32).astype(BF16)  6.94 us
    unnamed x30, local copies, waits for them, and re-layouts  4.8 us
    pallas_call x1, Pallas kernels, shards(): call(route_kernel, (1,), [fixed(picks.shape), fixed(latent.shape), fixed(...  4.14 us
  transfers between devices with their start and end apart: 4, of which 4 were waited for; matrix products, arithmetic and copies ran while one was open for 8% of the time, Pallas kernels for 24%

profile of v2, /device:TPU:0, one launch (start us, length us, event | category | flops | bytes accessed | tf_op | source)
XLA Modules:
  0.0 178.9 jit_solution(13841650578552215076)
XLA Ops:
  0.6 4.1 %shard_map.154 = (s32[4,128]{1,0:T(4,128)S(1)}, bf16[5120,256]{1,0:T(8,128)(2,1)}) custom-call(s32[4,128]{1,0:T(4,128)} %bitcast.40, bf16[128,1024]{1,0:T(8,128)(2,1)} %latent_ref.1, bf16[640,320]{1,0:T(8,128)(2,1)} %constant.10.clone.table), custom_call_target="tpu_custom_call" | custom-call | flops 335544320 | bytes 2883584 | tf_op jit(solution)/shard_map/pallas_call | solution.py:240
  4.8 0.0 copy-start.5
  4.8 0.0 copy-start.7
  4.8 0.0 copy-start.8
  4.8 11.1 %all-to-all-start = ((bf16[128,40,256]{2,1,0:T(8,128)(2,1)}), bf16[128,40,256]{2,1,0:T(8,128)(2,1)S(1)}, u32[]{:S(2)}, u32[]{:S(2)}) async-start(bf16[128,40,256]{2,1,0:T(8,128)(2,1)} %bitcast.37), calls=%async_computation | async-start | bytes 5242880 | tf_op jit(solution)/shard_map/all_to_all | solution.py:217
  16.0 0.0 copy-done.5
  16.0 0.0 copy-done.7
  16.0 0.0 copy-done.8
  16.0 3.4 %shard_map.157 = bf16[5120,256]{1,0:T(8,128)(2,1)} custom-call(s32[4,128]{1,0:T(4,128)S(1)} %get-tuple-element.21.target_ref, f32[4,128]{1,0:T(4,128)S(1)} %bitcast.31, bf16[128,1024]{1,0:T(8,128)(2,1)S(1)} %copy-done.5, bf16[640,320]{1,0:T(8,128)(2,1)S(1)} %copy-done.8), custom_call_target="tpu_custom_call" | custom-call | flops 1342177280 | bytes 2883584 | tf_op jit(solution)/shard_map/pallas_call | solution.py:251
  19.4 32.4 %all-to-all-done = bf16[128,40,256]{2,1,0:T(8,128)(2,1)S(1)} async-done(((bf16[128,40,256]{2,1,0:T(8,128)(2,1)}), bf16[128,40,256]{2,1,0:T(8,128)(2,1)S(1)}, u32[]{:S(2)}, u32[]{:S(2)}) %all-to-all-start) | async-done | bytes 2621472 | tf_op jit(solution)/shard_map/all_to_all | solution.py:217
  51.8 0.0 copy-start.10
  51.8 1.6 copy-done.10
  53.3 0.0 copy-start.1
  53.3 0.0 copy-start.2
  53.3 0.0 copy-start.9
  53.3 5.9 %all-to-all-start.2 = ((bf16[128,40,256]{2,1,0:T(8,128)(2,1)}), bf16[128,40,256]{2,1,0:T(8,128)(2,1)}, u32[]{:S(2)}, u32[]{:S(2)}) async-start(bf16[128,40,256]{2,1,0:T(8,128)(2,1)} %bitcast.36), calls=%async_computation.2 | async-start | bytes 5242880 | tf_op jit(solution)/shard_map/all_to_all | solution.py:217
  59.3 0.0 copy-done.1
  59.3 0.0 copy-done.2
  59.3 0.0 copy-done.9
  59.3 0.0 copy-start.3
  59.3 1.6 copy-done.3
  60.9 15.5 %shard_map.155 = (bf16[1280,1024]{1,0:T(8,128)(2,1)}, f32[1280,1024]{1,0:T(8,128)}, f32[1280,1024]{1,0:T(8,128)}, bf16[1280,1024]{1,0:T(8,128)(2,1)}, bf16[5120,256]{1,0:T(8,128)(2,1)}) custom-call(bf16[5120,256]{1,0:T(8,128)(2,1)} %bitcast.34, bf16[1024,1024]{1,0:T(8,128)(2,1)S(1)} %bitcast.27, bf16[1024,1024]{1,0:T(8,128)(2,1)S(1)} %bitcast.29, ...), custom_call_target="tpu_custom_call" | custom-call | flops 8053063680 | bytes 29884416 | tf_op jit(solution)/shard_map/pallas_call | solution.py:270
  76.4 18.2 %all-to-all-done.2 = bf16[128,40,256]{2,1,0:T(8,128)(2,1)} async-done(((bf16[128,40,256]{2,1,0:T(8,128)(2,1)}), bf16[128,40,256]{2,1,0:T(8,128)(2,1)}, u32[]{:S(2)}, u32[]{:S(2)}) %all-to-all-start.2) | async-done | bytes 2621472 | tf_op jit(solution)/shard_map/all_to_all | solution.py:217
  94.7 5.7 %all-to-all-start.1 = ((bf16[128,40,256]{2,1,0:T(8,128)(2,1)}), bf16[128,40,256]{2,1,0:T(8,128)(2,1)}, u32[]{:S(2)}, u32[]{:S(2)}) async-start(bf16[128,40,256]{2,1,0:T(8,128)(2,1)} %bitcast.35), calls=%async_computation.1 | async-start | bytes 5242880 | tf_op jit(solution)/shard_map/all_to_all | solution.py:217
  100.4 0.0 copy-start.4
  100.4 1.6 copy-done.4
  102.0 16.1 %shard_map.158 = (bf16[1280,1024]{1,0:T(8,128)(2,1)}, bf16[1280,1024]{1,0:T(8,128)(2,1)}, bf16[1280,1024]{1,0:T(8,128)(2,1)}, bf16[5120,256]{1,0:T(8,128)(2,1)}) custom-call(bf16[5120,256]{1,0:T(8,128)(2,1)} %bitcast.10.moved_ref, f32[1280,1024]{1,0:T(8,128)} %get-tuple-element.23.active_ref, f32[1280,1024]{1,0:T(8,128)} %get-tuple-element.24.slope_ref, ...), custom_call_target="tpu_custom_call" | custom-call | flops 8053063680 | bytes 29884416 | tf_op jit(solution)/shard_map/pallas_call | solution.py:280
  118.1 17.7 %all-to-all-done.1 = bf16[128,40,256]{2,1,0:T(8,128)(2,1)} async-done(((bf16[128,40,256]{2,1,0:T(8,128)(2,1)}), bf16[128,40,256]{2,1,0:T(8,128)(2,1)}, u32[]{:S(2)}, u32[]{:S(2)}) %all-to-all-start.1) | async-done | bytes 2621472 | tf_op jit(solution)/shard_map/all_to_all | solution.py:217
  135.8 4.8 %all-to-all-start.3 = ((bf16[128,40,256]{2,1,0:T(8,128)(2,1)}), bf16[128,40,256]{2,1,0:T(8,128)(2,1)S(1)}, u32[]{:S(2)}, u32[]{:S(2)}) async-start(bf16[128,40,256]{2,1,0:T(8,128)(2,1)} %bitcast.33), calls=%async_computation.3 | async-start | bytes 5242880 | tf_op jit(solution)/shard_map/all_to_all | solution.py:217
  140.7 0.0 copy-start.12
  140.7 0.0 copy-start.14
  140.7 6.9 %convert_bitcast_fusion.2 = bf16[1,1024,1024]{2,1,0:T(8,128)(2,1)} fusion(bf16[1280,1024]{1,0:T(8,128)(2,1)} %get-tuple-element.27, bf16[1280,1024]{1,0:T(8,128)(2,1)} %get-tuple-element.28), kind=kOutput, calls=%fused_computation.2 | convolution fusion | flops 2685403136 | bytes 7340032 | tf_op jit(solution)/shard_map/dot_general | solution.py:291
  147.6 0.0 copy-done.12
  147.6 0.0 copy-done.14
  147.6 0.0 copy-start.11
  147.6 0.0 copy-start.13
  147.7 4.1 %convert_bitcast_fusion.1 = bf16[1,1024,1024]{2,1,0:T(8,128)(2,1)} fusion(bf16[1280,1024]{1,0:T(8,128)(2,1)S(1)} %copy-done.14, bf16[1280,1024]{1,0:T(8,128)(2,1)S(1)} %copy-done.12), kind=kOutput, calls=%fused_computation.1 | convolution fusion | flops 2685403136 | bytes 7340032 | tf_op jit(solution)/shard_map/dot_general | solution.py:292
  151.8 0.0 copy-done.11
  151.8 0.0 copy-done.13
  151.8 0.0 copy-start
  151.8 0.0 copy-start.6
  151.8 4.1 %convert_bitcast_fusion = bf16[1,1024,1024]{2,1,0:T(8,128)(2,1)} fusion(bf16[1280,1024]{1,0:T(8,128)(2,1)S(1)} %copy-done.13, bf16[1280,1024]{1,0:T(8,128)(2,1)S(1)} %copy-done.11), kind=kOutput, calls=%fused_computation | convolution fusion | flops 2685403136 | bytes 7340032 | tf_op jit(solution)/shard_map/dot_general | solution.py:293
  155.9 0.0 copy-done
  155.9 0.0 copy-done.6
  155.9 7.5 %shard_map.156 = (bf16[128,1024]{1,0:T(8,128)(2,1)}, f32[4,128]{1,0:T(4,128)}) custom-call(bf16[5120,256]{1,0:T(8,128)(2,1)} %bitcast.7.back_ref, s32[1280,1]{1,0:T(8,128)S(1)} %copy-done, s32[4,128]{1,0:T(4,128)S(1)} %get-tuple-element.21.target_ref, f32[4,128]{1,0:T(4,128)S(1)} %bitcast.32, bf16[128,1024]{1,0:T(8,128)(2,1)S(1)} %copy-done.6, ...), custom_call_target="tpu_custom_call" | custom-call | flops 1342177280 | bytes 2621440 | tf_op jit(solution)/shard_map/pallas_call | solution.py:296
  163.4 12.9 %all-to-all-done.3 = bf16[128,40,256]{2,1,0:T(8,128)(2,1)S(1)} async-done(((bf16[128,40,256]{2,1,0:T(8,128)(2,1)}), bf16[128,40,256]{2,1,0:T(8,128)(2,1)S(1)}, u32[]{:S(2)}, u32[]{:S(2)}) %all-to-all-start.3) | async-done | bytes 2621472 | tf_op jit(solution)/shard_map/all_to_all | solution.py:217
  176.3 2.6 %shard_map.159 = bf16[128,1024]{1,0:T(8,128)(2,1)} custom-call(bf16[5120,256]{1,0:T(8,128)(2,1)S(1)} %bitcast.26, s32[1280,1]{1,0:T(8,128)S(1)} %copy-done, s32[4,128]{1,0:T(4,128)S(1)} %get-tuple-element.21.target_ref, bf16[320,320]{1,0:T(8,128)(2,1)S(1)} %copy-done.1), custom_call_target="tpu_custom_call" | custom-call | flops 335544320 | bytes 2621440 | tf_op jit(solution)/shard_map/pallas_call | solution.py:307
Async XLA Ops:
  4.8 11.2 %copy-start.5 = (bf16[128,1024]{1,0:T(8,128)(2,1)S(1)}, bf16[128,1024]{1,0:T(8,128)(2,1)}, u32[]{:S(2)}) copy-start(bf16[128,1024]{1,0:T(8,128)(2,1)} %cotangent_ref.3) | copy-start | bytes 786436
  4.8 11.2 %copy-start.7 = (f32[128,4]{0,1:T(4,128)S(1)}, f32[128,4]{0,1:T(4,128)}, u32[]{:S(2)}) copy-start(f32[128,4]{0,1:T(4,128)} %param.13) | copy-start | bytes 6148
  4.8 11.2 %copy-start.8 = (bf16[640,320]{1,0:T(8,128)(2,1)S(1)}, bf16[640,320]{1,0:T(8,128)(2,1)}, u32[]{:S(2)}) copy-start(bf16[640,320]{1,0:T(8,128)(2,1)} %constant.10.clone.table) | copy-start | bytes 1228804
  4.8 46.9 %all-to-all-start = ((bf16[128,40,256]{2,1,0:T(8,128)(2,1)}), bf16[128,40,256]{2,1,0:T(8,128)(2,1)S(1)}, u32[]{:S(2)}, u32[]{:S(2)}) async-start(bf16[128,40,256]{2,1,0:T(8,128)(2,1)} %bitcast.37), calls=%async_computation | async-start | bytes 5242880 | tf_op jit(solution)/shard_map/all_to_all | solution.py:217
  51.8 1.6 copy-start.10
  53.3 5.9 %copy-start.1 = (bf16[320,320]{1,0:T(8,128)(2,1)S(1)}, bf16[320,320]{1,0:T(8,128)(2,1)}, u32[]{:S(2)}) copy-start(bf16[320,320]{1,0:T(8,128)(2,1)} %constant.8.clone.apart.table) | copy-start | bytes 614404
  53.3 5.9 %copy-start.2 = (bf16[1,1024,1024]{2,1,0:T(8,128)(2,1)S(1)}, bf16[1,1024,1024]{2,1,0:T(8,128)(2,1)}, u32[]{:S(2)}) copy-start(bf16[1,1024,1024]{2,1,0:T(8,128)(2,1)} %param.14) | copy-start | bytes 6291460
  53.3 6.0 %copy-start.9 = (bf16[320,320]{1,0:T(8,128)(2,1)S(1)}, bf16[320,320]{1,0:T(8,128)(2,1)}, u32[]{:S(2)}) copy-start(bf16[320,320]{1,0:T(8,128)(2,1)} %constant.9.clone.together) | copy-start | bytes 614404
  53.3 41.3 %all-to-all-start.2 = ((bf16[128,40,256]{2,1,0:T(8,128)(2,1)}), bf16[128,40,256]{2,1,0:T(8,128)(2,1)}, u32[]{:S(2)}, u32[]{:S(2)}) async-start(bf16[128,40,256]{2,1,0:T(8,128)(2,1)} %bitcast.36), calls=%async_computation.2 | async-start | bytes 5242880 | tf_op jit(solution)/shard_map/all_to_all | solution.py:217
  59.3 1.6 copy-start.3
  94.7 41.2 %all-to-all-start.1 = ((bf16[128,40,256]{2,1,0:T(8,128)(2,1)}), bf16[128,40,256]{2,1,0:T(8,128)(2,1)}, u32[]{:S(2)}, u32[]{:S(2)}) async-start(bf16[128,40,256]{2,1,0:T(8,128)(2,1)} %bitcast.35), calls=%async_computation.1 | async-start | bytes 5242880 | tf_op jit(solution)/shard_map/all_to_all | solution.py:217
  100.4 1.6 copy-start.4
  135.8 40.4 %all-to-all-start.3 = ((bf16[128,40,256]{2,1,0:T(8,128)(2,1)}), bf16[128,40,256]{2,1,0:T(8,128)(2,1)S(1)}, u32[]{:S(2)}, u32[]{:S(2)}) async-start(bf16[128,40,256]{2,1,0:T(8,128)(2,1)} %bitcast.33), calls=%async_computation.3 | async-start | bytes 5242880 | tf_op jit(solution)/shard_map/all_to_all | solution.py:217
  140.7 7.0 %copy-start.12 = (bf16[1280,1024]{1,0:T(8,128)(2,1)S(1)}, bf16[1280,1024]{1,0:T(8,128)(2,1)}, u32[]{:S(2)}) copy-start(bf16[1280,1024]{1,0:T(8,128)(2,1)} %get-tuple-element.29) | copy-start | bytes 7864324
  140.7 7.0 %copy-start.14 = (bf16[1280,1024]{1,0:T(8,128)(2,1)S(1)}, bf16[1280,1024]{1,0:T(8,128)(2,1)}, u32[]{:S(2)}) copy-start(bf16[1280,1024]{1,0:T(8,128)(2,1)} %get-tuple-element.27) | copy-start | bytes 7864324
  147.6 4.1 %copy-start.11 = (bf16[1280,1024]{1,0:T(8,128)(2,1)S(1)}, bf16[1280,1024]{1,0:T(8,128)(2,1)}, u32[]{:S(2)}) copy-start(bf16[1280,1024]{1,0:T(8,128)(2,1)} %get-tuple-element.31) | copy-start | bytes 7864324
  147.6 4.1 %copy-start.13 = (bf16[1280,1024]{1,0:T(8,128)(2,1)S(1)}, bf16[1280,1024]{1,0:T(8,128)(2,1)}, u32[]{:S(2)}) copy-start(bf16[1280,1024]{1,0:T(8,128)(2,1)} %get-tuple-element.30) | copy-start | bytes 7864324
  151.8 4.1 %copy-start = (s32[1280,1]{1,0:T(8,128)S(1)}, s32[1280,1]{1,0:T(8,128)}, u32[]{:S(2)}) copy-start(s32[1280,1]{1,0:T(8,128)} %constant.11.clone.codes_ref) | copy-start | bytes 15364
  151.8 4.1 %copy-start.6 = (bf16[128,1024]{1,0:T(8,128)(2,1)S(1)}, bf16[128,1024]{1,0:T(8,128)(2,1)}, u32[]{:S(2)}) copy-start(bf16[128,1024]{1,0:T(8,128)(2,1)} %cotangent_ref.3) | copy-start | bytes 786436

commit v3 on v2

v3 whole, which is shorter than its diff:
```python
import functools

import jax
import jax.numpy as jnp
import numpy as np
from jax import lax
from jax.experimental import pallas as pl
from jax.experimental.pallas import tpu as pltpu
from jax.sharding import PartitionSpec as P

BF16 = jnp.bfloat16
F32 = jnp.float32
I32 = jnp.int32
TOPK = 4
CAP = 10
PIECES = 4
GROUP = 8
PLANES = 4
INNER = GROUP * CAP
SIZE = PIECES * INNER
NOTES = 16
VMEM_LIMIT = 48 * 1024 * 1024
WIDE_LIMIT = 60 * 1024 * 1024
WEIGHT = 8
SHARE_WEIGHT = 60


def dot(a, b, ca=1, cb=0):
    return lax.dot_general(a, b, (((ca,), (cb,)), ((), ())), preferred_element_type=F32)


def one_hot(mask):
    return jnp.where(mask, 1.0, 0.0).astype(BF16)


def tenth(rows):
    return (rows * 6554) >> 16


def row_numbers(count, tokens):
    return lax.broadcasted_iota(I32, (count, tokens), 0)


def slot_codes(rows, pair):
    device = tenth(rows)
    return (2 * device + pair) * CAP + rows - CAP * device


def apart_table():
    table = np.zeros((SIZE, SIZE), np.float32)
    for block in range(GROUP):
        for piece in range(PIECES):
            for slot in range(CAP):
                table[(piece * GROUP + block) * CAP + slot, (block * PIECES + piece) * CAP + slot] = 1
    return table


def call(kernel, grid, in_specs, out_specs, out_shape, scratch=(), flops=0, moved=0, limit=VMEM_LIMIT, prefetch=0, aliases=None):
    return pl.pallas_call(
        kernel,
        grid_spec=pltpu.PrefetchScalarGridSpec(
            num_scalar_prefetch=prefetch, grid=grid, in_specs=in_specs, out_specs=out_specs, scratch_shapes=list(scratch)
        ),
        out_shape=out_shape,
        input_output_aliases=aliases or {},
        compiler_params=pltpu.CompilerParams(vmem_limit_bytes=limit),
        cost_estimate=pl.CostEstimate(flops=flops, bytes_accessed=moved, transcendentals=0),
    )


def fixed(shape):
    return pl.BlockSpec(shape, lambda *i: (0,) * len(shape))


def rows_of(count, width):
    return pl.BlockSpec((count, width), lambda i, *_: (i, 0))


def in_hbm(value):
    return pltpu.with_memory_space_constraint(value, pltpu.HBM)


def column(row):
    count = row.shape[1]
    here = lax.broadcasted_iota(I32, (count, count), 0) == lax.broadcasted_iota(I32, (count, count), 1)
    return jnp.sum(jnp.where(here, row, 0), axis=1, keepdims=True)


def row_of(values):
    count = values.shape[0]
    here = lax.broadcasted_iota(I32, (count, count), 0) == lax.broadcasted_iota(I32, (count, count), 1)
    return jnp.sum(jnp.where(here, values, 0), axis=0, keepdims=True)


def pieces(rows, count=PIECES):
    width = rows.shape[1] // count
    return jnp.concatenate([rows[:, p * width : (p + 1) * width] for p in range(count)], axis=0)


def send(groups, together, sent_ref, ready, sems):
    copies = []
    for group, rows in enumerate(groups):
        ready[group] = dot(together[...], rows).astype(BF16)
        place = sent_ref.at[group * SIZE : (group + 1) * SIZE, :]
        copies.append(pltpu.make_async_copy(ready.at[group], place, sems.at[group]))
        copies[-1].start()
    for copy in copies:
        copy.wait()


def route_kernel(picks_ref, gates_ref, latent_ref, cotangent_ref, together, target_ref, shared_ref, sent_ref, notes, ready, sems):
    picks = picks_ref[...]
    tokens = picks.shape[1]
    half = sent_ref.shape[0] // 4
    names = row_numbers(2 * half // CAP, tokens)
    named = [picks[k : k + 1, :] == names for k in range(TOPK)]
    some = functools.reduce(jnp.logical_or, named)
    other = lax.broadcasted_iota(I32, (tokens, tokens), 0)
    now = lax.broadcasted_iota(I32, (tokens, tokens), 1)
    before = dot(one_hot(some), one_hot(other < now))
    slots = [jnp.sum(jnp.where(named[k], before, 0.0), axis=0, keepdims=True) for k in range(TOPK)]
    targets = [picks[k : k + 1, :] * CAP + slots[k].astype(I32) for k in range(TOPK)]
    target_ref[...] = jnp.concatenate(targets, axis=0)

    gates = [gates_ref[k : k + 1, :] for k in range(TOPK)]
    high = [g.astype(BF16).astype(F32) for g in gates]
    rest = [g - h for g, h in zip(gates, high)]
    middle = [r.astype(BF16).astype(F32) for r in rest]
    low = [r - m for r, m in zip(rest, middle)]
    values = [picks[k : k + 1, :].astype(F32) for k in range(TOPK)] + slots + high + middle + low
    across = cotangent_ref.shape[1] // tokens
    notes[...] = jnp.zeros_like(notes)
    for i, value in enumerate(values):
        notes[i // across : i // across + 1, (i % across) * tokens : (i % across + 1) * tokens] = value
    shared_ref[:tokens, :] = cotangent_ref[...]
    shared_ref[tokens:, :] = notes[...].astype(BF16)

    rows = row_numbers(half, tokens)
    parts = []
    for pair in range(2):
        codes = slot_codes(rows, pair)
        hit = functools.reduce(jnp.logical_or, [codes == target for target in targets])
        parts.append(dot(one_hot(hit), latent_ref[...]).astype(BF16))
    width = sent_ref.shape[1]
    groups = []
    for group in range(half // INNER):
        mine = slice(group * INNER, (group + 1) * INNER)
        groups.append(jnp.concatenate([part[mine, p * width : (p + 1) * width] for p in range(2) for part in parts], axis=0))
    send(groups, together, sent_ref, ready, sems)


def share_kernel(z_ref, *refs):
    shared, (together, sent_ref, ready, sems) = refs[:PLANES], refs[PLANES:]
    tokens = shared[0].shape[0] - NOTES
    across = shared[0].shape[1] // tokens
    half = sent_ref.shape[0] // PLANES
    codes = slot_codes(row_numbers(half, tokens), z_ref[0] >> 1)
    planes = []
    for plane in shared:
        notes = plane[tokens:, :].astype(F32)
        value = lambda i: notes[i // across : i // across + 1, (i % across) * tokens : (i % across + 1) * tokens]
        cotangent = plane[:tokens, :].astype(F32)
        hits, weighted = [], []
        for k in range(TOPK):
            target = (value(k) * CAP + value(TOPK + k)).astype(I32)
            gate = value(2 * TOPK + k) + value(3 * TOPK + k) + value(4 * TOPK + k)
            hits.append(one_hot(codes == target))
            weighted.append((column(gate) * cotangent).astype(BF16))
        planes.append(dot(jnp.concatenate(hits, axis=1), jnp.concatenate(weighted, axis=0)).astype(BF16))
    groups = []
    for group in range(half // INNER):
        groups.append(jnp.concatenate([rows[group * INNER : (group + 1) * INNER, :] for rows in planes], axis=0))
    send(groups, together, sent_ref, ready, sems)


def split_kernel(z_ref, moved_ref, apart, own_ref, other_ref):
    pair = z_ref[0] >> 1
    for group in range(moved_ref.shape[0] // SIZE):
        mixed = dot(apart[...], moved_ref[group * SIZE : (group + 1) * SIZE, :]).astype(BF16)
        quarters = [mixed[p * INNER : (p + 1) * INNER, :] for p in range(PIECES)]
        rows = [jnp.concatenate([quarters[i], quarters[2 + i]], axis=1) for i in range(2)]
        mine = slice(group * INNER, (group + 1) * INNER)

        @pl.when(pair == 0)
        def _():
            own_ref[mine, :] = rows[0]
            other_ref[mine, :] = rows[1]

        @pl.when(pair == 1)
        def _():
            own_ref[mine, :] = rows[1]
            other_ref[mine, :] = rows[0]


def forward_kernel(z_ref, first_ref, second_ref, w_gate, w_up, w_down, together, *refs):
    rows_ref, active_ref, slope_ref, hidden_ref, back_ref = refs[-5:]
    step = pl.program_id(0)

    @pl.when(step == 0)
    def _():
        rows_ref[0] = first_ref[...]

    @pl.when(step == 1)
    def _():
        rows_ref[0] = second_ref[...]

    rows = rows_ref[0]
    pre_gate = dot(rows, w_gate[...])
    pre_up = dot(rows, w_up[...])
    sigma = jax.nn.sigmoid(pre_gate)
    active = pre_gate * sigma
    hidden = (active * pre_up).astype(BF16)
    active_ref[0] = active
    slope_ref[0] = pre_up * (sigma * (1.0 + pre_gate * (1.0 - sigma)))
    hidden_ref[0] = hidden
    done = dot(hidden, w_down[...]).astype(BF16)
    for group in range(done.shape[0] // INNER):
        part = dot(together[...], pieces(done[group * INNER : (group + 1) * INNER, :]))
        back_ref[0, group * SIZE : (group + 1) * SIZE, :] = part.astype(BF16)


def backward_kernel(z_ref, moved_ref, active_ref, slope_ref, w_gate, w_up, w_down, apart, together, rows_ref, d_gate_ref, d_up_ref, back_ref):
    rows = dot(apart[...], moved_ref[...]).astype(BF16)
    rows_ref[...] = rows.reshape(rows_ref.shape)
    d_hidden = dot(rows, w_down[...], 1, 1)
    shape = d_hidden.shape
    d_gate = (d_hidden * slope_ref[...].reshape(shape)).astype(BF16)
    d_up = (d_hidden * active_ref[...].reshape(shape)).astype(BF16)
    d_gate_ref[...] = d_gate.reshape(d_gate_ref.shape)
    d_up_ref[...] = d_up.reshape(d_up_ref.shape)
    d_rows = (dot(d_gate, w_gate[...], 1, 1) + dot(d_up, w_up[...], 1, 1)).astype(BF16)
    for b in range(PLANES):
        part = dot(together[...], pieces(d_rows[b * INNER : (b + 1) * INNER, :]))
        back_ref[z_ref[0] ^ b, 0] = part.astype(BF16)


def unpack(back_ref, apart):
    groups = []
    for group in range(back_ref.shape[0] // SIZE):
        mixed = dot(apart[...], back_ref[group * SIZE : (group + 1) * SIZE, :]).astype(BF16)
        groups.append(jnp.concatenate([mixed[p * INNER : (p + 1) * INNER, :] for p in range(PIECES)], axis=1))
    return jnp.concatenate(groups, axis=0)


def moe_kernel(back_ref, target_ref, gates_ref, cotangent_ref, apart, moe_ref, gate_grad_ref, picked):
    step = pl.program_id(0)
    tokens = target_ref.shape[1]
    codes = slot_codes(row_numbers(back_ref.shape[0] // PIECES, tokens), step >> 1)
    hits = jnp.concatenate([one_hot(codes == target_ref[k : k + 1, :]) for k in range(TOPK)], axis=1)
    part = dot(hits, unpack(back_ref, apart), 0, 0)

    @pl.when(step == 0)
    def _():
        picked[...] = part

    @pl.when(step > 0)
    def _():
        picked[...] += part

    @pl.when(step == pl.num_programs(0) - 1)
    def _():
        cotangent = cotangent_ref[...].astype(F32)
        total = None
        for k in range(TOPK):
            mine = picked[k * tokens : (k + 1) * tokens, :]
            gate_grad_ref[k : k + 1, :] = row_of(jnp.sum(cotangent * mine, axis=1, keepdims=True))
            term = column(gates_ref[k : k + 1, :]) * mine
            total = term if total is None else total + term
        moe_ref[...] = total.astype(BF16)


def latent_kernel(back_ref, target_ref, apart, out_ref):
    tokens = target_ref.shape[1]
    half = back_ref.shape[0] // PIECES // PLANES
    hits = []
    for pair in range(2):
        codes = slot_codes(row_numbers(half, tokens), pair)
        hit = one_hot(functools.reduce(jnp.logical_or, [codes == target_ref[k : k + 1, :] for k in range(TOPK)]))
        hits += [hit, hit]
    out_ref[...] = dot(jnp.concatenate(hits, axis=0), unpack(back_ref, apart), 0, 0).astype(BF16)


def exchange(rows, blocks, axes):
    shape = rows.shape
    rows = rows.reshape(blocks, -1, shape[-1])
    return lax.all_to_all(rows, axes, split_axis=0, concat_axis=0, tiled=True).reshape(shape)


def from_plane(value, b):
    return lax.ppermute(value, "ex", [(z, z ^ b) for z in range(PLANES)])


def shards(latent, picks, gates, gate_w, up_w, down_w, cotangent):
    tokens, width = latent.shape
    columns = lax.axis_size("ep")
    devices = columns * PLANES
    w_gate, w_up, w_down = gate_w[0], up_w[0], down_w[0]
    hidden_width = w_gate.shape[1]
    plane_rows = columns * CAP
    total_rows = PLANES * plane_rows
    piece = width // PIECES
    apart, together = jnp.asarray(apart_table(), BF16), jnp.asarray(apart_table().T, BF16)
    picks, gates = picks.T, gates.T
    z = lax.axis_index("ex").astype(I32).reshape(1)
    scalar = pl.BlockSpec(memory_space=pltpu.SMEM)
    anywhere = pl.BlockSpec(memory_space=pltpu.HBM)
    whole = pl.BlockSpec(memory_space=pltpu.VMEM)
    table = fixed((SIZE, SIZE))
    groups = total_rows // SIZE

    target, shared, sent = call(
        route_kernel,
        (1,),
        [fixed(picks.shape), fixed(gates.shape), fixed(latent.shape), fixed(cotangent.shape), table],
        [fixed(picks.shape), fixed((tokens + NOTES, width)), anywhere],
        [
            jax.ShapeDtypeStruct(picks.shape, I32),
            jax.ShapeDtypeStruct((tokens + NOTES, width), BF16),
            pltpu.HBM((total_rows, width // 2), BF16),
        ],
        [
            pltpu.VMEM((NOTES, width), F32),
            pltpu.VMEM((groups, SIZE, width // 2), BF16),
            pltpu.SemaphoreType.DMA((groups,)),
        ],
        flops=2 * total_rows * tokens * width,
        moved=2 * (total_rows + tokens) * width,
    )(in_hbm(picks), in_hbm(gates), in_hbm(latent), in_hbm(cotangent), in_hbm(together))
    moved = exchange(sent, columns, "ep")
    others = [from_plane(shared, b) for b in range(1, PLANES)]
    d_sent = call(
        share_kernel,
        (),
        [scalar] + [whole] * (PLANES + 1),
        anywhere,
        pltpu.HBM((total_rows, width), BF16),
        [pltpu.VMEM((groups, SIZE, width), BF16), pltpu.SemaphoreType.DMA((groups,))],
        flops=SHARE_WEIGHT * 2 * total_rows * tokens * TOPK * width,
        moved=2 * (total_rows + tokens) * width,
    )(z, shared, *others, together)

    plane_shape = jax.ShapeDtypeStruct((plane_rows, width), BF16)
    own, other = call(
        split_kernel,
        (),
        [scalar, whole, whole],
        [whole, whole],
        [plane_shape, plane_shape],
        flops=2 * total_rows * SIZE * width,
        moved=4 * total_rows * width,
    )(z, moved, apart)
    own, other, d_sent = lax.optimization_barrier((own, other, d_sent))
    planes = [own, from_plane(own, 1), from_plane(other, 2), from_plane(other, 3)]
    d_moved = in_hbm(exchange(d_sent, columns, "ep"))

    wide = (PLANES, plane_rows, hidden_width)
    kept = [
        jax.ShapeDtypeStruct((PLANES, plane_rows, width), BF16),
        jax.ShapeDtypeStruct(wide, F32),
        jax.ShapeDtypeStruct(wide, F32),
        jax.ShapeDtypeStruct(wide, BF16),
        pltpu.HBM((PLANES, plane_rows * PIECES, piece), BF16),
    ]
    weights = [fixed(w_gate.shape), fixed(w_up.shape), fixed(w_down.shape)]
    held = ()
    for first, second in ((0, 1), (3, 2)):
        spot = lambda i, _, f=first, d=second - first: (f + d * i, 0, 0)
        turned = lambda i, z_ref, f=first, d=second - first: (z_ref[0] ^ (f + d * i), 0, 0)
        specs = [pl.BlockSpec((1,) + shape.shape[1:], spot) for shape in kept[:4]]
        specs.append(pl.BlockSpec((1,) + kept[4].shape[1:], turned))
        held = call(
            forward_kernel,
            (2,),
            [fixed((plane_rows, width))] * 2 + weights + [table] + [pl.BlockSpec(memory_space=pl.ANY)] * len(held),
            specs,
            kept,
            flops=WEIGHT * 3 * total_rows * width * hidden_width,
            moved=6 * width * hidden_width + 9 * total_rows * width,
            prefetch=1,
            aliases={7 + i: i for i in range(len(held))},
        )(z, planes[first], planes[second], w_gate, w_up, w_down, together, *held)
    rows, active, slope, hidden, back = held
    returned = in_hbm(exchange(back, devices, ("ex", "ep")).reshape(-1, piece))

    strip = lambda last: pl.BlockSpec((PLANES, INNER, last), lambda i, _: (0, i, 0))
    d_rows, d_gate, d_up, d_back = call(
        backward_kernel,
        (groups,),
        [rows_of(SIZE, width), strip(hidden_width), strip(hidden_width)] + weights + [table, table],
        [strip(width), strip(hidden_width), strip(hidden_width), pl.BlockSpec((PLANES, 1, SIZE, piece), lambda i, _: (0, i, 0, 0))],
        [
            jax.ShapeDtypeStruct((PLANES, plane_rows, width), BF16),
            jax.ShapeDtypeStruct(wide, BF16),
            jax.ShapeDtypeStruct(wide, BF16),
            pltpu.HBM((PLANES, groups, SIZE, piece), BF16),
        ],
        flops=WEIGHT * 6 * total_rows * width * hidden_width,
        moved=6 * width * hidden_width + 18 * total_rows * width,
        prefetch=1,
    )(z, d_moved, active, slope, w_gate, w_up, w_down, apart, together)
    d_returned = exchange(d_back, devices, ("ex", "ep"))

    rows, hidden, d_rows, d_gate, d_up = [v.reshape(total_rows, -1) for v in (rows, hidden, d_rows, d_gate, d_up)]
    grad_gate = jnp.dot(rows.T, d_gate, preferred_element_type=F32).astype(BF16)
    grad_up = jnp.dot(rows.T, d_up, preferred_element_type=F32).astype(BF16)
    grad_down = jnp.dot(hidden.T, d_rows, preferred_element_type=F32).astype(BF16)

    moe_out, gate_grad = call(
        moe_kernel,
        (PLANES,),
        [rows_of(plane_rows * PIECES, piece), fixed(picks.shape), fixed(gates.shape), fixed(cotangent.shape), table],
        [fixed(latent.shape), fixed(gates.shape)],
        [jax.ShapeDtypeStruct(latent.shape, BF16), jax.ShapeDtypeStruct(gates.shape, F32)],
        [pltpu.VMEM((TOPK * tokens, width), F32)],
        flops=2 * total_rows * tokens * TOPK * width,
        moved=2 * total_rows * width,
    )(returned, target, gates, cotangent, apart)
    d_latent = call(
        latent_kernel,
        (),
        [whole, whole, whole],
        whole,
        jax.ShapeDtypeStruct(latent.shape, BF16),
        flops=2 * total_rows * tokens * width,
        moved=2 * total_rows * width,
    )(d_returned.reshape(-1, piece), target, apart)
    return (moe_out, d_latent, gate_grad.T, grad_gate[None], grad_up[None], grad_down[None])


def solution(mesh):
    both = ("ep", "ex")
    rows, blocks = P(both, None), P(both, None, None)
    return jax.shard_map(
        shards,
        mesh=mesh,
        in_specs=(rows, rows, rows, blocks, blocks, blocks, rows),
        out_specs=(rows, rows, rows, blocks, blocks, blocks),
        check_vma=False,
    )
```

time: 180 us -> 170 us (0.944)
  waiting for transfers between devices: 81.2 us -> 63.3 us
  starting transfers between devices: 27.6 us -> 33.1 us
  Pallas kernels: 49.3 us -> 53.3 us
    all_to_all x4, waiting for transfers between devices: 81.2 us -> 41.2 us  [exchange(): lax.all_to_all(rows, axes, split_axis=0, concat_axis=0, tiled=True)]
    ppermute x0 -> x6, waiting for transfers between devices: none -> 22.1 us  [from_plane(): return lax.ppermute(value, 'ex', [(z, z ^ b) for z in range(PLANES)])]
    ppermute x0 -> x6, starting transfers between devices: none -> 9.86 us  [from_plane(): return lax.ppermute(value, 'ex', [(z, z ^ b) for z in range(PLANES)])]
    all_to_all x4, starting transfers between devices: 27.6 us -> 23.2 us  [exchange(): lax.all_to_all(rows, axes, split_axis=0, concat_axis=0, tiled=True)]
    pallas_call x6 -> x8, Pallas kernels: 49.3 us -> 53.3 us  [the longest x2 17.1 us: shards(): call(forward_kernel, (2,), [fixed((plane_rows, width))] * 2 + weights + [...]
    unnamed x30 -> x24, local copies, waits for them, and re-layouts: 4.8 us -> 3.22 us
  transfers between devices with their start and end apart: 4 -> 10, of which waited for: 4 -> 8; matrix products, arithmetic and copies ran while one was open for 8% -> 9% of each run, Pallas kernels for 24% -> 27%
where the time goes in v3:
time: 170 us; the launch traced here: 169 us
  waiting for transfers between devices  63.3 us (37%)
  Pallas kernels  53.3 us (31%)
  starting transfers between devices  33.1 us (19%)
  matrix products  15.2 us (9%)
  local copies, waits for them, and re-layouts  3.22 us (2%)
    all_to_all x4, waiting for transfers between devices, exchange(): lax.all_to_all(rows, axes, split_axis=0, concat_axis=0, tiled=True)  41.2 us
    all_to_all x4, starting transfers between devices, exchange(): lax.all_to_all(rows, axes, split_axis=0, concat_axis=0, tiled=True)  23.2 us
    ppermute x6, waiting for transfers between devices, from_plane(): return lax.ppermute(value, 'ex', [(z, z ^ b) for z in range(PLANES)])  22.1 us
    pallas_call x2, Pallas kernels, shards(): call(forward_kernel, (2,), [fixed((plane_rows, width))] * 2 + weights + [...  17.1 us
    pallas_call x1, Pallas kernels, shards(): call(backward_kernel, (groups,), [rows_of(SIZE, width), strip(hidden_widt...  16.4 us
    ppermute x6, starting transfers between devices, from_plane(): return lax.ppermute(value, 'ex', [(z, z ^ b) for z in range(PLANES)])  9.86 us
    pallas_call x1, Pallas kernels, shards(): call(moe_kernel, (PLANES,), [rows_of(plane_rows * PIECES, piece), fixed(p...  7.45 us
    dot_general x1, matrix products, shards(): grad_gate = jnp.dot(rows.T, d_gate, preferred_element_type=F32).astype(BF16)  6.94 us
  transfers between devices with their start and end apart: 10, of which 8 were waited for; matrix products, arithmetic and copies ran while one was open for 9% of the time, Pallas kernels for 27%

profile of v3, /device:TPU:0, one launch (start us, length us, event | category | flops | bytes accessed | tf_op | source)
XLA Modules:
  0.0 168.8 jit_solution(16559933696620896158)
XLA Ops:
  0.6 0.0 copy-start.6
  0.6 3.3 %shard_map.136 = (s32[4,128]{1,0:T(4,128)S(1)}, bf16[144,1024]{1,0:T(8,128)(2,1)S(1)}, bf16[1280,512]{1,0:T(8,128)(2,1)}) custom-call(s32[4,128]{1,0:T(4,128)} %bitcast.56, f32[4,128]{1,0:T(4,128)} %bitcast.47, bf16[128,1024]{1,0:T(8,128)(2,1)} %latent_ref.1, bf16[128,1024]{1,0:T(8,128)(2,1)} %cotangent_ref.3, bf16[320,320]{1,0:T(8,128)(2,1)} %constant.9.clone.together.refs_4_), custom_call_target="tpu_custom_call" | custom-call | flops 335544320 | bytes 2883584 | tf_op jit(solution)/shard_map/pallas_call | solution.py:311
  4.0 4.2 %collective-permute-start.2 = (bf16[144,1024]{1,0:T(8,128)(2,1)S(1)}, bf16[144,1024]{1,0:T(8,128)(2,1)S(1)}, u32[]{:S(2)}, u32[]{:S(2)}) collective-permute-start(bf16[144,1024]{1,0:T(8,128)(2,1)S(1)} %get-tuple-element.33.refs_0_), channel_id=1, source_target_pairs={{0,3},{1,2},{2,1},{3,0},{4,7},{5,6},{6,5},{7,4},{8,11},{9,10},{10,... | collective-permute-start | bytes 884744 | tf_op jit(solution)/shard_map/ppermute | solution.py:290
  8.2 0.0 collective-permute-start.1
  8.2 0.9 collective-permute-start
  9.1 7.3 %all-to-all-start = ((bf16[32,40,512]{2,1,0:T(8,128)(2,1)}), bf16[32,40,512]{2,1,0:T(8,128)(2,1)S(1)}, u32[]{:S(2)}, u32[]{:S(2)}) async-start(bf16[32,40,512]{2,1,0:T(8,128)(2,1)} %bitcast.52), calls=%async_computation | async-start | bytes 2621440 | tf_op jit(solution)/shard_map/all_to_all | solution.py:286
  16.5 5.0 %collective-permute-done.2.refs_3_ = bf16[144,1024]{1,0:T(8,128)(2,1)S(1)} collective-permute-done((bf16[144,1024]{1,0:T(8,128)(2,1)S(1)}, bf16[144,1024]{1,0:T(8,128)(2,1)S(1)}, u32[]{:S(2)}, u32[]{:S(2)}) %collective-permute-start.2) | collective-permute-done | bytes 294944 | tf_op jit(solution)/shard_map/ppermute | solution.py:290
  21.5 0.0 collective-permute-done.1.refs_2_
  21.5 0.7 collective-permute-done.refs_1_
  22.2 0.0 copy-done.6
  22.2 0.0 copy-start
  22.2 4.0 %shard_map.138 = bf16[1280,1024]{1,0:T(8,128)(2,1)} custom-call(s32[1]{0:T(128)} %bitcast.z_ref, bf16[144,1024]{1,0:T(8,128)(2,1)S(1)} %get-tuple-element.33.refs_0_, bf16[144,1024]{1,0:T(8,128)(2,1)S(1)} %collective-permute-done.refs_1_, bf16[144,1024]{1,0:T(8,128)(2,1)S(1)} %collective-permute-done.1.refs_2_, ...), custom_call_target="tpu_custom_call" | custom-call | flops 80530636800 | bytes 2883584 | tf_op jit(solution)/shard_map/pallas_call | solution.py:331
  26.2 10.2 %all-to-all-done = bf16[32,40,512]{2,1,0:T(8,128)(2,1)S(1)} async-done(((bf16[32,40,512]{2,1,0:T(8,128)(2,1)}), bf16[32,40,512]{2,1,0:T(8,128)(2,1)S(1)}, u32[]{:S(2)}, u32[]{:S(2)}) %all-to-all-start) | async-done | bytes 1310752 | tf_op jit(solution)/shard_map/all_to_all | solution.py:286
  36.4 0.0 copy-done
  36.4 2.5 %shard_map.137 = (bf16[320,1024]{1,0:T(8,128)(2,1)}, bf16[320,1024]{1,0:T(8,128)(2,1)}) custom-call(s32[1]{0:T(128)} %bitcast.z_ref, bf16[1280,512]{1,0:T(8,128)(2,1)S(1)} %bitcast.40, bf16[320,320]{1,0:T(8,128)(2,1)S(1)} %copy-done), custom_call_target="tpu_custom_call" | custom-call | flops 838860800 | bytes 5242880 | tf_op jit(solution)/shard_map/pallas_call | solution.py:343
  38.9 1.1 collective-permute-start.5
  40.0 3.5 %collective-permute-start.4 = (bf16[320,1024]{1,0:T(8,128)(2,1)}, bf16[320,1024]{1,0:T(8,128)(2,1)S(1)}, u32[]{:S(2)}, u32[]{:S(2)}) collective-permute-start(bf16[320,1024]{1,0:T(8,128)(2,1)} %get-tuple-element.34), channel_id=1, source_target_pairs={{0,2},{1,3},{2,0},{3,1},{4,6},{5,7},{6,4},{7,5},{8,10},{9,11},{10,... | collective-permute-start | bytes 1966088 | tf_op jit(solution)/shard_map/ppermute | solution.py:290
  43.5 0.1 collective-permute-start.3
  43.6 0.0 copy-start.1
  43.6 0.0 copy-start.7
  43.6 4.9 %all-to-all-start.2 = ((bf16[32,40,1024]{2,1,0:T(8,128)(2,1)}), bf16[32,40,1024]{2,1,0:T(8,128)(2,1)}, u32[]{:S(2)}, u32[]{:S(2)}) async-start(bf16[32,40,1024]{2,1,0:T(8,128)(2,1)} %bitcast.49), calls=%async_computation.2 | async-start | bytes 5242880 | tf_op jit(solution)/shard_map/all_to_all | solution.py:286
  48.6 8.2 %collective-permute-done.5.second_ref = bf16[320,1024]{1,0:T(8,128)(2,1)} collective-permute-done((bf16[320,1024]{1,0:T(8,128)(2,1)}, bf16[320,1024]{1,0:T(8,128)(2,1)}, u32[]{:S(2)}, u32[]{:S(2)}) %collective-permute-start.5) | collective-permute-done | bytes 655392 | tf_op jit(solution)/shard_map/ppermute | solution.py:290
  56.8 0.0 copy-done.1
  56.8 0.0 copy-done.7
  56.8 0.0 copy-start.2
  56.8 1.6 copy-done.2
  58.4 8.8 %shard_map.139 = (bf16[4,320,1024]{2,1,0:T(8,128)(2,1)}, f32[4,320,1024]{2,1,0:T(8,128)}, f32[4,320,1024]{2,1,0:T(8,128)}, bf16[4,320,1024]{2,1,0:T(8,128)(2,1)}, bf16[4,1280,256]{2,1,0:T(8,128)(2,1)}) custom-call(s32[1]{0:T(128)} %bitcast.z_ref, bf16[320,1024]{1,0:T(8,128)(2,1)} %get-tuple-element.35.first_ref, ...), custom_call_target="tpu_custom_call" | custom-call | flops 32212254720 | bytes 18087936 | tf_op jit(solution)/shard_map/pallas_call | solution.py:371
  67.2 5.5 %collective-permute-done.4.second_ref = bf16[320,1024]{1,0:T(8,128)(2,1)S(1)} collective-permute-done((bf16[320,1024]{1,0:T(8,128)(2,1)}, bf16[320,1024]{1,0:T(8,128)(2,1)S(1)}, u32[]{:S(2)}, u32[]{:S(2)}) %collective-permute-start.4) | collective-permute-done | bytes 655392 | tf_op jit(solution)/shard_map/ppermute | solution.py:290
  72.6 2.7 %collective-permute-done.3.first_ref = bf16[320,1024]{1,0:T(8,128)(2,1)} collective-permute-done((bf16[320,1024]{1,0:T(8,128)(2,1)}, bf16[320,1024]{1,0:T(8,128)(2,1)}, u32[]{:S(2)}, u32[]{:S(2)}) %collective-permute-start.3) | collective-permute-done | bytes 655392 | tf_op jit(solution)/shard_map/ppermute | solution.py:290
  75.3 8.3 %shard_map.140 = (bf16[4,320,1024]{2,1,0:T(8,128)(2,1)}, f32[4,320,1024]{2,1,0:T(8,128)}, f32[4,320,1024]{2,1,0:T(8,128)}, bf16[4,320,1024]{2,1,0:T(8,128)(2,1)}, bf16[4,1280,256]{2,1,0:T(8,128)(2,1)}) custom-call(s32[1]{0:T(128)} %bitcast.z_ref, ...), custom_call_target="tpu_custom_call", output_to_operand_aliasing={{0}: (7, {}), {1}: (8, {}), {2}: (9, {}), {3}: (10, {}), {4... | custom-call | flops 32212254720 | bytes 18087936 | tf_op jit(solution)/shard_map/pallas_call | solution.py:371
  83.6 0.0 all-to-all-done.2
  83.6 6.3 %all-to-all-start.1 = ((bf16[128,40,256]{2,1,0:T(8,128)(2,1)}), bf16[128,40,256]{2,1,0:T(8,128)(2,1)}, u32[]{:S(2)}, u32[]{:S(2)}) async-start(bf16[128,40,256]{2,1,0:T(8,128)(2,1)} %bitcast.51), calls=%async_computation.1 | async-start | bytes 5242880 | tf_op jit(solution)/shard_map/all_to_all | solution.py:286
  89.9 0.0 copy-start.3
  89.9 1.6 copy-done.3
  91.5 16.4 %shard_map.142 = (bf16[4,320,1024]{2,1,0:T(8,128)(2,1)}, bf16[4,320,1024]{2,1,0:T(8,128)(2,1)}, bf16[4,320,1024]{2,1,0:T(8,128)(2,1)}, bf16[4,4,320,256]{3,2,1,0:T(8,128)(2,1)}) custom-call(s32[1]{0:T(128)} %bitcast.z_ref, bf16[1280,1024]{1,0:T(8,128)(2,1)} %bitcast.11.moved_ref, f32[4,320,1024]{2,1,0:T(8,128)} %get-tuple-element.45.active_ref, ...), custom_call_target="tpu_custom_call" | custom-call | flops 64424509440 | bytes 29884416 | tf_op jit(solution)/shard_map/pallas_call | solution.py:386
  107.9 17.6 %all-to-all-done.1 = bf16[128,40,256]{2,1,0:T(8,128)(2,1)} async-done(((bf16[128,40,256]{2,1,0:T(8,128)(2,1)}), bf16[128,40,256]{2,1,0:T(8,128)(2,1)}, u32[]{:S(2)}, u32[]{:S(2)}) %all-to-all-start.1) | async-done | bytes 2621472 | tf_op jit(solution)/shard_map/all_to_all | solution.py:286
  125.6 4.7 %all-to-all-start.3 = ((bf16[128,40,256]{2,1,0:T(8,128)(2,1)}), bf16[128,40,256]{2,1,0:T(8,128)(2,1)S(1)}, u32[]{:S(2)}, u32[]{:S(2)}) async-start(bf16[128,40,256]{2,1,0:T(8,128)(2,1)} %bitcast.50), calls=%async_computation.3 | async-start | bytes 5242880 | tf_op jit(solution)/shard_map/all_to_all | solution.py:286
  130.2 0.0 copy-start.9
  130.2 0.0 copy-start.11
  130.3 6.9 %fusion = bf16[1,1024,1024]{2,1,0:T(8,128)(2,1)} fusion(bf16[4,320,1024]{2,1,0:T(8,128)(2,1)} %get-tuple-element.49, bf16[4,320,1024]{2,1,0:T(8,128)(2,1)} %get-tuple-element.50), kind=kOutput, calls=%fused_computation.3 | convolution fusion | flops 2685403136 | bytes 7340032 | tf_op jit(solution)/shard_map/dot_general | solution.py:404
  137.2 0.0 copy-done.9
  137.2 0.0 copy-done.11
  137.2 0.0 copy-start.8
  137.2 0.0 copy-start.10
  137.2 4.1 %fusion.1 = bf16[1,1024,1024]{2,1,0:T(8,128)(2,1)} fusion(bf16[4,320,1024]{2,1,0:T(8,128)(2,1)S(1)} %copy-done.9, bf16[4,320,1024]{2,1,0:T(8,128)(2,1)S(1)} %copy-done.11), kind=kOutput, calls=%fused_computation.4 | convolution fusion | flops 2685403136 | bytes 7340032 | tf_op jit(solution)/shard_map/dot_general | solution.py:405
  141.3 0.0 copy-done.8
  141.3 0.0 copy-done.10
  141.3 0.0 copy-start.4
  141.3 0.0 copy-start.5
  141.3 4.1 %fusion.2 = bf16[1,1024,1024]{2,1,0:T(8,128)(2,1)} fusion(bf16[4,320,1024]{2,1,0:T(8,128)(2,1)S(1)} %copy-done.10, bf16[4,320,1024]{2,1,0:T(8,128)(2,1)S(1)} %copy-done.8), kind=kOutput, calls=%fused_computation.5 | convolution fusion | flops 2685403136 | bytes 7340032 | tf_op jit(solution)/shard_map/dot_general | solution.py:406
  145.5 0.0 copy-done.4
  145.5 0.0 copy-done.5
  145.5 7.5 %shard_map.141 = (bf16[128,1024]{1,0:T(8,128)(2,1)}, f32[4,128]{1,0:T(4,128)}) custom-call(bf16[5120,256]{1,0:T(8,128)(2,1)} %bitcast.9.back_ref, s32[4,128]{1,0:T(4,128)S(1)} %get-tuple-element.42.target_ref, f32[4,128]{1,0:T(4,128)S(1)} %bitcast.48, bf16[128,1024]{1,0:T(8,128)(2,1)S(1)} %copy-done.4, bf16[320,320]{1,0:T(8,128)(2,1)S(1)} %copy-done), custom_call_target="tpu_custom_call" | custom-call | flops 1342177280 | bytes 2621440 | tf_op jit(solution)/shard_map/pallas_call | solution.py:408
  152.9 13.3 %all-to-all-done.3 = bf16[128,40,256]{2,1,0:T(8,128)(2,1)S(1)} async-done(((bf16[128,40,256]{2,1,0:T(8,128)(2,1)}), bf16[128,40,256]{2,1,0:T(8,128)(2,1)S(1)}, u32[]{:S(2)}, u32[]{:S(2)}) %all-to-all-start.3) | async-done | bytes 2621472 | tf_op jit(solution)/shard_map/all_to_all | solution.py:286
  166.3 2.6 %shard_map.143 = bf16[128,1024]{1,0:T(8,128)(2,1)} custom-call(bf16[5120,256]{1,0:T(8,128)(2,1)S(1)} %bitcast.39, s32[4,128]{1,0:T(4,128)S(1)} %get-tuple-element.42.target_ref, bf16[320,320]{1,0:T(8,128)(2,1)S(1)} %copy-done), custom_call_target="tpu_custom_call" | custom-call | flops 335544320 | bytes 2621440 | tf_op jit(solution)/shard_map/pallas_call | solution.py:418
Async XLA Ops:
  0.6 21.6 %copy-start.6 = (bf16[320,320]{1,0:T(8,128)(2,1)S(1)}, bf16[320,320]{1,0:T(8,128)(2,1)}, u32[]{:S(2)}) copy-start(bf16[320,320]{1,0:T(8,128)(2,1)} %constant.9.clone.together.refs_4_) | copy-start | bytes 614404
  4.0 17.5 %collective-permute-start.2 = (bf16[144,1024]{1,0:T(8,128)(2,1)S(1)}, bf16[144,1024]{1,0:T(8,128)(2,1)S(1)}, u32[]{:S(2)}, u32[]{:S(2)}) collective-permute-start(bf16[144,1024]{1,0:T(8,128)(2,1)S(1)} %get-tuple-element.33.refs_0_), channel_id=1, source_target_pairs={{0,3},{1,2},{2,1},{3,0},{4,7},{5,6},{6,5},{7,4},{8,11},{9,10},{10,... | collective-permute-start | bytes 884744 | tf_op jit(solution)/shard_map/ppermute | solution.py:290
  8.2 13.3 %collective-permute-start.1 = (bf16[144,1024]{1,0:T(8,128)(2,1)S(1)}, bf16[144,1024]{1,0:T(8,128)(2,1)S(1)}, u32[]{:S(2)}, u32[]{:S(2)}) collective-permute-start(bf16[144,1024]{1,0:T(8,128)(2,1)S(1)} %get-tuple-element.33.refs_0_), channel_id=1, source_target_pairs={{0,2},{1,3},{2,0},{3,1},{4,6},{5,7},{6,4},{7,5},{8,10},{9,11},{10,... | collective-permute-start | bytes 884744 | tf_op jit(solution)/shard_map/ppermute | solution.py:290
  8.2 14.0 %collective-permute-start = (bf16[144,1024]{1,0:T(8,128)(2,1)S(1)}, bf16[144,1024]{1,0:T(8,128)(2,1)S(1)}, u32[]{:S(2)}, u32[]{:S(2)}) collective-permute-start(bf16[144,1024]{1,0:T(8,128)(2,1)S(1)} %get-tuple-element.33.refs_0_), channel_id=1, source_target_pairs={{0,1},{1,0},{2,3},{3,2},{4,5},{5,4},{6,7},{7,6},{8,9},{9,8},{10,11... | collective-permute-start | bytes 884744 | tf_op jit(solution)/shard_map/ppermute | solution.py:290
  9.1 27.3 %all-to-all-start = ((bf16[32,40,512]{2,1,0:T(8,128)(2,1)}), bf16[32,40,512]{2,1,0:T(8,128)(2,1)S(1)}, u32[]{:S(2)}, u32[]{:S(2)}) async-start(bf16[32,40,512]{2,1,0:T(8,128)(2,1)} %bitcast.52), calls=%async_computation | async-start | bytes 2621440 | tf_op jit(solution)/shard_map/all_to_all | solution.py:286
  22.2 14.2 %copy-start = (bf16[320,320]{1,0:T(8,128)(2,1)S(1)}, bf16[320,320]{1,0:T(8,128)(2,1)}, u32[]{:S(2)}) copy-start(bf16[320,320]{1,0:T(8,128)(2,1)} %constant.8.clone.apart) | copy-start | bytes 614404
  38.9 17.9 %collective-permute-start.5 = (bf16[320,1024]{1,0:T(8,128)(2,1)}, bf16[320,1024]{1,0:T(8,128)(2,1)}, u32[]{:S(2)}, u32[]{:S(2)}) collective-permute-start(bf16[320,1024]{1,0:T(8,128)(2,1)} %get-tuple-element.35.first_ref), channel_id=1, source_target_pairs={{0,1},{1,0},{2,3},{3,2},{4,5},{5,4},{6,7},{7,6},{8,9},{9,8},{10,11... | collective-permute-start | bytes 1966088 | tf_op jit(solution)/shard_map/ppermute | solution.py:290
  40.0 32.6 %collective-permute-start.4 = (bf16[320,1024]{1,0:T(8,128)(2,1)}, bf16[320,1024]{1,0:T(8,128)(2,1)S(1)}, u32[]{:S(2)}, u32[]{:S(2)}) collective-permute-start(bf16[320,1024]{1,0:T(8,128)(2,1)} %get-tuple-element.34), channel_id=1, source_target_pairs={{0,2},{1,3},{2,0},{3,1},{4,6},{5,7},{6,4},{7,5},{8,10},{9,11},{10,... | collective-permute-start | bytes 1966088 | tf_op jit(solution)/shard_map/ppermute | solution.py:290
  43.5 31.8 %collective-permute-start.3 = (bf16[320,1024]{1,0:T(8,128)(2,1)}, bf16[320,1024]{1,0:T(8,128)(2,1)}, u32[]{:S(2)}, u32[]{:S(2)}) collective-permute-start(bf16[320,1024]{1,0:T(8,128)(2,1)} %get-tuple-element.34), channel_id=1, source_target_pairs={{0,3},{1,2},{2,1},{3,0},{4,7},{5,6},{6,5},{7,4},{8,11},{9,10},{10,... | collective-permute-start | bytes 1966088 | tf_op jit(solution)/shard_map/ppermute | solution.py:290
  43.6 13.2 %copy-start.1 = (bf16[1,1024,1024]{2,1,0:T(8,128)(2,1)S(1)}, bf16[1,1024,1024]{2,1,0:T(8,128)(2,1)}, u32[]{:S(2)}) copy-start(bf16[1,1024,1024]{2,1,0:T(8,128)(2,1)} %param.12) | copy-start | bytes 6291460
  43.6 13.2 %copy-start.7 = (bf16[320,320]{1,0:T(8,128)(2,1)S(1)}, bf16[320,320]{1,0:T(8,128)(2,1)}, u32[]{:S(2)}) copy-start(bf16[320,320]{1,0:T(8,128)(2,1)} %constant.9.clone.together.refs_4_) | copy-start | bytes 614404
  43.6 40.0 %all-to-all-start.2 = ((bf16[32,40,1024]{2,1,0:T(8,128)(2,1)}), bf16[32,40,1024]{2,1,0:T(8,128)(2,1)}, u32[]{:S(2)}, u32[]{:S(2)}) async-start(bf16[32,40,1024]{2,1,0:T(8,128)(2,1)} %bitcast.49), calls=%async_computation.2 | async-start | bytes 5242880 | tf_op jit(solution)/shard_map/all_to_all | solution.py:286
  56.8 1.6 copy-start.2
  83.6 42.0 %all-to-all-start.1 = ((bf16[128,40,256]{2,1,0:T(8,128)(2,1)}), bf16[128,40,256]{2,1,0:T(8,128)(2,1)}, u32[]{:S(2)}, u32[]{:S(2)}) async-start(bf16[128,40,256]{2,1,0:T(8,128)(2,1)} %bitcast.51), calls=%async_computation.1 | async-start | bytes 5242880 | tf_op jit(solution)/shard_map/all_to_all | solution.py:286
  89.9 1.6 copy-start.3
  125.6 40.7 %all-to-all-start.3 = ((bf16[128,40,256]{2,1,0:T(8,128)(2,1)}), bf16[128,40,256]{2,1,0:T(8,128)(2,1)S(1)}, u32[]{:S(2)}, u32[]{:S(2)}) async-start(bf16[128,40,256]{2,1,0:T(8,128)(2,1)} %bitcast.50), calls=%async_computation.3 | async-start | bytes 5242880 | tf_op jit(solution)/shard_map/all_to_all | solution.py:286
  130.2 7.0 %copy-start.9 = (bf16[4,320,1024]{2,1,0:T(8,128)(2,1)S(1)}, bf16[4,320,1024]{2,1,0:T(8,128)(2,1)}, u32[]{:S(2)}) copy-start(bf16[4,320,1024]{2,1,0:T(8,128)(2,1)} %get-tuple-element.49) | copy-start | bytes 7864324
  130.2 7.0 %copy-start.11 = (bf16[4,320,1024]{2,1,0:T(8,128)(2,1)S(1)}, bf16[4,320,1024]{2,1,0:T(8,128)(2,1)}, u32[]{:S(2)}) copy-start(bf16[4,320,1024]{2,1,0:T(8,128)(2,1)} %get-tuple-element.51) | copy-start | bytes 7864324
  137.2 4.1 %copy-start.8 = (bf16[4,320,1024]{2,1,0:T(8,128)(2,1)S(1)}, bf16[4,320,1024]{2,1,0:T(8,128)(2,1)}, u32[]{:S(2)}) copy-start(bf16[4,320,1024]{2,1,0:T(8,128)(2,1)} %get-tuple-element.53) | copy-start | bytes 7864324
  137.2 4.1 %copy-start.10 = (bf16[4,320,1024]{2,1,0:T(8,128)(2,1)S(1)}, bf16[4,320,1024]{2,1,0:T(8,128)(2,1)}, u32[]{:S(2)}) copy-start(bf16[4,320,1024]{2,1,0:T(8,128)(2,1)} %get-tuple-element.52) | copy-start | bytes 7864324
  141.3 4.1 %copy-start.4 = (bf16[128,1024]{1,0:T(8,128)(2,1)S(1)}, bf16[128,1024]{1,0:T(8,128)(2,1)}, u32[]{:S(2)}) copy-start(bf16[128,1024]{1,0:T(8,128)(2,1)} %cotangent_ref.3) | copy-start | bytes 786436
  141.3 4.1 %copy-start.5 = (f32[128,4]{0,1:T(4,128)S(1)}, f32[128,4]{0,1:T(4,128)}, u32[]{:S(2)}) copy-start(f32[128,4]{0,1:T(4,128)} %param.11) | copy-start | bytes 6148

commit v4 on v3

--- a/solution.py
+++ b/solution.py
@@ -14,10 +14,13 @@
 TOPK = 4
 CAP = 10
 PIECES = 4
-GROUP = 8
+GROUP = 4
 PLANES = 4
 INNER = GROUP * CAP
 SIZE = PIECES * INNER
+STEP_GROUP = 8
+STEP_INNER = STEP_GROUP * CAP
+STEP_SIZE = PIECES * STEP_INNER
 NOTES = 16
 VMEM_LIMIT = 48 * 1024 * 1024
 WIDE_LIMIT = 60 * 1024 * 1024
@@ -46,12 +49,13 @@
     return (2 * device + pair) * CAP + rows - CAP * device
 
 
-def apart_table():
-    table = np.zeros((SIZE, SIZE), np.float32)
-    for block in range(GROUP):
+def apart_table(group):
+    size = group * PIECES * CAP
+    table = np.zeros((size, size), np.float32)
+    for block in range(group):
         for piece in range(PIECES):
             for slot in range(CAP):
-                table[(piece * GROUP + block) * CAP + slot, (block * PIECES + piece) * CAP + slot] = 1
+                table[(piece * group + block) * CAP + slot, (block * PIECES + piece) * CAP + slot] = 1
     return table
 
 
@@ -100,7 +104,7 @@
 def send(groups, together, sent_ref, ready, sems):
     copies = []
     for group, rows in enumerate(groups):
-        ready[group] = dot(together[...], rows).astype(BF16)
+        ready[group] = dot(together[...], rows.astype(BF16)).astype(BF16)
         place = sent_ref.at[group * SIZE : (group + 1) * SIZE, :]
         copies.append(pltpu.make_async_copy(ready.at[group], place, sems.at[group]))
         copies[-1].start()
@@ -140,7 +144,7 @@
     for pair in range(2):
         codes = slot_codes(rows, pair)
         hit = functools.reduce(jnp.logical_or, [codes == target for target in targets])
-        parts.append(dot(one_hot(hit), latent_ref[...]).astype(BF16))
+        parts.append(dot(one_hot(hit), latent_ref[...]))
     width = sent_ref.shape[1]
     groups = []
     for group in range(half // INNER):
@@ -166,7 +170,7 @@
             gate = value(2 * TOPK + k) + value(3 * TOPK + k) + value(4 * TOPK + k)
             hits.append(one_hot(codes == target))
             weighted.append((column(gate) * cotangent).astype(BF16))
-        planes.append(dot(jnp.concatenate(hits, axis=1), jnp.concatenate(weighted, axis=0)).astype(BF16))
+        planes.append(dot(jnp.concatenate(hits, axis=1), jnp.concatenate(weighted, axis=0)))
     groups = []
     for group in range(half // INNER):
         groups.append(jnp.concatenate([rows[group * INNER : (group + 1) * INNER, :] for rows in planes], axis=0))
@@ -174,22 +178,16 @@
 
 
 def split_kernel(z_ref, moved_ref, apart, own_ref, other_ref):
-    pair = z_ref[0] >> 1
+    first = (z_ref[0] >> 1) == 0
+    halves = [[], []]
     for group in range(moved_ref.shape[0] // SIZE):
-        mixed = dot(apart[...], moved_ref[group * SIZE : (group + 1) * SIZE, :]).astype(BF16)
-        quarters = [mixed[p * INNER : (p + 1) * INNER, :] for p in range(PIECES)]
-        rows = [jnp.concatenate([quarters[i], quarters[2 + i]], axis=1) for i in range(2)]
-        mine = slice(group * INNER, (group + 1) * INNER)
-
-        @pl.when(pair == 0)
-        def _():
-            own_ref[mine, :] = rows[0]
-            other_ref[mine, :] = rows[1]
-
-        @pl.when(pair == 1)
-        def _():
-            own_ref[mine, :] = rows[1]
-            other_ref[mine, :] = rows[0]
+        mixed = dot(apart[...], moved_ref[group * SIZE : (group + 1) * SIZE, :])
+        for i in range(2):
+            parts = [mixed[p * INNER : (p + 1) * INNER, :] for p in (i, 2 + i)]
+            halves[i].append(jnp.concatenate(parts, axis=1))
+    rows = [jnp.concatenate(half, axis=0) for half in halves]
+    own_ref[...] = jnp.where(first, rows[0], rows[1]).astype(BF16)
+    other_ref[...] = jnp.where(first, rows[1], rows[0]).astype(BF16)
 
 
 def forward_kernel(z_ref, first_ref, second_ref, w_gate, w_up, w_down, together, *refs):
@@ -213,9 +211,9 @@
     active_ref[0] = active
     slope_ref[0] = pre_up * (sigma * (1.0 + pre_gate * (1.0 - sigma)))
     hidden_ref[0] = hidden
-    done = dot(hidden, w_down[...]).astype(BF16)
+    done = dot(hidden, w_down[...])
     for group in range(done.shape[0] // INNER):
-        part = dot(together[...], pieces(done[group * INNER : (group + 1) * INNER, :]))
+        part = dot(together[...], pieces(done[group * INNER : (group + 1) * INNER, :]).astype(BF16))
         back_ref[0, group * SIZE : (group + 1) * SIZE, :] = part.astype(BF16)
 
 
@@ -228,18 +226,18 @@
     d_up = (d_hidden * active_ref[...].reshape(shape)).astype(BF16)
     d_gate_ref[...] = d_gate.reshape(d_gate_ref.shape)
     d_up_ref[...] = d_up.reshape(d_up_ref.shape)
-    d_rows = (dot(d_gate, w_gate[...], 1, 1) + dot(d_up, w_up[...], 1, 1)).astype(BF16)
+    d_rows = dot(d_gate, w_gate[...], 1, 1) + dot(d_up, w_up[...], 1, 1)
     for b in range(PLANES):
-        part = dot(together[...], pieces(d_rows[b * INNER : (b + 1) * INNER, :]))
+        part = dot(together[...], pieces(d_rows[b * STEP_INNER : (b + 1) * STEP_INNER, :]).astype(BF16))
         back_ref[z_ref[0] ^ b, 0] = part.astype(BF16)
 
 
 def unpack(back_ref, apart):
     groups = []
     for group in range(back_ref.shape[0] // SIZE):
-        mixed = dot(apart[...], back_ref[group * SIZE : (group + 1) * SIZE, :]).astype(BF16)
+        mixed = dot(apart[...], back_ref[group * SIZE : (group + 1) * SIZE, :])
         groups.append(jnp.concatenate([mixed[p * INNER : (p + 1) * INNER, :] for p in range(PIECES)], axis=1))
-    return jnp.concatenate(groups, axis=0)
+    return jnp.concatenate(groups, axis=0).astype(BF16)
 
 
 def moe_kernel(back_ref, target_ref, gates_ref, cotangent_ref, apart, moe_ref, gate_grad_ref, picked):
@@ -299,14 +297,16 @@
     plane_rows = columns * CAP
     total_rows = PLANES * plane_rows
     piece = width // PIECES
-    apart, together = jnp.asarray(apart_table(), BF16), jnp.asarray(apart_table().T, BF16)
+    apart, together = jnp.asarray(apart_table(GROUP), BF16), jnp.asarray(apart_table(GROUP).T, BF16)
+    step_apart, step_together = jnp.asarray(apart_table(STEP_GROUP), BF16), jnp.asarray(apart_table(STEP_GROUP).T, BF16)
     picks, gates = picks.T, gates.T
     z = lax.axis_index("ex").astype(I32).reshape(1)
     scalar = pl.BlockSpec(memory_space=pltpu.SMEM)
     anywhere = pl.BlockSpec(memory_space=pltpu.HBM)
     whole = pl.BlockSpec(memory_space=pltpu.VMEM)
     table = fixed((SIZE, SIZE))
-    groups = total_rows // SIZE
+    groups, steps = total_rows // SIZE, total_rows // STEP_SIZE
+    step_table = fixed((STEP_SIZE, STEP_SIZE))
 
     target, shared, sent = call(
         route_kernel,
@@ -382,22 +382,22 @@
     rows, active, slope, hidden, back = held
     returned = in_hbm(exchange(back, devices, ("ex", "ep")).reshape(-1, piece))
 
-    strip = lambda last: pl.BlockSpec((PLANES, INNER, last), lambda i, _: (0, i, 0))
+    strip = lambda last: pl.BlockSpec((PLANES, STEP_INNER, last), lambda i, _: (0, i, 0))
     d_rows, d_gate, d_up, d_back = call(
         backward_kernel,
-        (groups,),
-        [rows_of(SIZE, width), strip(hidden_width), strip(hidden_width)] + weights + [table, table],
-        [strip(width), strip(hidden_width), strip(hidden_width), pl.BlockSpec((PLANES, 1, SIZE, piece), lambda i, _: (0, i, 0, 0))],
+        (steps,),
+        [rows_of(STEP_SIZE, width), strip(hidden_width), strip(hidden_width)] + weights + [step_table, step_table],
+        [strip(width), strip(hidden_width), strip(hidden_width), pl.BlockSpec((PLANES, 1, STEP_SIZE, piece), lambda i, _: (0, i, 0, 0))],
         [
             jax.ShapeDtypeStruct((PLANES, plane_rows, width), BF16),
             jax.ShapeDtypeStruct(wide, BF16),
             jax.ShapeDtypeStruct(wide, BF16),
-            pltpu.HBM((PLANES, groups, SIZE, piece), BF16),
+            pltpu.HBM((PLANES, steps, STEP_SIZE, piece), BF16),
         ],
         flops=WEIGHT * 6 * total_rows * width * hidden_width,
         moved=6 * width * hidden_width + 18 * total_rows * width,
         prefetch=1,
-    )(z, d_moved, active, slope, w_gate, w_up, w_down, apart, together)
+    )(z, d_moved, active, slope, w_gate, w_up, w_down, step_apart, step_together)
     d_returned = exchange(d_back, devices, ("ex", "ep"))
 
     rows, hidden, d_rows, d_gate, d_up = [v.reshape(total_rows, -1) for v in (rows, hidden, d_rows, d_gate, d_up)]

time: 170 us -> 168 us (0.988)
  Pallas kernels: 53.3 us -> 50.2 us
  transfers between devices with their start and end apart: 10 -> 10, of which waited for: 8 -> 8; matrix products, arithmetic and copies ran while one was open for 9% -> 9% of each run, Pallas kernels for 27% -> 26%
where the time goes in v4:
time: 168 us; the launch traced here: 167 us
  waiting for transfers between devices  64.4 us (38%)
  Pallas kernels  50.2 us (30%)
  starting transfers between devices  33.1 us (20%)
  matrix products  15.2 us (9%)
  local copies, waits for them, and re-layouts  3.22 us (2%)
    all_to_all x4, waiting for transfers between devices, exchange(): lax.all_to_all(rows, axes, split_axis=0, concat_axis=0, tiled=True)  42.2 us
    all_to_all x4, starting transfers between devices, exchange(): lax.all_to_all(rows, axes, split_axis=0, concat_axis=0, tiled=True)  23.3 us
    ppermute x6, waiting for transfers between devices, from_plane(): return lax.ppermute(value, 'ex', [(z, z ^ b) for z in range(PLANES)])  22.2 us
    pallas_call x2, Pallas kernels, shards(): call(forward_kernel, (2,), [fixed((plane_rows, width))] * 2 + weights + [...  17.1 us
    pallas_call x1, Pallas kernels, shards(): call(backward_kernel, (steps,), [rows_of(STEP_SIZE, width), strip(hidden_...  16.5 us
    ppermute x6, starting transfers between devices, from_plane(): return lax.ppermute(value, 'ex', [(z, z ^ b) for z in range(PLANES)])  9.84 us
    dot_general x1, matrix products, shards(): grad_gate = jnp.dot(rows.T, d_gate, preferred_element_type=F32).astype(BF16)  6.94 us
    pallas_call x1, Pallas kernels, shards(): call(moe_kernel, (PLANES,), [rows_of(plane_rows * PIECES, piece), fixed(p...  6.82 us
  transfers between devices with their start and end apart: 10, of which 8 were waited for; matrix products, arithmetic and copies ran while one was open for 9% of the time, Pallas kernels for 26%

profile of v4, /device:TPU:0, one launch (start us, length us, event | category | flops | bytes accessed | tf_op | source)
XLA Modules:
  0.0 166.9 jit_solution(7709055294464006987)
XLA Ops:
  0.6 0.0 copy-start
  0.6 3.0 %shard_map.154 = (s32[4,128]{1,0:T(4,128)S(1)}, bf16[144,1024]{1,0:T(8,128)(2,1)S(1)}, bf16[1280,512]{1,0:T(8,128)(2,1)}) custom-call(s32[4,128]{1,0:T(4,128)} %bitcast.56, f32[4,128]{1,0:T(4,128)} %bitcast.47, bf16[128,1024]{1,0:T(8,128)(2,1)} %latent_ref.1, bf16[128,1024]{1,0:T(8,128)(2,1)} %cotangent_ref.3, ...), custom_call_target="tpu_custom_call" | custom-call | flops 335544320 | bytes 2883584 | tf_op jit(solution)/shard_map/pallas_call | solution.py:311
  3.6 4.2 %collective-permute-start.2 = (bf16[144,1024]{1,0:T(8,128)(2,1)S(1)}, bf16[144,1024]{1,0:T(8,128)(2,1)S(1)}, u32[]{:S(2)}, u32[]{:S(2)}) collective-permute-start(bf16[144,1024]{1,0:T(8,128)(2,1)S(1)} %get-tuple-element.33.refs_0_), channel_id=1, source_target_pairs={{0,3},{1,2},{2,1},{3,0},{4,7},{5,6},{6,5},{7,4},{8,11},{9,10},{10,... | collective-permute-start | bytes 884744 | tf_op jit(solution)/shard_map/ppermute | solution.py:288
  7.8 0.0 collective-permute-start.1
  7.8 0.9 collective-permute-start
  8.8 7.3 %all-to-all-start = ((bf16[32,40,512]{2,1,0:T(8,128)(2,1)}), bf16[32,40,512]{2,1,0:T(8,128)(2,1)S(1)}, u32[]{:S(2)}, u32[]{:S(2)}) async-start(bf16[32,40,512]{2,1,0:T(8,128)(2,1)} %bitcast.52), calls=%async_computation | async-start | bytes 2621440 | tf_op jit(solution)/shard_map/all_to_all | solution.py:284
  16.1 5.1 %collective-permute-done.2.refs_3_ = bf16[144,1024]{1,0:T(8,128)(2,1)S(1)} collective-permute-done((bf16[144,1024]{1,0:T(8,128)(2,1)S(1)}, bf16[144,1024]{1,0:T(8,128)(2,1)S(1)}, u32[]{:S(2)}, u32[]{:S(2)}) %collective-permute-start.2) | collective-permute-done | bytes 294944 | tf_op jit(solution)/shard_map/ppermute | solution.py:288
  21.2 0.0 collective-permute-done.1.refs_2_
  21.2 0.7 collective-permute-done.refs_1_
  21.9 0.0 copy-done
  21.9 3.3 %shard_map.156 = bf16[1280,1024]{1,0:T(8,128)(2,1)} custom-call(s32[1]{0:T(128)} %bitcast.z_ref, bf16[144,1024]{1,0:T(8,128)(2,1)S(1)} %get-tuple-element.33.refs_0_, bf16[144,1024]{1,0:T(8,128)(2,1)S(1)} %collective-permute-done.refs_1_, bf16[144,1024]{1,0:T(8,128)(2,1)S(1)} %collective-permute-done.1.refs_2_, ...), custom_call_target="tpu_custom_call" | custom-call | flops 80530636800 | bytes 2883584 | tf_op jit(solution)/shard_map/pallas_call | solution.py:331
  25.2 10.8 %all-to-all-done = bf16[32,40,512]{2,1,0:T(8,128)(2,1)S(1)} async-done(((bf16[32,40,512]{2,1,0:T(8,128)(2,1)}), bf16[32,40,512]{2,1,0:T(8,128)(2,1)S(1)}, u32[]{:S(2)}, u32[]{:S(2)}) %all-to-all-start) | async-done | bytes 1310752 | tf_op jit(solution)/shard_map/all_to_all | solution.py:284
  36.1 1.6 shard_map.155
  37.6 1.1 collective-permute-start.5
  38.7 3.5 %collective-permute-start.4 = (bf16[320,1024]{1,0:T(8,128)(2,1)}, bf16[320,1024]{1,0:T(8,128)(2,1)S(1)}, u32[]{:S(2)}, u32[]{:S(2)}) collective-permute-start(bf16[320,1024]{1,0:T(8,128)(2,1)} %get-tuple-element.34), channel_id=1, source_target_pairs={{0,2},{1,3},{2,0},{3,1},{4,6},{5,7},{6,4},{7,5},{8,10},{9,11},{10,... | collective-permute-start | bytes 1966088 | tf_op jit(solution)/shard_map/ppermute | solution.py:288
  42.2 0.1 collective-permute-start.3
  42.3 0.0 copy-start.1
  42.3 4.9 %all-to-all-start.2 = ((bf16[32,40,1024]{2,1,0:T(8,128)(2,1)}), bf16[32,40,1024]{2,1,0:T(8,128)(2,1)}, u32[]{:S(2)}, u32[]{:S(2)}) async-start(bf16[32,40,1024]{2,1,0:T(8,128)(2,1)} %bitcast.49), calls=%async_computation.2 | async-start | bytes 5242880 | tf_op jit(solution)/shard_map/all_to_all | solution.py:284
  47.3 8.2 %collective-permute-done.5.second_ref = bf16[320,1024]{1,0:T(8,128)(2,1)} collective-permute-done((bf16[320,1024]{1,0:T(8,128)(2,1)}, bf16[320,1024]{1,0:T(8,128)(2,1)}, u32[]{:S(2)}, u32[]{:S(2)}) %collective-permute-start.5) | collective-permute-done | bytes 655392 | tf_op jit(solution)/shard_map/ppermute | solution.py:288
  55.5 0.0 copy-done.1
  55.5 0.0 copy-start.2
  55.5 1.6 copy-done.2
  57.1 8.6 %shard_map.157 = (bf16[4,320,1024]{2,1,0:T(8,128)(2,1)}, f32[4,320,1024]{2,1,0:T(8,128)}, f32[4,320,1024]{2,1,0:T(8,128)}, bf16[4,320,1024]{2,1,0:T(8,128)(2,1)}, bf16[4,1280,256]{2,1,0:T(8,128)(2,1)}) custom-call(s32[1]{0:T(128)} %bitcast.z_ref, bf16[320,1024]{1,0:T(8,128)(2,1)} %get-tuple-element.35.first_ref, ...), custom_call_target="tpu_custom_call" | custom-call | flops 32212254720 | bytes 18087936 | tf_op jit(solution)/shard_map/pallas_call | solution.py:371
  65.7 5.6 %collective-permute-done.4.second_ref = bf16[320,1024]{1,0:T(8,128)(2,1)S(1)} collective-permute-done((bf16[320,1024]{1,0:T(8,128)(2,1)}, bf16[320,1024]{1,0:T(8,128)(2,1)S(1)}, u32[]{:S(2)}, u32[]{:S(2)}) %collective-permute-start.4) | collective-permute-done | bytes 655392 | tf_op jit(solution)/shard_map/ppermute | solution.py:288
  71.3 2.7 %collective-permute-done.3.first_ref = bf16[320,1024]{1,0:T(8,128)(2,1)} collective-permute-done((bf16[320,1024]{1,0:T(8,128)(2,1)}, bf16[320,1024]{1,0:T(8,128)(2,1)}, u32[]{:S(2)}, u32[]{:S(2)}) %collective-permute-start.3) | collective-permute-done | bytes 655392 | tf_op jit(solution)/shard_map/ppermute | solution.py:288
  74.0 8.4 %shard_map.158 = (bf16[4,320,1024]{2,1,0:T(8,128)(2,1)}, f32[4,320,1024]{2,1,0:T(8,128)}, f32[4,320,1024]{2,1,0:T(8,128)}, bf16[4,320,1024]{2,1,0:T(8,128)(2,1)}, bf16[4,1280,256]{2,1,0:T(8,128)(2,1)}) custom-call(s32[1]{0:T(128)} %bitcast.z_ref, ...), custom_call_target="tpu_custom_call", output_to_operand_aliasing={{0}: (7, {}), {1}: (8, {}), {2}: (9, {}), {3}: (10, {}), {4... | custom-call | flops 32212254720 | bytes 18087936 | tf_op jit(solution)/shard_map/pallas_call | solution.py:371
  82.4 0.0 all-to-all-done.2
  82.4 0.0 copy-start.6
  82.4 0.0 copy-start.7
  82.4 6.3 %all-to-all-start.1 = ((bf16[128,40,256]{2,1,0:T(8,128)(2,1)}), bf16[128,40,256]{2,1,0:T(8,128)(2,1)}, u32[]{:S(2)}, u32[]{:S(2)}) async-start(bf16[128,40,256]{2,1,0:T(8,128)(2,1)} %bitcast.51), calls=%async_computation.1 | async-start | bytes 5242880 | tf_op jit(solution)/shard_map/all_to_all | solution.py:284
  88.8 0.0 copy-done.6
  88.8 0.0 copy-done.7
  88.8 0.0 copy-start.3
  88.8 1.6 copy-done.3
  90.4 16.5 %shard_map.160 = (bf16[4,320,1024]{2,1,0:T(8,128)(2,1)}, bf16[4,320,1024]{2,1,0:T(8,128)(2,1)}, bf16[4,320,1024]{2,1,0:T(8,128)(2,1)}, bf16[4,4,320,256]{3,2,1,0:T(8,128)(2,1)}) custom-call(s32[1]{0:T(128)} %bitcast.z_ref, bf16[1280,1024]{1,0:T(8,128)(2,1)} %bitcast.11.moved_ref, f32[4,320,1024]{2,1,0:T(8,128)} %get-tuple-element.45.active_ref, ...), custom_call_target="tpu_custom_call" | custom-call | flops 64424509440 | bytes 29884416 | tf_op jit(solution)/shard_map/pallas_call | solution.py:386
  106.9 17.4 %all-to-all-done.1 = bf16[128,40,256]{2,1,0:T(8,128)(2,1)} async-done(((bf16[128,40,256]{2,1,0:T(8,128)(2,1)}), bf16[128,40,256]{2,1,0:T(8,128)(2,1)}, u32[]{:S(2)}, u32[]{:S(2)}) %all-to-all-start.1) | async-done | bytes 2621472 | tf_op jit(solution)/shard_map/all_to_all | solution.py:284
  124.3 4.7 %all-to-all-start.3 = ((bf16[128,40,256]{2,1,0:T(8,128)(2,1)}), bf16[128,40,256]{2,1,0:T(8,128)(2,1)S(1)}, u32[]{:S(2)}, u32[]{:S(2)}) async-start(bf16[128,40,256]{2,1,0:T(8,128)(2,1)} %bitcast.50), calls=%async_computation.3 | async-start | bytes 5242880 | tf_op jit(solution)/shard_map/all_to_all | solution.py:284
  128.9 0.0 copy-start.9
  128.9 0.0 copy-start.10
  129.0 6.9 %fusion = bf16[1,1024,1024]{2,1,0:T(8,128)(2,1)} fusion(bf16[4,320,1024]{2,1,0:T(8,128)(2,1)} %get-tuple-element.49, bf16[4,320,1024]{2,1,0:T(8,128)(2,1)} %get-tuple-element.50), kind=kOutput, calls=%fused_computation.3 | convolution fusion | flops 2685403136 | bytes 7340032 | tf_op jit(solution)/shard_map/dot_general | solution.py:404
  135.9 0.0 copy-done.9
  135.9 0.0 copy-done.10
  135.9 0.0 copy-start.8
  135.9 0.0 copy-start.11
  135.9 4.1 %fusion.1 = bf16[1,1024,1024]{2,1,0:T(8,128)(2,1)} fusion(bf16[4,320,1024]{2,1,0:T(8,128)(2,1)S(1)} %copy-done.10, bf16[4,320,1024]{2,1,0:T(8,128)(2,1)S(1)} %copy-done.9), kind=kOutput, calls=%fused_computation.4 | convolution fusion | flops 2685403136 | bytes 7340032 | tf_op jit(solution)/shard_map/dot_general | solution.py:405
  140.0 0.0 copy-done.8
  140.0 0.0 copy-done.11
  140.0 0.0 copy-start.4
  140.0 0.0 copy-start.5
  140.0 4.1 %fusion.2 = bf16[1,1024,1024]{2,1,0:T(8,128)(2,1)} fusion(bf16[4,320,1024]{2,1,0:T(8,128)(2,1)S(1)} %copy-done.11, bf16[4,320,1024]{2,1,0:T(8,128)(2,1)S(1)} %copy-done.8), kind=kOutput, calls=%fused_computation.5 | convolution fusion | flops 2685403136 | bytes 7340032 | tf_op jit(solution)/shard_map/dot_general | solution.py:406
  144.2 0.0 copy-done.4
  144.2 0.0 copy-done.5
  144.2 6.8 %shard_map.159 = (bf16[128,1024]{1,0:T(8,128)(2,1)}, f32[4,128]{1,0:T(4,128)}) custom-call(bf16[5120,256]{1,0:T(8,128)(2,1)} %bitcast.9.back_ref, s32[4,128]{1,0:T(4,128)S(1)} %get-tuple-element.42.target_ref, f32[4,128]{1,0:T(4,128)S(1)} %bitcast.48, bf16[128,1024]{1,0:T(8,128)(2,1)S(1)} %copy-done.4, bf16[160,160]{1,0:T(8,128)(2,1)S(1)} %copy-done), custom_call_target="tpu_custom_call" | custom-call | flops 1342177280 | bytes 2621440 | tf_op jit(solution)/shard_map/pallas_call | solution.py:408
  151.0 14.0 %all-to-all-done.3 = bf16[128,40,256]{2,1,0:T(8,128)(2,1)S(1)} async-done(((bf16[128,40,256]{2,1,0:T(8,128)(2,1)}), bf16[128,40,256]{2,1,0:T(8,128)(2,1)S(1)}, u32[]{:S(2)}, u32[]{:S(2)}) %all-to-all-start.3) | async-done | bytes 2621472 | tf_op jit(solution)/shard_map/all_to_all | solution.py:284
  165.0 1.9 %shard_map.161 = bf16[128,1024]{1,0:T(8,128)(2,1)} custom-call(bf16[5120,256]{1,0:T(8,128)(2,1)S(1)} %bitcast.39, s32[4,128]{1,0:T(4,128)S(1)} %get-tuple-element.42.target_ref, bf16[160,160]{1,0:T(8,128)(2,1)S(1)} %copy-done), custom_call_target="tpu_custom_call" | custom-call | flops 335544320 | bytes 2621440 | tf_op jit(solution)/shard_map/pallas_call | solution.py:418
Async XLA Ops:
  0.6 21.3 %copy-start = (bf16[160,160]{1,0:T(8,128)(2,1)S(1)}, bf16[160,160]{1,0:T(8,128)(2,1)}, u32[]{:S(2)}) copy-start(bf16[160,160]{1,0:T(8,128)(2,1)} %constant.10.clone.together.apart.refs_4_) | copy-start | bytes 153604
  3.6 17.5 %collective-permute-start.2 = (bf16[144,1024]{1,0:T(8,128)(2,1)S(1)}, bf16[144,1024]{1,0:T(8,128)(2,1)S(1)}, u32[]{:S(2)}, u32[]{:S(2)}) collective-permute-start(bf16[144,1024]{1,0:T(8,128)(2,1)S(1)} %get-tuple-element.33.refs_0_), channel_id=1, source_target_pairs={{0,3},{1,2},{2,1},{3,0},{4,7},{5,6},{6,5},{7,4},{8,11},{9,10},{10,... | collective-permute-start | bytes 884744 | tf_op jit(solution)/shard_map/ppermute | solution.py:288
  7.8 13.3 %collective-permute-start.1 = (bf16[144,1024]{1,0:T(8,128)(2,1)S(1)}, bf16[144,1024]{1,0:T(8,128)(2,1)S(1)}, u32[]{:S(2)}, u32[]{:S(2)}) collective-permute-start(bf16[144,1024]{1,0:T(8,128)(2,1)S(1)} %get-tuple-element.33.refs_0_), channel_id=1, source_target_pairs={{0,2},{1,3},{2,0},{3,1},{4,6},{5,7},{6,4},{7,5},{8,10},{9,11},{10,... | collective-permute-start | bytes 884744 | tf_op jit(solution)/shard_map/ppermute | solution.py:288
  7.8 14.0 %collective-permute-start = (bf16[144,1024]{1,0:T(8,128)(2,1)S(1)}, bf16[144,1024]{1,0:T(8,128)(2,1)S(1)}, u32[]{:S(2)}, u32[]{:S(2)}) collective-permute-start(bf16[144,1024]{1,0:T(8,128)(2,1)S(1)} %get-tuple-element.33.refs_0_), channel_id=1, source_target_pairs={{0,1},{1,0},{2,3},{3,2},{4,5},{5,4},{6,7},{7,6},{8,9},{9,8},{10,11... | collective-permute-start | bytes 884744 | tf_op jit(solution)/shard_map/ppermute | solution.py:288
  8.8 27.3 %all-to-all-start = ((bf16[32,40,512]{2,1,0:T(8,128)(2,1)}), bf16[32,40,512]{2,1,0:T(8,128)(2,1)S(1)}, u32[]{:S(2)}, u32[]{:S(2)}) async-start(bf16[32,40,512]{2,1,0:T(8,128)(2,1)} %bitcast.52), calls=%async_computation | async-start | bytes 2621440 | tf_op jit(solution)/shard_map/all_to_all | solution.py:284
  37.6 17.9 %collective-permute-start.5 = (bf16[320,1024]{1,0:T(8,128)(2,1)}, bf16[320,1024]{1,0:T(8,128)(2,1)}, u32[]{:S(2)}, u32[]{:S(2)}) collective-permute-start(bf16[320,1024]{1,0:T(8,128)(2,1)} %get-tuple-element.35.first_ref), channel_id=1, source_target_pairs={{0,1},{1,0},{2,3},{3,2},{4,5},{5,4},{6,7},{7,6},{8,9},{9,8},{10,11... | collective-permute-start | bytes 1966088 | tf_op jit(solution)/shard_map/ppermute | solution.py:288
  38.7 32.6 %collective-permute-start.4 = (bf16[320,1024]{1,0:T(8,128)(2,1)}, bf16[320,1024]{1,0:T(8,128)(2,1)S(1)}, u32[]{:S(2)}, u32[]{:S(2)}) collective-permute-start(bf16[320,1024]{1,0:T(8,128)(2,1)} %get-tuple-element.34), channel_id=1, source_target_pairs={{0,2},{1,3},{2,0},{3,1},{4,6},{5,7},{6,4},{7,5},{8,10},{9,11},{10,... | collective-permute-start | bytes 1966088 | tf_op jit(solution)/shard_map/ppermute | solution.py:288
  42.2 31.8 %collective-permute-start.3 = (bf16[320,1024]{1,0:T(8,128)(2,1)}, bf16[320,1024]{1,0:T(8,128)(2,1)}, u32[]{:S(2)}, u32[]{:S(2)}) collective-permute-start(bf16[320,1024]{1,0:T(8,128)(2,1)} %get-tuple-element.34), channel_id=1, source_target_pairs={{0,3},{1,2},{2,1},{3,0},{4,7},{5,6},{6,5},{7,4},{8,11},{9,10},{10,... | collective-permute-start | bytes 1966088 | tf_op jit(solution)/shard_map/ppermute | solution.py:288
  42.3 13.2 %copy-start.1 = (bf16[1,1024,1024]{2,1,0:T(8,128)(2,1)S(1)}, bf16[1,1024,1024]{2,1,0:T(8,128)(2,1)}, u32[]{:S(2)}) copy-start(bf16[1,1024,1024]{2,1,0:T(8,128)(2,1)} %param.14) | copy-start | bytes 6291460
  42.3 40.1 %all-to-all-start.2 = ((bf16[32,40,1024]{2,1,0:T(8,128)(2,1)}), bf16[32,40,1024]{2,1,0:T(8,128)(2,1)}, u32[]{:S(2)}, u32[]{:S(2)}) async-start(bf16[32,40,1024]{2,1,0:T(8,128)(2,1)} %bitcast.49), calls=%async_computation.2 | async-start | bytes 5242880 | tf_op jit(solution)/shard_map/all_to_all | solution.py:284
  55.5 1.6 copy-start.2
  82.4 6.4 %copy-start.6 = (bf16[320,320]{1,0:T(8,128)(2,1)S(1)}, bf16[320,320]{1,0:T(8,128)(2,1)}, u32[]{:S(2)}) copy-start(bf16[320,320]{1,0:T(8,128)(2,1)} %constant.12.clone.together) | copy-start | bytes 614404
  82.4 6.4 %copy-start.7 = (bf16[320,320]{1,0:T(8,128)(2,1)S(1)}, bf16[320,320]{1,0:T(8,128)(2,1)}, u32[]{:S(2)}) copy-start(bf16[320,320]{1,0:T(8,128)(2,1)} %constant.11.clone.apart) | copy-start | bytes 614404
  82.4 41.8 %all-to-all-start.1 = ((bf16[128,40,256]{2,1,0:T(8,128)(2,1)}), bf16[128,40,256]{2,1,0:T(8,128)(2,1)}, u32[]{:S(2)}, u32[]{:S(2)}) async-start(bf16[128,40,256]{2,1,0:T(8,128)(2,1)} %bitcast.51), calls=%async_computation.1 | async-start | bytes 5242880 | tf_op jit(solution)/shard_map/all_to_all | solution.py:284
  88.8 1.6 copy-start.3
  124.3 40.7 %all-to-all-start.3 = ((bf16[128,40,256]{2,1,0:T(8,128)(2,1)}), bf16[128,40,256]{2,1,0:T(8,128)(2,1)S(1)}, u32[]{:S(2)}, u32[]{:S(2)}) async-start(bf16[128,40,256]{2,1,0:T(8,128)(2,1)} %bitcast.50), calls=%async_computation.3 | async-start | bytes 5242880 | tf_op jit(solution)/shard_map/all_to_all | solution.py:284
  128.9 7.0 %copy-start.9 = (bf16[4,320,1024]{2,1,0:T(8,128)(2,1)S(1)}, bf16[4,320,1024]{2,1,0:T(8,128)(2,1)}, u32[]{:S(2)}) copy-start(bf16[4,320,1024]{2,1,0:T(8,128)(2,1)} %get-tuple-element.51) | copy-start | bytes 7864324
  128.9 7.0 %copy-start.10 = (bf16[4,320,1024]{2,1,0:T(8,128)(2,1)S(1)}, bf16[4,320,1024]{2,1,0:T(8,128)(2,1)}, u32[]{:S(2)}) copy-start(bf16[4,320,1024]{2,1,0:T(8,128)(2,1)} %get-tuple-element.49) | copy-start | bytes 7864324
  135.9 4.1 %copy-start.8 = (bf16[4,320,1024]{2,1,0:T(8,128)(2,1)S(1)}, bf16[4,320,1024]{2,1,0:T(8,128)(2,1)}, u32[]{:S(2)}) copy-start(bf16[4,320,1024]{2,1,0:T(8,128)(2,1)} %get-tuple-element.53) | copy-start | bytes 7864324
  135.9 4.1 %copy-start.11 = (bf16[4,320,1024]{2,1,0:T(8,128)(2,1)S(1)}, bf16[4,320,1024]{2,1,0:T(8,128)(2,1)}, u32[]{:S(2)}) copy-start(bf16[4,320,1024]{2,1,0:T(8,128)(2,1)} %get-tuple-element.52) | copy-start | bytes 7864324
  140.0 4.1 %copy-start.4 = (bf16[128,1024]{1,0:T(8,128)(2,1)S(1)}, bf16[128,1024]{1,0:T(8,128)(2,1)}, u32[]{:S(2)}) copy-start(bf16[128,1024]{1,0:T(8,128)(2,1)} %cotangent_ref.3) | copy-start | bytes 786436
  140.0 4.1 %copy-start.5 = (f32[128,4]{0,1:T(4,128)S(1)}, f32[128,4]{0,1:T(4,128)}, u32[]{:S(2)}) copy-start(f32[128,4]{0,1:T(4,128)} %param.13) | copy-start | bytes 6148

commit v5 on v4

--- a/solution.py
+++ b/solution.py
@@ -350,7 +350,8 @@
         moved=4 * total_rows * width,
     )(z, moved, apart)
     own, other, d_sent = lax.optimization_barrier((own, other, d_sent))
-    planes = [own, from_plane(own, 1), from_plane(other, 2), from_plane(other, 3)]
+    far, near, pair = from_plane(other, 2), from_plane(other, 3), from_plane(own, 1)
+    planes = [own, pair, far, near]
     d_moved = in_hbm(exchange(d_sent, columns, "ep"))
 
     wide = (PLANES, plane_rows, hidden_width)

time: 168 us -> 168 us (level)
  no operation moved by 1% of the time
where the time goes in v5:
time: 168 us; the launch traced here: 167 us
  waiting for transfers between devices  64.4 us (38%)
  Pallas kernels  50.2 us (30%)
  starting transfers between devices  33.1 us (20%)
  matrix products  15.2 us (9%)
  local copies, waits for them, and re-layouts  3.22 us (2%)
    all_to_all x4, waiting for transfers between devices, exchange(): lax.all_to_all(rows, axes, split_axis=0, concat_axis=0, tiled=True)  42.2 us
    all_to_all x4, starting transfers between devices, exchange(): lax.all_to_all(rows, axes, split_axis=0, concat_axis=0, tiled=True)  23.3 us
    ppermute x6, waiting for transfers between devices, from_plane(): return lax.ppermute(value, 'ex', [(z, z ^ b) for z in range(PLANES)])  22.2 us
    pallas_call x2, Pallas kernels, shards(): call(forward_kernel, (2,), [fixed((plane_rows, width))] * 2 + weights + [...  17.1 us
    pallas_call x1, Pallas kernels, shards(): call(backward_kernel, (steps,), [rows_of(STEP_SIZE, width), strip(hidden_...  16.5 us
    ppermute x6, starting transfers between devices, from_plane(): return lax.ppermute(value, 'ex', [(z, z ^ b) for z in range(PLANES)])  9.84 us
    dot_general x1, matrix products, shards(): grad_gate = jnp.dot(rows.T, d_gate, preferred_element_type=F32).astype(BF16)  6.94 us
    pallas_call x1, Pallas kernels, shards(): call(moe_kernel, (PLANES,), [rows_of(plane_rows * PIECES, piece), fixed(p...  6.82 us
  transfers between devices with their start and end apart: 10, of which 8 were waited for; matrix products, arithmetic and copies ran while one was open for 9% of the time, Pallas kernels for 26%

profile of v5, /device:TPU:0, one launch (start us, length us, event | category | flops | bytes accessed | tf_op | source)
XLA Modules:
  0.0 166.9 jit_solution(7709055294464006987)
XLA Ops:
  0.6 0.0 copy-start
  0.6 3.0 %shard_map.154 = (s32[4,128]{1,0:T(4,128)S(1)}, bf16[144,1024]{1,0:T(8,128)(2,1)S(1)}, bf16[1280,512]{1,0:T(8,128)(2,1)}) custom-call(s32[4,128]{1,0:T(4,128)} %bitcast.56, f32[4,128]{1,0:T(4,128)} %bitcast.47, bf16[128,1024]{1,0:T(8,128)(2,1)} %latent_ref.1, bf16[128,1024]{1,0:T(8,128)(2,1)} %cotangent_ref.3, ...), custom_call_target="tpu_custom_call" | custom-call | flops 335544320 | bytes 2883584 | tf_op jit(solution)/shard_map/pallas_call | solution.py:311
  3.6 4.2 %collective-permute-start.2 = (bf16[144,1024]{1,0:T(8,128)(2,1)S(1)}, bf16[144,1024]{1,0:T(8,128)(2,1)S(1)}, u32[]{:S(2)}, u32[]{:S(2)}) collective-permute-start(bf16[144,1024]{1,0:T(8,128)(2,1)S(1)} %get-tuple-element.33.refs_0_), channel_id=1, source_target_pairs={{0,3},{1,2},{2,1},{3,0},{4,7},{5,6},{6,5},{7,4},{8,11},{9,10},{10,... | collective-permute-start | bytes 884744 | tf_op jit(solution)/shard_map/ppermute | solution.py:288
  7.8 0.0 collective-permute-start.1
  7.8 0.9 collective-permute-start
  8.8 7.3 %all-to-all-start = ((bf16[32,40,512]{2,1,0:T(8,128)(2,1)}), bf16[32,40,512]{2,1,0:T(8,128)(2,1)S(1)}, u32[]{:S(2)}, u32[]{:S(2)}) async-start(bf16[32,40,512]{2,1,0:T(8,128)(2,1)} %bitcast.52), calls=%async_computation | async-start | bytes 2621440 | tf_op jit(solution)/shard_map/all_to_all | solution.py:284
  16.1 5.1 %collective-permute-done.2.refs_3_ = bf16[144,1024]{1,0:T(8,128)(2,1)S(1)} collective-permute-done((bf16[144,1024]{1,0:T(8,128)(2,1)S(1)}, bf16[144,1024]{1,0:T(8,128)(2,1)S(1)}, u32[]{:S(2)}, u32[]{:S(2)}) %collective-permute-start.2) | collective-permute-done | bytes 294944 | tf_op jit(solution)/shard_map/ppermute | solution.py:288
  21.2 0.0 collective-permute-done.1.refs_2_
  21.2 0.7 collective-permute-done.refs_1_
  21.9 0.0 copy-done
  21.9 3.3 %shard_map.156 = bf16[1280,1024]{1,0:T(8,128)(2,1)} custom-call(s32[1]{0:T(128)} %bitcast.z_ref, bf16[144,1024]{1,0:T(8,128)(2,1)S(1)} %get-tuple-element.33.refs_0_, bf16[144,1024]{1,0:T(8,128)(2,1)S(1)} %collective-permute-done.refs_1_, bf16[144,1024]{1,0:T(8,128)(2,1)S(1)} %collective-permute-done.1.refs_2_, ...), custom_call_target="tpu_custom_call" | custom-call | flops 80530636800 | bytes 2883584 | tf_op jit(solution)/shard_map/pallas_call | solution.py:331
  25.2 10.8 %all-to-all-done = bf16[32,40,512]{2,1,0:T(8,128)(2,1)S(1)} async-done(((bf16[32,40,512]{2,1,0:T(8,128)(2,1)}), bf16[32,40,512]{2,1,0:T(8,128)(2,1)S(1)}, u32[]{:S(2)}, u32[]{:S(2)}) %all-to-all-start) | async-done | bytes 1310752 | tf_op jit(solution)/shard_map/all_to_all | solution.py:284
  36.1 1.6 shard_map.155
  37.6 1.1 collective-permute-start.5
  38.7 3.5 %collective-permute-start.4 = (bf16[320,1024]{1,0:T(8,128)(2,1)}, bf16[320,1024]{1,0:T(8,128)(2,1)S(1)}, u32[]{:S(2)}, u32[]{:S(2)}) collective-permute-start(bf16[320,1024]{1,0:T(8,128)(2,1)} %get-tuple-element.34), channel_id=1, source_target_pairs={{0,2},{1,3},{2,0},{3,1},{4,6},{5,7},{6,4},{7,5},{8,10},{9,11},{10,... | collective-permute-start | bytes 1966088 | tf_op jit(solution)/shard_map/ppermute | solution.py:288
  42.2 0.1 collective-permute-start.3
  42.3 0.0 copy-start.1
  42.3 4.9 %all-to-all-start.2 = ((bf16[32,40,1024]{2,1,0:T(8,128)(2,1)}), bf16[32,40,1024]{2,1,0:T(8,128)(2,1)}, u32[]{:S(2)}, u32[]{:S(2)}) async-start(bf16[32,40,1024]{2,1,0:T(8,128)(2,1)} %bitcast.49), calls=%async_computation.2 | async-start | bytes 5242880 | tf_op jit(solution)/shard_map/all_to_all | solution.py:284
  47.3 8.2 %collective-permute-done.5.second_ref = bf16[320,1024]{1,0:T(8,128)(2,1)} collective-permute-done((bf16[320,1024]{1,0:T(8,128)(2,1)}, bf16[320,1024]{1,0:T(8,128)(2,1)}, u32[]{:S(2)}, u32[]{:S(2)}) %collective-permute-start.5) | collective-permute-done | bytes 655392 | tf_op jit(solution)/shard_map/ppermute | solution.py:288
  55.5 0.0 copy-done.1
  55.5 0.0 copy-start.2
  55.5 1.6 copy-done.2
  57.1 8.6 %shard_map.157 = (bf16[4,320,1024]{2,1,0:T(8,128)(2,1)}, f32[4,320,1024]{2,1,0:T(8,128)}, f32[4,320,1024]{2,1,0:T(8,128)}, bf16[4,320,1024]{2,1,0:T(8,128)(2,1)}, bf16[4,1280,256]{2,1,0:T(8,128)(2,1)}) custom-call(s32[1]{0:T(128)} %bitcast.z_ref, bf16[320,1024]{1,0:T(8,128)(2,1)} %get-tuple-element.35.first_ref, ...), custom_call_target="tpu_custom_call" | custom-call | flops 32212254720 | bytes 18087936 | tf_op jit(solution)/shard_map/pallas_call | solution.py:372
  65.7 5.6 %collective-permute-done.4.second_ref = bf16[320,1024]{1,0:T(8,128)(2,1)S(1)} collective-permute-done((bf16[320,1024]{1,0:T(8,128)(2,1)}, bf16[320,1024]{1,0:T(8,128)(2,1)S(1)}, u32[]{:S(2)}, u32[]{:S(2)}) %collective-permute-start.4) | collective-permute-done | bytes 655392 | tf_op jit(solution)/shard_map/ppermute | solution.py:288
  71.3 2.7 %collective-permute-done.3.first_ref = bf16[320,1024]{1,0:T(8,128)(2,1)} collective-permute-done((bf16[320,1024]{1,0:T(8,128)(2,1)}, bf16[320,1024]{1,0:T(8,128)(2,1)}, u32[]{:S(2)}, u32[]{:S(2)}) %collective-permute-start.3) | collective-permute-done | bytes 655392 | tf_op jit(solution)/shard_map/ppermute | solution.py:288
  74.0 8.4 %shard_map.158 = (bf16[4,320,1024]{2,1,0:T(8,128)(2,1)}, f32[4,320,1024]{2,1,0:T(8,128)}, f32[4,320,1024]{2,1,0:T(8,128)}, bf16[4,320,1024]{2,1,0:T(8,128)(2,1)}, bf16[4,1280,256]{2,1,0:T(8,128)(2,1)}) custom-call(s32[1]{0:T(128)} %bitcast.z_ref, ...), custom_call_target="tpu_custom_call", output_to_operand_aliasing={{0}: (7, {}), {1}: (8, {}), {2}: (9, {}), {3}: (10, {}), {4... | custom-call | flops 32212254720 | bytes 18087936 | tf_op jit(solution)/shard_map/pallas_call | solution.py:372
  82.4 0.0 all-to-all-done.2
  82.4 0.0 copy-start.6
  82.4 0.0 copy-start.7
  82.4 6.3 %all-to-all-start.1 = ((bf16[128,40,256]{2,1,0:T(8,128)(2,1)}), bf16[128,40,256]{2,1,0:T(8,128)(2,1)}, u32[]{:S(2)}, u32[]{:S(2)}) async-start(bf16[128,40,256]{2,1,0:T(8,128)(2,1)} %bitcast.51), calls=%async_computation.1 | async-start | bytes 5242880 | tf_op jit(solution)/shard_map/all_to_all | solution.py:284
  88.8 0.0 copy-done.6
  88.8 0.0 copy-done.7
  88.8 0.0 copy-start.3
  88.8 1.6 copy-done.3
  90.4 16.5 %shard_map.160 = (bf16[4,320,1024]{2,1,0:T(8,128)(2,1)}, bf16[4,320,1024]{2,1,0:T(8,128)(2,1)}, bf16[4,320,1024]{2,1,0:T(8,128)(2,1)}, bf16[4,4,320,256]{3,2,1,0:T(8,128)(2,1)}) custom-call(s32[1]{0:T(128)} %bitcast.z_ref, bf16[1280,1024]{1,0:T(8,128)(2,1)} %bitcast.11.moved_ref, f32[4,320,1024]{2,1,0:T(8,128)} %get-tuple-element.45.active_ref, ...), custom_call_target="tpu_custom_call" | custom-call | flops 64424509440 | bytes 29884416 | tf_op jit(solution)/shard_map/pallas_call | solution.py:387
  106.9 17.4 %all-to-all-done.1 = bf16[128,40,256]{2,1,0:T(8,128)(2,1)} async-done(((bf16[128,40,256]{2,1,0:T(8,128)(2,1)}), bf16[128,40,256]{2,1,0:T(8,128)(2,1)}, u32[]{:S(2)}, u32[]{:S(2)}) %all-to-all-start.1) | async-done | bytes 2621472 | tf_op jit(solution)/shard_map/all_to_all | solution.py:284
  124.3 4.7 %all-to-all-start.3 = ((bf16[128,40,256]{2,1,0:T(8,128)(2,1)}), bf16[128,40,256]{2,1,0:T(8,128)(2,1)S(1)}, u32[]{:S(2)}, u32[]{:S(2)}) async-start(bf16[128,40,256]{2,1,0:T(8,128)(2,1)} %bitcast.50), calls=%async_computation.3 | async-start | bytes 5242880 | tf_op jit(solution)/shard_map/all_to_all | solution.py:284
  128.9 0.0 copy-start.9
  128.9 0.0 copy-start.10
  129.0 6.9 %fusion = bf16[1,1024,1024]{2,1,0:T(8,128)(2,1)} fusion(bf16[4,320,1024]{2,1,0:T(8,128)(2,1)} %get-tuple-element.49, bf16[4,320,1024]{2,1,0:T(8,128)(2,1)} %get-tuple-element.50), kind=kOutput, calls=%fused_computation.3 | convolution fusion | flops 2685403136 | bytes 7340032 | tf_op jit(solution)/shard_map/dot_general | solution.py:405
  135.9 0.0 copy-done.9
  135.9 0.0 copy-done.10
  135.9 0.0 copy-start.8
  135.9 0.0 copy-start.11
  135.9 4.1 %fusion.1 = bf16[1,1024,1024]{2,1,0:T(8,128)(2,1)} fusion(bf16[4,320,1024]{2,1,0:T(8,128)(2,1)S(1)} %copy-done.10, bf16[4,320,1024]{2,1,0:T(8,128)(2,1)S(1)} %copy-done.9), kind=kOutput, calls=%fused_computation.4 | convolution fusion | flops 2685403136 | bytes 7340032 | tf_op jit(solution)/shard_map/dot_general | solution.py:406
  140.0 0.0 copy-done.8
  140.0 0.0 copy-done.11
  140.0 0.0 copy-start.4
  140.0 0.0 copy-start.5
  140.0 4.1 %fusion.2 = bf16[1,1024,1024]{2,1,0:T(8,128)(2,1)} fusion(bf16[4,320,1024]{2,1,0:T(8,128)(2,1)S(1)} %copy-done.11, bf16[4,320,1024]{2,1,0:T(8,128)(2,1)S(1)} %copy-done.8), kind=kOutput, calls=%fused_computation.5 | convolution fusion | flops 2685403136 | bytes 7340032 | tf_op jit(solution)/shard_map/dot_general | solution.py:407
  144.2 0.0 copy-done.4
  144.2 0.0 copy-done.5
  144.2 6.8 %shard_map.159 = (bf16[128,1024]{1,0:T(8,128)(2,1)}, f32[4,128]{1,0:T(4,128)}) custom-call(bf16[5120,256]{1,0:T(8,128)(2,1)} %bitcast.9.back_ref, s32[4,128]{1,0:T(4,128)S(1)} %get-tuple-element.42.target_ref, f32[4,128]{1,0:T(4,128)S(1)} %bitcast.48, bf16[128,1024]{1,0:T(8,128)(2,1)S(1)} %copy-done.4, bf16[160,160]{1,0:T(8,128)(2,1)S(1)} %copy-done), custom_call_target="tpu_custom_call" | custom-call | flops 1342177280 | bytes 2621440 | tf_op jit(solution)/shard_map/pallas_call | solution.py:409
  151.0 14.0 %all-to-all-done.3 = bf16[128,40,256]{2,1,0:T(8,128)(2,1)S(1)} async-done(((bf16[128,40,256]{2,1,0:T(8,128)(2,1)}), bf16[128,40,256]{2,1,0:T(8,128)(2,1)S(1)}, u32[]{:S(2)}, u32[]{:S(2)}) %all-to-all-start.3) | async-done | bytes 2621472 | tf_op jit(solution)/shard_map/all_to_all | solution.py:284
  165.0 1.9 %shard_map.161 = bf16[128,1024]{1,0:T(8,128)(2,1)} custom-call(bf16[5120,256]{1,0:T(8,128)(2,1)S(1)} %bitcast.39, s32[4,128]{1,0:T(4,128)S(1)} %get-tuple-element.42.target_ref, bf16[160,160]{1,0:T(8,128)(2,1)S(1)} %copy-done), custom_call_target="tpu_custom_call" | custom-call | flops 335544320 | bytes 2621440 | tf_op jit(solution)/shard_map/pallas_call | solution.py:419
Async XLA Ops:
  0.6 21.3 %copy-start = (bf16[160,160]{1,0:T(8,128)(2,1)S(1)}, bf16[160,160]{1,0:T(8,128)(2,1)}, u32[]{:S(2)}) copy-start(bf16[160,160]{1,0:T(8,128)(2,1)} %constant.10.clone.together.apart.refs_4_) | copy-start | bytes 153604
  3.6 17.5 %collective-permute-start.2 = (bf16[144,1024]{1,0:T(8,128)(2,1)S(1)}, bf16[144,1024]{1,0:T(8,128)(2,1)S(1)}, u32[]{:S(2)}, u32[]{:S(2)}) collective-permute-start(bf16[144,1024]{1,0:T(8,128)(2,1)S(1)} %get-tuple-element.33.refs_0_), channel_id=1, source_target_pairs={{0,3},{1,2},{2,1},{3,0},{4,7},{5,6},{6,5},{7,4},{8,11},{9,10},{10,... | collective-permute-start | bytes 884744 | tf_op jit(solution)/shard_map/ppermute | solution.py:288
  7.8 13.3 %collective-permute-start.1 = (bf16[144,1024]{1,0:T(8,128)(2,1)S(1)}, bf16[144,1024]{1,0:T(8,128)(2,1)S(1)}, u32[]{:S(2)}, u32[]{:S(2)}) collective-permute-start(bf16[144,1024]{1,0:T(8,128)(2,1)S(1)} %get-tuple-element.33.refs_0_), channel_id=1, source_target_pairs={{0,2},{1,3},{2,0},{3,1},{4,6},{5,7},{6,4},{7,5},{8,10},{9,11},{10,... | collective-permute-start | bytes 884744 | tf_op jit(solution)/shard_map/ppermute | solution.py:288
  7.8 14.0 %collective-permute-start = (bf16[144,1024]{1,0:T(8,128)(2,1)S(1)}, bf16[144,1024]{1,0:T(8,128)(2,1)S(1)}, u32[]{:S(2)}, u32[]{:S(2)}) collective-permute-start(bf16[144,1024]{1,0:T(8,128)(2,1)S(1)} %get-tuple-element.33.refs_0_), channel_id=1, source_target_pairs={{0,1},{1,0},{2,3},{3,2},{4,5},{5,4},{6,7},{7,6},{8,9},{9,8},{10,11... | collective-permute-start | bytes 884744 | tf_op jit(solution)/shard_map/ppermute | solution.py:288
  8.8 27.3 %all-to-all-start = ((bf16[32,40,512]{2,1,0:T(8,128)(2,1)}), bf16[32,40,512]{2,1,0:T(8,128)(2,1)S(1)}, u32[]{:S(2)}, u32[]{:S(2)}) async-start(bf16[32,40,512]{2,1,0:T(8,128)(2,1)} %bitcast.52), calls=%async_computation | async-start | bytes 2621440 | tf_op jit(solution)/shard_map/all_to_all | solution.py:284
  37.6 17.9 %collective-permute-start.5 = (bf16[320,1024]{1,0:T(8,128)(2,1)}, bf16[320,1024]{1,0:T(8,128)(2,1)}, u32[]{:S(2)}, u32[]{:S(2)}) collective-permute-start(bf16[320,1024]{1,0:T(8,128)(2,1)} %get-tuple-element.35.first_ref), channel_id=1, source_target_pairs={{0,1},{1,0},{2,3},{3,2},{4,5},{5,4},{6,7},{7,6},{8,9},{9,8},{10,11... | collective-permute-start | bytes 1966088 | tf_op jit(solution)/shard_map/ppermute | solution.py:288
  38.7 32.6 %collective-permute-start.4 = (bf16[320,1024]{1,0:T(8,128)(2,1)}, bf16[320,1024]{1,0:T(8,128)(2,1)S(1)}, u32[]{:S(2)}, u32[]{:S(2)}) collective-permute-start(bf16[320,1024]{1,0:T(8,128)(2,1)} %get-tuple-element.34), channel_id=1, source_target_pairs={{0,2},{1,3},{2,0},{3,1},{4,6},{5,7},{6,4},{7,5},{8,10},{9,11},{10,... | collective-permute-start | bytes 1966088 | tf_op jit(solution)/shard_map/ppermute | solution.py:288
  42.2 31.8 %collective-permute-start.3 = (bf16[320,1024]{1,0:T(8,128)(2,1)}, bf16[320,1024]{1,0:T(8,128)(2,1)}, u32[]{:S(2)}, u32[]{:S(2)}) collective-permute-start(bf16[320,1024]{1,0:T(8,128)(2,1)} %get-tuple-element.34), channel_id=1, source_target_pairs={{0,3},{1,2},{2,1},{3,0},{4,7},{5,6},{6,5},{7,4},{8,11},{9,10},{10,... | collective-permute-start | bytes 1966088 | tf_op jit(solution)/shard_map/ppermute | solution.py:288
  42.3 13.2 %copy-start.1 = (bf16[1,1024,1024]{2,1,0:T(8,128)(2,1)S(1)}, bf16[1,1024,1024]{2,1,0:T(8,128)(2,1)}, u32[]{:S(2)}) copy-start(bf16[1,1024,1024]{2,1,0:T(8,128)(2,1)} %param.14) | copy-start | bytes 6291460
  42.3 40.1 %all-to-all-start.2 = ((bf16[32,40,1024]{2,1,0:T(8,128)(2,1)}), bf16[32,40,1024]{2,1,0:T(8,128)(2,1)}, u32[]{:S(2)}, u32[]{:S(2)}) async-start(bf16[32,40,1024]{2,1,0:T(8,128)(2,1)} %bitcast.49), calls=%async_computation.2 | async-start | bytes 5242880 | tf_op jit(solution)/shard_map/all_to_all | solution.py:284
  55.5 1.6 copy-start.2
  82.4 6.4 %copy-start.6 = (bf16[320,320]{1,0:T(8,128)(2,1)S(1)}, bf16[320,320]{1,0:T(8,128)(2,1)}, u32[]{:S(2)}) copy-start(bf16[320,320]{1,0:T(8,128)(2,1)} %constant.12.clone.together) | copy-start | bytes 614404
  82.4 6.4 %copy-start.7 = (bf16[320,320]{1,0:T(8,128)(2,1)S(1)}, bf16[320,320]{1,0:T(8,128)(2,1)}, u32[]{:S(2)}) copy-start(bf16[320,320]{1,0:T(8,128)(2,1)} %constant.11.clone.apart) | copy-start | bytes 614404
  82.4 41.8 %all-to-all-start.1 = ((bf16[128,40,256]{2,1,0:T(8,128)(2,1)}), bf16[128,40,256]{2,1,0:T(8,128)(2,1)}, u32[]{:S(2)}, u32[]{:S(2)}) async-start(bf16[128,40,256]{2,1,0:T(8,128)(2,1)} %bitcast.51), calls=%async_computation.1 | async-start | bytes 5242880 | tf_op jit(solution)/shard_map/all_to_all | solution.py:284
  88.8 1.6 copy-start.3
  124.3 40.7 %all-to-all-start.3 = ((bf16[128,40,256]{2,1,0:T(8,128)(2,1)}), bf16[128,40,256]{2,1,0:T(8,128)(2,1)S(1)}, u32[]{:S(2)}, u32[]{:S(2)}) async-start(bf16[128,40,256]{2,1,0:T(8,128)(2,1)} %bitcast.50), calls=%async_computation.3 | async-start | bytes 5242880 | tf_op jit(solution)/shard_map/all_to_all | solution.py:284
  128.9 7.0 %copy-start.9 = (bf16[4,320,1024]{2,1,0:T(8,128)(2,1)S(1)}, bf16[4,320,1024]{2,1,0:T(8,128)(2,1)}, u32[]{:S(2)}) copy-start(bf16[4,320,1024]{2,1,0:T(8,128)(2,1)} %get-tuple-element.51) | copy-start | bytes 7864324
  128.9 7.0 %copy-start.10 = (bf16[4,320,1024]{2,1,0:T(8,128)(2,1)S(1)}, bf16[4,320,1024]{2,1,0:T(8,128)(2,1)}, u32[]{:S(2)}) copy-start(bf16[4,320,1024]{2,1,0:T(8,128)(2,1)} %get-tuple-element.49) | copy-start | bytes 7864324
  135.9 4.1 %copy-start.8 = (bf16[4,320,1024]{2,1,0:T(8,128)(2,1)S(1)}, bf16[4,320,1024]{2,1,0:T(8,128)(2,1)}, u32[]{:S(2)}) copy-start(bf16[4,320,1024]{2,1,0:T(8,128)(2,1)} %get-tuple-element.53) | copy-start | bytes 7864324
  135.9 4.1 %copy-start.11 = (bf16[4,320,1024]{2,1,0:T(8,128)(2,1)S(1)}, bf16[4,320,1024]{2,1,0:T(8,128)(2,1)}, u32[]{:S(2)}) copy-start(bf16[4,320,1024]{2,1,0:T(8,128)(2,1)} %get-tuple-element.52) | copy-start | bytes 7864324
  140.0 4.1 %copy-start.4 = (bf16[128,1024]{1,0:T(8,128)(2,1)S(1)}, bf16[128,1024]{1,0:T(8,128)(2,1)}, u32[]{:S(2)}) copy-start(bf16[128,1024]{1,0:T(8,128)(2,1)} %cotangent_ref.3) | copy-start | bytes 786436
  140.0 4.1 %copy-start.5 = (f32[128,4]{0,1:T(4,128)S(1)}, f32[128,4]{0,1:T(4,128)}, u32[]{:S(2)}) copy-start(f32[128,4]{0,1:T(4,128)} %param.13) | copy-start | bytes 6148

commit v6 on v5

--- a/solution.py
+++ b/solution.py
@@ -240,12 +240,13 @@
     return jnp.concatenate(groups, axis=0).astype(BF16)
 
 
-def moe_kernel(back_ref, target_ref, gates_ref, cotangent_ref, apart, moe_ref, gate_grad_ref, picked):
+def moe_kernel(back_ref, target_ref, gates_ref, cotangent_ref, apart, moe_ref, gate_grad_ref, table_ref, picked, named):
     step = pl.program_id(0)
     tokens = target_ref.shape[1]
     codes = slot_codes(row_numbers(back_ref.shape[0] // PIECES, tokens), step >> 1)
-    hits = jnp.concatenate([one_hot(codes == target_ref[k : k + 1, :]) for k in range(TOPK)], axis=1)
-    part = dot(hits, unpack(back_ref, apart), 0, 0)
+    masks = [codes == target_ref[k : k + 1, :] for k in range(TOPK)]
+    part = dot(jnp.concatenate([one_hot(mask) for mask in masks], axis=1), unpack(back_ref, apart), 0, 0)
+    named[step] = jnp.where(functools.reduce(jnp.logical_or, masks), 1.0, 0.0)
 
     @pl.when(step == 0)
     def _():
@@ -265,17 +266,11 @@
             term = column(gates_ref[k : k + 1, :]) * mine
             total = term if total is None else total + term
         moe_ref[...] = total.astype(BF16)
-
-
-def latent_kernel(back_ref, target_ref, apart, out_ref):
-    tokens = target_ref.shape[1]
-    half = back_ref.shape[0] // PIECES // PLANES
-    hits = []
-    for pair in range(2):
-        codes = slot_codes(row_numbers(half, tokens), pair)
-        hit = one_hot(functools.reduce(jnp.logical_or, [codes == target_ref[k : k + 1, :] for k in range(TOPK)]))
-        hits += [hit, hit]
-    out_ref[...] = dot(jnp.concatenate(hits, axis=0), unpack(back_ref, apart), 0, 0).astype(BF16)
+        table_ref[...] = named[...].reshape(-1, tokens).T.astype(BF16)
+
+
+def latent_kernel(back_ref, table_ref, apart, out_ref):
+    out_ref[...] = dot(table_ref[...], unpack(back_ref, apart)).astype(BF16)
 
 
 def exchange(rows, blocks, axes):
@@ -406,13 +401,17 @@
     grad_up = jnp.dot(rows.T, d_up, preferred_element_type=F32).astype(BF16)
     grad_down = jnp.dot(hidden.T, d_rows, preferred_element_type=F32).astype(BF16)
 
-    moe_out, gate_grad = call(
+    moe_out, gate_grad, named = call(
         moe_kernel,
         (PLANES,),
         [rows_of(plane_rows * PIECES, piece), fixed(picks.shape), fixed(gates.shape), fixed(cotangent.shape), table],
-        [fixed(latent.shape), fixed(gates.shape)],
-        [jax.ShapeDtypeStruct(latent.shape, BF16), jax.ShapeDtypeStruct(gates.shape, F32)],
-        [pltpu.VMEM((TOPK * tokens, width), F32)],
+        [fixed(latent.shape), fixed(gates.shape), fixed((tokens, total_rows))],
+        [
+            jax.ShapeDtypeStruct(latent.shape, BF16),
+            jax.ShapeDtypeStruct(gates.shape, F32),
+            jax.ShapeDtypeStruct((tokens, total_rows), BF16),
+        ],
+        [pltpu.VMEM((TOPK * tokens, width), F32), pltpu.VMEM((PLANES, plane_rows, tokens), F32)],
         flops=2 * total_rows * tokens * TOPK * width,
         moved=2 * total_rows * width,
     )(returned, target, gates, cotangent, apart)
@@ -424,7 +423,7 @@
         jax.ShapeDtypeStruct(latent.shape, BF16),
         flops=2 * total_rows * tokens * width,
         moved=2 * total_rows * width,
-    )(d_returned.reshape(-1, piece), target, apart)
+    )(d_returned.reshape(-1, piece), named, apart)
     return (moe_out, d_latent, gate_grad.T, grad_gate[None], grad_up[None], grad_down[None])
 
 

time: 168 us -> 168 us (level)
  no operation moved by 1% of the time
where the time goes in v6:
time: 168 us; the launch traced here: 167 us
  waiting for transfers between devices  64.3 us (38%)
  Pallas kernels  50.4 us (30%)
  starting transfers between devices  33.1 us (20%)
  matrix products  15.2 us (9%)
  local copies, waits for them, and re-layouts  3.22 us (2%)
    all_to_all x4, waiting for transfers between devices, exchange(): lax.all_to_all(rows, axes, split_axis=0, concat_axis=0, tiled=True)  42 us
    all_to_all x4, starting transfers between devices, exchange(): lax.all_to_all(rows, axes, split_axis=0, concat_axis=0, tiled=True)  23.3 us
    ppermute x6, waiting for transfers between devices, from_plane(): return lax.ppermute(value, 'ex', [(z, z ^ b) for z in range(PLANES)])  22.2 us
    pallas_call x2, Pallas kernels, shards(): call(forward_kernel, (2,), [fixed((plane_rows, width))] * 2 + weights + [...  17.1 us
    pallas_call x1, Pallas kernels, shards(): call(backward_kernel, (steps,), [rows_of(STEP_SIZE, width), strip(hidden_...  16.5 us
    ppermute x6, starting transfers between devices, from_plane(): return lax.ppermute(value, 'ex', [(z, z ^ b) for z in range(PLANES)])  9.84 us
    pallas_call x1, Pallas kernels, shards(): call(moe_kernel, (PLANES,), [rows_of(plane_rows * PIECES, piece), fixed(p...  7.01 us
    dot_general x1, matrix products, shards(): grad_gate = jnp.dot(rows.T, d_gate, preferred_element_type=F32).astype(BF16)  6.94 us
  transfers between devices with their start and end apart: 10, of which 8 were waited for; matrix products, arithmetic and copies ran while one was open for 9% of the time, Pallas kernels for 26%

profile of v6, /device:TPU:0, one launch (start us, length us, event | category | flops | bytes accessed | tf_op | source)
XLA Modules:
  0.0 166.9 jit_solution(15498090687333076492)
XLA Ops:
  0.6 0.0 copy-start
  0.6 3.0 %shard_map.154 = (s32[4,128]{1,0:T(4,128)S(1)}, bf16[144,1024]{1,0:T(8,128)(2,1)S(1)}, bf16[1280,512]{1,0:T(8,128)(2,1)}) custom-call(s32[4,128]{1,0:T(4,128)} %bitcast.56, f32[4,128]{1,0:T(4,128)} %bitcast.47, bf16[128,1024]{1,0:T(8,128)(2,1)} %latent_ref.1, bf16[128,1024]{1,0:T(8,128)(2,1)} %cotangent_ref.3, ...), custom_call_target="tpu_custom_call" | custom-call | flops 335544320 | bytes 2883584 | tf_op jit(solution)/shard_map/pallas_call | solution.py:306
  3.6 4.2 %collective-permute-start.2 = (bf16[144,1024]{1,0:T(8,128)(2,1)S(1)}, bf16[144,1024]{1,0:T(8,128)(2,1)S(1)}, u32[]{:S(2)}, u32[]{:S(2)}) collective-permute-start(bf16[144,1024]{1,0:T(8,128)(2,1)S(1)} %get-tuple-element.34.refs_0_), channel_id=1, source_target_pairs={{0,3},{1,2},{2,1},{3,0},{4,7},{5,6},{6,5},{7,4},{8,11},{9,10},{10,... | collective-permute-start | bytes 884744 | tf_op jit(solution)/shard_map/ppermute | solution.py:283
  7.8 0.0 collective-permute-start.1
  7.8 0.9 collective-permute-start
  8.8 7.3 %all-to-all-start = ((bf16[32,40,512]{2,1,0:T(8,128)(2,1)}), bf16[32,40,512]{2,1,0:T(8,128)(2,1)S(1)}, u32[]{:S(2)}, u32[]{:S(2)}) async-start(bf16[32,40,512]{2,1,0:T(8,128)(2,1)} %bitcast.52), calls=%async_computation | async-start | bytes 2621440 | tf_op jit(solution)/shard_map/all_to_all | solution.py:279
  16.1 5.1 %collective-permute-done.2.refs_3_ = bf16[144,1024]{1,0:T(8,128)(2,1)S(1)} collective-permute-done((bf16[144,1024]{1,0:T(8,128)(2,1)S(1)}, bf16[144,1024]{1,0:T(8,128)(2,1)S(1)}, u32[]{:S(2)}, u32[]{:S(2)}) %collective-permute-start.2) | collective-permute-done | bytes 294944 | tf_op jit(solution)/shard_map/ppermute | solution.py:283
  21.2 0.0 collective-permute-done.1.refs_2_
  21.2 0.7 collective-permute-done.refs_1_
  21.9 0.0 copy-done
  21.9 3.3 %shard_map.156 = bf16[1280,1024]{1,0:T(8,128)(2,1)} custom-call(s32[1]{0:T(128)} %bitcast.z_ref, bf16[144,1024]{1,0:T(8,128)(2,1)S(1)} %get-tuple-element.34.refs_0_, bf16[144,1024]{1,0:T(8,128)(2,1)S(1)} %collective-permute-done.refs_1_, bf16[144,1024]{1,0:T(8,128)(2,1)S(1)} %collective-permute-done.1.refs_2_, ...), custom_call_target="tpu_custom_call" | custom-call | flops 80530636800 | bytes 2883584 | tf_op jit(solution)/shard_map/pallas_call | solution.py:326
  25.2 10.8 %all-to-all-done = bf16[32,40,512]{2,1,0:T(8,128)(2,1)S(1)} async-done(((bf16[32,40,512]{2,1,0:T(8,128)(2,1)}), bf16[32,40,512]{2,1,0:T(8,128)(2,1)S(1)}, u32[]{:S(2)}, u32[]{:S(2)}) %all-to-all-start) | async-done | bytes 1310752 | tf_op jit(solution)/shard_map/all_to_all | solution.py:279
  36.1 1.6 shard_map.155
  37.6 1.1 collective-permute-start.5
  38.7 3.5 %collective-permute-start.4 = (bf16[320,1024]{1,0:T(8,128)(2,1)}, bf16[320,1024]{1,0:T(8,128)(2,1)S(1)}, u32[]{:S(2)}, u32[]{:S(2)}) collective-permute-start(bf16[320,1024]{1,0:T(8,128)(2,1)} %get-tuple-element.35), channel_id=1, source_target_pairs={{0,2},{1,3},{2,0},{3,1},{4,6},{5,7},{6,4},{7,5},{8,10},{9,11},{10,... | collective-permute-start | bytes 1966088 | tf_op jit(solution)/shard_map/ppermute | solution.py:283
  42.2 0.1 collective-permute-start.3
  42.3 0.0 copy-start.1
  42.3 4.9 %all-to-all-start.2 = ((bf16[32,40,1024]{2,1,0:T(8,128)(2,1)}), bf16[32,40,1024]{2,1,0:T(8,128)(2,1)}, u32[]{:S(2)}, u32[]{:S(2)}) async-start(bf16[32,40,1024]{2,1,0:T(8,128)(2,1)} %bitcast.49), calls=%async_computation.2 | async-start | bytes 5242880 | tf_op jit(solution)/shard_map/all_to_all | solution.py:279
  47.3 8.2 %collective-permute-done.5.second_ref = bf16[320,1024]{1,0:T(8,128)(2,1)} collective-permute-done((bf16[320,1024]{1,0:T(8,128)(2,1)}, bf16[320,1024]{1,0:T(8,128)(2,1)}, u32[]{:S(2)}, u32[]{:S(2)}) %collective-permute-start.5) | collective-permute-done | bytes 655392 | tf_op jit(solution)/shard_map/ppermute | solution.py:283
  55.5 0.0 copy-done.1
  55.5 0.0 copy-start.2
  55.5 1.6 copy-done.2
  57.1 8.6 %shard_map.157 = (bf16[4,320,1024]{2,1,0:T(8,128)(2,1)}, f32[4,320,1024]{2,1,0:T(8,128)}, f32[4,320,1024]{2,1,0:T(8,128)}, bf16[4,320,1024]{2,1,0:T(8,128)(2,1)}, bf16[4,1280,256]{2,1,0:T(8,128)(2,1)}) custom-call(s32[1]{0:T(128)} %bitcast.z_ref, bf16[320,1024]{1,0:T(8,128)(2,1)} %get-tuple-element.36.first_ref, ...), custom_call_target="tpu_custom_call" | custom-call | flops 32212254720 | bytes 18087936 | tf_op jit(solution)/shard_map/pallas_call | solution.py:367
  65.7 5.6 %collective-permute-done.4.second_ref = bf16[320,1024]{1,0:T(8,128)(2,1)S(1)} collective-permute-done((bf16[320,1024]{1,0:T(8,128)(2,1)}, bf16[320,1024]{1,0:T(8,128)(2,1)S(1)}, u32[]{:S(2)}, u32[]{:S(2)}) %collective-permute-start.4) | collective-permute-done | bytes 655392 | tf_op jit(solution)/shard_map/ppermute | solution.py:283
  71.3 2.7 %collective-permute-done.3.first_ref = bf16[320,1024]{1,0:T(8,128)(2,1)} collective-permute-done((bf16[320,1024]{1,0:T(8,128)(2,1)}, bf16[320,1024]{1,0:T(8,128)(2,1)}, u32[]{:S(2)}, u32[]{:S(2)}) %collective-permute-start.3) | collective-permute-done | bytes 655392 | tf_op jit(solution)/shard_map/ppermute | solution.py:283
  74.0 8.4 %shard_map.158 = (bf16[4,320,1024]{2,1,0:T(8,128)(2,1)}, f32[4,320,1024]{2,1,0:T(8,128)}, f32[4,320,1024]{2,1,0:T(8,128)}, bf16[4,320,1024]{2,1,0:T(8,128)(2,1)}, bf16[4,1280,256]{2,1,0:T(8,128)(2,1)}) custom-call(s32[1]{0:T(128)} %bitcast.z_ref, ...), custom_call_target="tpu_custom_call", output_to_operand_aliasing={{0}: (7, {}), {1}: (8, {}), {2}: (9, {}), {3}: (10, {}), {4... | custom-call | flops 32212254720 | bytes 18087936 | tf_op jit(solution)/shard_map/pallas_call | solution.py:367
  82.4 0.0 all-to-all-done.2
  82.4 0.0 copy-start.6
  82.4 0.0 copy-start.7
  82.4 6.3 %all-to-all-start.1 = ((bf16[128,40,256]{2,1,0:T(8,128)(2,1)}), bf16[128,40,256]{2,1,0:T(8,128)(2,1)}, u32[]{:S(2)}, u32[]{:S(2)}) async-start(bf16[128,40,256]{2,1,0:T(8,128)(2,1)} %bitcast.51), calls=%async_computation.1 | async-start | bytes 5242880 | tf_op jit(solution)/shard_map/all_to_all | solution.py:279
  88.8 0.0 copy-done.6
  88.8 0.0 copy-done.7
  88.8 0.0 copy-start.3
  88.8 1.6 copy-done.3
  90.4 16.5 %shard_map.160 = (bf16[4,320,1024]{2,1,0:T(8,128)(2,1)}, bf16[4,320,1024]{2,1,0:T(8,128)(2,1)}, bf16[4,320,1024]{2,1,0:T(8,128)(2,1)}, bf16[4,4,320,256]{3,2,1,0:T(8,128)(2,1)}) custom-call(s32[1]{0:T(128)} %bitcast.z_ref, bf16[1280,1024]{1,0:T(8,128)(2,1)} %bitcast.11.moved_ref, f32[4,320,1024]{2,1,0:T(8,128)} %get-tuple-element.46.active_ref, ...), custom_call_target="tpu_custom_call" | custom-call | flops 64424509440 | bytes 29884416 | tf_op jit(solution)/shard_map/pallas_call | solution.py:382
  106.9 17.4 %all-to-all-done.1 = bf16[128,40,256]{2,1,0:T(8,128)(2,1)} async-done(((bf16[128,40,256]{2,1,0:T(8,128)(2,1)}), bf16[128,40,256]{2,1,0:T(8,128)(2,1)}, u32[]{:S(2)}, u32[]{:S(2)}) %all-to-all-start.1) | async-done | bytes 2621472 | tf_op jit(solution)/shard_map/all_to_all | solution.py:279
  124.3 4.7 %all-to-all-start.3 = ((bf16[128,40,256]{2,1,0:T(8,128)(2,1)}), bf16[128,40,256]{2,1,0:T(8,128)(2,1)S(1)}, u32[]{:S(2)}, u32[]{:S(2)}) async-start(bf16[128,40,256]{2,1,0:T(8,128)(2,1)} %bitcast.50), calls=%async_computation.3 | async-start | bytes 5242880 | tf_op jit(solution)/shard_map/all_to_all | solution.py:279
  128.9 0.0 copy-start.9
  128.9 0.0 copy-start.10
  129.0 6.9 %fusion = bf16[1,1024,1024]{2,1,0:T(8,128)(2,1)} fusion(bf16[4,320,1024]{2,1,0:T(8,128)(2,1)} %get-tuple-element.51, bf16[4,320,1024]{2,1,0:T(8,128)(2,1)} %get-tuple-element.52), kind=kOutput, calls=%fused_computation.3 | convolution fusion | flops 2685403136 | bytes 7340032 | tf_op jit(solution)/shard_map/dot_general | solution.py:400
  135.9 0.0 copy-done.9
  135.9 0.0 copy-done.10
  135.9 0.0 copy-start.8
  135.9 0.0 copy-start.11
  135.9 4.1 %fusion.1 = bf16[1,1024,1024]{2,1,0:T(8,128)(2,1)} fusion(bf16[4,320,1024]{2,1,0:T(8,128)(2,1)S(1)} %copy-done.10, bf16[4,320,1024]{2,1,0:T(8,128)(2,1)S(1)} %copy-done.9), kind=kOutput, calls=%fused_computation.4 | convolution fusion | flops 2685403136 | bytes 7340032 | tf_op jit(solution)/shard_map/dot_general | solution.py:401
  140.0 0.0 copy-done.8
  140.0 0.0 copy-done.11
  140.0 0.0 copy-start.4
  140.0 0.0 copy-start.5
  140.0 4.1 %fusion.2 = bf16[1,1024,1024]{2,1,0:T(8,128)(2,1)} fusion(bf16[4,320,1024]{2,1,0:T(8,128)(2,1)S(1)} %copy-done.11, bf16[4,320,1024]{2,1,0:T(8,128)(2,1)S(1)} %copy-done.8), kind=kOutput, calls=%fused_computation.5 | convolution fusion | flops 2685403136 | bytes 7340032 | tf_op jit(solution)/shard_map/dot_general | solution.py:402
  144.2 0.0 copy-done.4
  144.2 0.0 copy-done.5
  144.2 7.0 %shard_map.159 = (bf16[128,1024]{1,0:T(8,128)(2,1)}, f32[4,128]{1,0:T(4,128)}, bf16[128,1280]{1,0:T(8,128)(2,1)S(1)}) custom-call(bf16[5120,256]{1,0:T(8,128)(2,1)} %bitcast.9.back_ref, s32[4,128]{1,0:T(4,128)S(1)} %get-tuple-element.43.target_ref, f32[4,128]{1,0:T(4,128)S(1)} %bitcast.48, bf16[128,1024]{1,0:T(8,128)(2,1)S(1)} %copy-done.4, ...), custom_call_target="tpu_custom_call" | custom-call | flops 1342177280 | bytes 2621440 | tf_op jit(solution)/shard_map/pallas_call | solution.py:404
  151.2 13.8 %all-to-all-done.3 = bf16[128,40,256]{2,1,0:T(8,128)(2,1)S(1)} async-done(((bf16[128,40,256]{2,1,0:T(8,128)(2,1)}), bf16[128,40,256]{2,1,0:T(8,128)(2,1)S(1)}, u32[]{:S(2)}, u32[]{:S(2)}) %all-to-all-start.3) | async-done | bytes 2621472 | tf_op jit(solution)/shard_map/all_to_all | solution.py:279
  165.0 1.9 %shard_map.161 = bf16[128,1024]{1,0:T(8,128)(2,1)} custom-call(bf16[5120,256]{1,0:T(8,128)(2,1)S(1)} %bitcast.39, bf16[128,1280]{1,0:T(8,128)(2,1)S(1)} %get-tuple-element.49.table_ref, bf16[160,160]{1,0:T(8,128)(2,1)S(1)} %copy-done), custom_call_target="tpu_custom_call" | custom-call | flops 335544320 | bytes 2621440 | tf_op jit(solution)/shard_map/pallas_call | solution.py:418
Async XLA Ops:
  0.6 21.3 %copy-start = (bf16[160,160]{1,0:T(8,128)(2,1)S(1)}, bf16[160,160]{1,0:T(8,128)(2,1)}, u32[]{:S(2)}) copy-start(bf16[160,160]{1,0:T(8,128)(2,1)} %constant.10.clone.together.apart.refs_4_) | copy-start | bytes 153604
  3.6 17.5 %collective-permute-start.2 = (bf16[144,1024]{1,0:T(8,128)(2,1)S(1)}, bf16[144,1024]{1,0:T(8,128)(2,1)S(1)}, u32[]{:S(2)}, u32[]{:S(2)}) collective-permute-start(bf16[144,1024]{1,0:T(8,128)(2,1)S(1)} %get-tuple-element.34.refs_0_), channel_id=1, source_target_pairs={{0,3},{1,2},{2,1},{3,0},{4,7},{5,6},{6,5},{7,4},{8,11},{9,10},{10,... | collective-permute-start | bytes 884744 | tf_op jit(solution)/shard_map/ppermute | solution.py:283
  7.8 13.3 %collective-permute-start.1 = (bf16[144,1024]{1,0:T(8,128)(2,1)S(1)}, bf16[144,1024]{1,0:T(8,128)(2,1)S(1)}, u32[]{:S(2)}, u32[]{:S(2)}) collective-permute-start(bf16[144,1024]{1,0:T(8,128)(2,1)S(1)} %get-tuple-element.34.refs_0_), channel_id=1, source_target_pairs={{0,2},{1,3},{2,0},{3,1},{4,6},{5,7},{6,4},{7,5},{8,10},{9,11},{10,... | collective-permute-start | bytes 884744 | tf_op jit(solution)/shard_map/ppermute | solution.py:283
  7.8 14.0 %collective-permute-start = (bf16[144,1024]{1,0:T(8,128)(2,1)S(1)}, bf16[144,1024]{1,0:T(8,128)(2,1)S(1)}, u32[]{:S(2)}, u32[]{:S(2)}) collective-permute-start(bf16[144,1024]{1,0:T(8,128)(2,1)S(1)} %get-tuple-element.34.refs_0_), channel_id=1, source_target_pairs={{0,1},{1,0},{2,3},{3,2},{4,5},{5,4},{6,7},{7,6},{8,9},{9,8},{10,11... | collective-permute-start | bytes 884744 | tf_op jit(solution)/shard_map/ppermute | solution.py:283
  8.8 27.3 %all-to-all-start = ((bf16[32,40,512]{2,1,0:T(8,128)(2,1)}), bf16[32,40,512]{2,1,0:T(8,128)(2,1)S(1)}, u32[]{:S(2)}, u32[]{:S(2)}) async-start(bf16[32,40,512]{2,1,0:T(8,128)(2,1)} %bitcast.52), calls=%async_computation | async-start | bytes 2621440 | tf_op jit(solution)/shard_map/all_to_all | solution.py:279
  37.6 17.9 %collective-permute-start.5 = (bf16[320,1024]{1,0:T(8,128)(2,1)}, bf16[320,1024]{1,0:T(8,128)(2,1)}, u32[]{:S(2)}, u32[]{:S(2)}) collective-permute-start(bf16[320,1024]{1,0:T(8,128)(2,1)} %get-tuple-element.36.first_ref), channel_id=1, source_target_pairs={{0,1},{1,0},{2,3},{3,2},{4,5},{5,4},{6,7},{7,6},{8,9},{9,8},{10,11... | collective-permute-start | bytes 1966088 | tf_op jit(solution)/shard_map/ppermute | solution.py:283
  38.7 32.6 %collective-permute-start.4 = (bf16[320,1024]{1,0:T(8,128)(2,1)}, bf16[320,1024]{1,0:T(8,128)(2,1)S(1)}, u32[]{:S(2)}, u32[]{:S(2)}) collective-permute-start(bf16[320,1024]{1,0:T(8,128)(2,1)} %get-tuple-element.35), channel_id=1, source_target_pairs={{0,2},{1,3},{2,0},{3,1},{4,6},{5,7},{6,4},{7,5},{8,10},{9,11},{10,... | collective-permute-start | bytes 1966088 | tf_op jit(solution)/shard_map/ppermute | solution.py:283
  42.2 31.8 %collective-permute-start.3 = (bf16[320,1024]{1,0:T(8,128)(2,1)}, bf16[320,1024]{1,0:T(8,128)(2,1)}, u32[]{:S(2)}, u32[]{:S(2)}) collective-permute-start(bf16[320,1024]{1,0:T(8,128)(2,1)} %get-tuple-element.35), channel_id=1, source_target_pairs={{0,3},{1,2},{2,1},{3,0},{4,7},{5,6},{6,5},{7,4},{8,11},{9,10},{10,... | collective-permute-start | bytes 1966088 | tf_op jit(solution)/shard_map/ppermute | solution.py:283
  42.3 13.2 %copy-start.1 = (bf16[1,1024,1024]{2,1,0:T(8,128)(2,1)S(1)}, bf16[1,1024,1024]{2,1,0:T(8,128)(2,1)}, u32[]{:S(2)}) copy-start(bf16[1,1024,1024]{2,1,0:T(8,128)(2,1)} %param.14) | copy-start | bytes 6291460
  42.3 40.1 %all-to-all-start.2 = ((bf16[32,40,1024]{2,1,0:T(8,128)(2,1)}), bf16[32,40,1024]{2,1,0:T(8,128)(2,1)}, u32[]{:S(2)}, u32[]{:S(2)}) async-start(bf16[32,40,1024]{2,1,0:T(8,128)(2,1)} %bitcast.49), calls=%async_computation.2 | async-start | bytes 5242880 | tf_op jit(solution)/shard_map/all_to_all | solution.py:279
  55.5 1.6 copy-start.2
  82.4 6.4 %copy-start.6 = (bf16[320,320]{1,0:T(8,128)(2,1)S(1)}, bf16[320,320]{1,0:T(8,128)(2,1)}, u32[]{:S(2)}) copy-start(bf16[320,320]{1,0:T(8,128)(2,1)} %constant.12.clone.together) | copy-start | bytes 614404
  82.4 6.4 %copy-start.7 = (bf16[320,320]{1,0:T(8,128)(2,1)S(1)}, bf16[320,320]{1,0:T(8,128)(2,1)}, u32[]{:S(2)}) copy-start(bf16[320,320]{1,0:T(8,128)(2,1)} %constant.11.clone.apart) | copy-start | bytes 614404
  82.4 41.8 %all-to-all-start.1 = ((bf16[128,40,256]{2,1,0:T(8,128)(2,1)}), bf16[128,40,256]{2,1,0:T(8,128)(2,1)}, u32[]{:S(2)}, u32[]{:S(2)}) async-start(bf16[128,40,256]{2,1,0:T(8,128)(2,1)} %bitcast.51), calls=%async_computation.1 | async-start | bytes 5242880 | tf_op jit(solution)/shard_map/all_to_all | solution.py:279
  88.8 1.6 copy-start.3
  124.3 40.7 %all-to-all-start.3 = ((bf16[128,40,256]{2,1,0:T(8,128)(2,1)}), bf16[128,40,256]{2,1,0:T(8,128)(2,1)S(1)}, u32[]{:S(2)}, u32[]{:S(2)}) async-start(bf16[128,40,256]{2,1,0:T(8,128)(2,1)} %bitcast.50), calls=%async_computation.3 | async-start | bytes 5242880 | tf_op jit(solution)/shard_map/all_to_all | solution.py:279
  128.9 7.0 %copy-start.9 = (bf16[4,320,1024]{2,1,0:T(8,128)(2,1)S(1)}, bf16[4,320,1024]{2,1,0:T(8,128)(2,1)}, u32[]{:S(2)}) copy-start(bf16[4,320,1024]{2,1,0:T(8,128)(2,1)} %get-tuple-element.53) | copy-start | bytes 7864324
  128.9 7.0 %copy-start.10 = (bf16[4,320,1024]{2,1,0:T(8,128)(2,1)S(1)}, bf16[4,320,1024]{2,1,0:T(8,128)(2,1)}, u32[]{:S(2)}) copy-start(bf16[4,320,1024]{2,1,0:T(8,128)(2,1)} %get-tuple-element.51) | copy-start | bytes 7864324
  135.9 4.1 %copy-start.8 = (bf16[4,320,1024]{2,1,0:T(8,128)(2,1)S(1)}, bf16[4,320,1024]{2,1,0:T(8,128)(2,1)}, u32[]{:S(2)}) copy-start(bf16[4,320,1024]{2,1,0:T(8,128)(2,1)} %get-tuple-element.55) | copy-start | bytes 7864324
  135.9 4.1 %copy-start.11 = (bf16[4,320,1024]{2,1,0:T(8,128)(2,1)S(1)}, bf16[4,320,1024]{2,1,0:T(8,128)(2,1)}, u32[]{:S(2)}) copy-start(bf16[4,320,1024]{2,1,0:T(8,128)(2,1)} %get-tuple-element.54) | copy-start | bytes 7864324
  140.0 4.1 %copy-start.4 = (bf16[128,1024]{1,0:T(8,128)(2,1)S(1)}, bf16[128,1024]{1,0:T(8,128)(2,1)}, u32[]{:S(2)}) copy-start(bf16[128,1024]{1,0:T(8,128)(2,1)} %cotangent_ref.3) | copy-start | bytes 786436
  140.0 4.1 %copy-start.5 = (f32[128,4]{0,1:T(4,128)S(1)}, f32[128,4]{0,1:T(4,128)}, u32[]{:S(2)}) copy-start(f32[128,4]{0,1:T(4,128)} %param.13) | copy-start | bytes 6148

commit v7 on v6

--- a/solution.py
+++ b/solution.py
@@ -101,13 +101,14 @@
     return jnp.concatenate([rows[:, p * width : (p + 1) * width] for p in range(count)], axis=0)
 
 
-def send(groups, together, sent_ref, ready, sems):
+def send(groups, together, sent_ref, ready, sems, beside=lambda: None):
     copies = []
     for group, rows in enumerate(groups):
         ready[group] = dot(together[...], rows.astype(BF16)).astype(BF16)
         place = sent_ref.at[group * SIZE : (group + 1) * SIZE, :]
         copies.append(pltpu.make_async_copy(ready.at[group], place, sems.at[group]))
         copies[-1].start()
+    beside()
     for copy in copies:
         copy.wait()
 
@@ -126,19 +127,6 @@
     targets = [picks[k : k + 1, :] * CAP + slots[k].astype(I32) for k in range(TOPK)]
     target_ref[...] = jnp.concatenate(targets, axis=0)
 
-    gates = [gates_ref[k : k + 1, :] for k in range(TOPK)]
-    high = [g.astype(BF16).astype(F32) for g in gates]
-    rest = [g - h for g, h in zip(gates, high)]
-    middle = [r.astype(BF16).astype(F32) for r in rest]
-    low = [r - m for r, m in zip(rest, middle)]
-    values = [picks[k : k + 1, :].astype(F32) for k in range(TOPK)] + slots + high + middle + low
-    across = cotangent_ref.shape[1] // tokens
-    notes[...] = jnp.zeros_like(notes)
-    for i, value in enumerate(values):
-        notes[i // across : i // across + 1, (i % across) * tokens : (i % across + 1) * tokens] = value
-    shared_ref[:tokens, :] = cotangent_ref[...]
-    shared_ref[tokens:, :] = notes[...].astype(BF16)
-
     rows = row_numbers(half, tokens)
     parts = []
     for pair in range(2):
@@ -150,7 +138,21 @@
     for group in range(half // INNER):
         mine = slice(group * INNER, (group + 1) * INNER)
         groups.append(jnp.concatenate([part[mine, p * width : (p + 1) * width] for p in range(2) for part in parts], axis=0))
-    send(groups, together, sent_ref, ready, sems)
+    def share():
+        gates = [gates_ref[k : k + 1, :] for k in range(TOPK)]
+        high = [g.astype(BF16).astype(F32) for g in gates]
+        rest = [g - h for g, h in zip(gates, high)]
+        middle = [r.astype(BF16).astype(F32) for r in rest]
+        low = [r - m for r, m in zip(rest, middle)]
+        values = [picks[k : k + 1, :].astype(F32) for k in range(TOPK)] + slots + high + middle + low
+        across = cotangent_ref.shape[1] // tokens
+        notes[...] = jnp.zeros_like(notes)
+        for i, value in enumerate(values):
+            notes[i // across : i // across + 1, (i % across) * tokens : (i % across + 1) * tokens] = value
+        shared_ref[:tokens, :] = cotangent_ref[...]
+        shared_ref[tokens:, :] = notes[...].astype(BF16)
+
+    send(groups, together, sent_ref, ready, sems, share)
 
 
 def share_kernel(z_ref, *refs):

time: 168 us -> 168 us (level)
  no operation moved by 1% of the time
where the time goes in v7:
time: 168 us; the launch traced here: 167 us
  waiting for transfers between devices  64.3 us (38%)
  Pallas kernels  50.4 us (30%)
  starting transfers between devices  33.1 us (20%)
  matrix products  15.2 us (9%)
  local copies, waits for them, and re-layouts  3.22 us (2%)
    all_to_all x4, waiting for transfers between devices, exchange(): lax.all_to_all(rows, axes, split_axis=0, concat_axis=0, tiled=True)  42 us
    all_to_all x4, starting transfers between devices, exchange(): lax.all_to_all(rows, axes, split_axis=0, concat_axis=0, tiled=True)  23.3 us
    ppermute x6, waiting for transfers between devices, from_plane(): return lax.ppermute(value, 'ex', [(z, z ^ b) for z in range(PLANES)])  22.2 us
    pallas_call x2, Pallas kernels, shards(): call(forward_kernel, (2,), [fixed((plane_rows, width))] * 2 + weights + [...  17.1 us
    pallas_call x1, Pallas kernels, shards(): call(backward_kernel, (steps,), [rows_of(STEP_SIZE, width), strip(hidden_...  16.5 us
    ppermute x6, starting transfers between devices, from_plane(): return lax.ppermute(value, 'ex', [(z, z ^ b) for z in range(PLANES)])  9.84 us
    pallas_call x1, Pallas kernels, shards(): call(moe_kernel, (PLANES,), [rows_of(plane_rows * PIECES, piece), fixed(p...  7.01 us
    dot_general x1, matrix products, shards(): grad_gate = jnp.dot(rows.T, d_gate, preferred_element_type=F32).astype(BF16)  6.94 us
  transfers between devices with their start and end apart: 10, of which 8 were waited for; matrix products, arithmetic and copies ran while one was open for 9% of the time, Pallas kernels for 26%

profile of v7, /device:TPU:0, one launch (start us, length us, event | category | flops | bytes accessed | tf_op | source)
XLA Modules:
  0.0 166.9 jit_solution(12033718869645935108)
XLA Ops:
  0.6 0.0 copy-start
  0.6 3.0 %shard_map.154 = (s32[4,128]{1,0:T(4,128)S(1)}, bf16[144,1024]{1,0:T(8,128)(2,1)S(1)}, bf16[1280,512]{1,0:T(8,128)(2,1)}) custom-call(s32[4,128]{1,0:T(4,128)} %bitcast.56, f32[4,128]{1,0:T(4,128)} %bitcast.47, bf16[128,1024]{1,0:T(8,128)(2,1)} %latent_ref.1, bf16[128,1024]{1,0:T(8,128)(2,1)} %cotangent_ref.3, ...), custom_call_target="tpu_custom_call" | custom-call | flops 335544320 | bytes 2883584 | tf_op jit(solution)/shard_map/pallas_call | solution.py:308
  3.6 4.2 %collective-permute-start.2 = (bf16[144,1024]{1,0:T(8,128)(2,1)S(1)}, bf16[144,1024]{1,0:T(8,128)(2,1)S(1)}, u32[]{:S(2)}, u32[]{:S(2)}) collective-permute-start(bf16[144,1024]{1,0:T(8,128)(2,1)S(1)} %get-tuple-element.34.refs_0_), channel_id=1, source_target_pairs={{0,3},{1,2},{2,1},{3,0},{4,7},{5,6},{6,5},{7,4},{8,11},{9,10},{10,... | collective-permute-start | bytes 884744 | tf_op jit(solution)/shard_map/ppermute | solution.py:285
  7.8 0.0 collective-permute-start.1
  7.8 0.9 collective-permute-start
  8.8 7.3 %all-to-all-start = ((bf16[32,40,512]{2,1,0:T(8,128)(2,1)}), bf16[32,40,512]{2,1,0:T(8,128)(2,1)S(1)}, u32[]{:S(2)}, u32[]{:S(2)}) async-start(bf16[32,40,512]{2,1,0:T(8,128)(2,1)} %bitcast.52), calls=%async_computation | async-start | bytes 2621440 | tf_op jit(solution)/shard_map/all_to_all | solution.py:281
  16.1 5.1 %collective-permute-done.2.refs_3_ = bf16[144,1024]{1,0:T(8,128)(2,1)S(1)} collective-permute-done((bf16[144,1024]{1,0:T(8,128)(2,1)S(1)}, bf16[144,1024]{1,0:T(8,128)(2,1)S(1)}, u32[]{:S(2)}, u32[]{:S(2)}) %collective-permute-start.2) | collective-permute-done | bytes 294944 | tf_op jit(solution)/shard_map/ppermute | solution.py:285
  21.2 0.0 collective-permute-done.1.refs_2_
  21.2 0.7 collective-permute-done.refs_1_
  21.9 0.0 copy-done
  21.9 3.3 %shard_map.156 = bf16[1280,1024]{1,0:T(8,128)(2,1)} custom-call(s32[1]{0:T(128)} %bitcast.z_ref, bf16[144,1024]{1,0:T(8,128)(2,1)S(1)} %get-tuple-element.34.refs_0_, bf16[144,1024]{1,0:T(8,128)(2,1)S(1)} %collective-permute-done.refs_1_, bf16[144,1024]{1,0:T(8,128)(2,1)S(1)} %collective-permute-done.1.refs_2_, ...), custom_call_target="tpu_custom_call" | custom-call | flops 80530636800 | bytes 2883584 | tf_op jit(solution)/shard_map/pallas_call | solution.py:328
  25.2 10.8 %all-to-all-done = bf16[32,40,512]{2,1,0:T(8,128)(2,1)S(1)} async-done(((bf16[32,40,512]{2,1,0:T(8,128)(2,1)}), bf16[32,40,512]{2,1,0:T(8,128)(2,1)S(1)}, u32[]{:S(2)}, u32[]{:S(2)}) %all-to-all-start) | async-done | bytes 1310752 | tf_op jit(solution)/shard_map/all_to_all | solution.py:281
  36.1 1.6 shard_map.155
  37.6 1.1 collective-permute-start.5
  38.7 3.5 %collective-permute-start.4 = (bf16[320,1024]{1,0:T(8,128)(2,1)}, bf16[320,1024]{1,0:T(8,128)(2,1)S(1)}, u32[]{:S(2)}, u32[]{:S(2)}) collective-permute-start(bf16[320,1024]{1,0:T(8,128)(2,1)} %get-tuple-element.35), channel_id=1, source_target_pairs={{0,2},{1,3},{2,0},{3,1},{4,6},{5,7},{6,4},{7,5},{8,10},{9,11},{10,... | collective-permute-start | bytes 1966088 | tf_op jit(solution)/shard_map/ppermute | solution.py:285
  42.2 0.1 collective-permute-start.3
  42.3 0.0 copy-start.1
  42.3 4.9 %all-to-all-start.2 = ((bf16[32,40,1024]{2,1,0:T(8,128)(2,1)}), bf16[32,40,1024]{2,1,0:T(8,128)(2,1)}, u32[]{:S(2)}, u32[]{:S(2)}) async-start(bf16[32,40,1024]{2,1,0:T(8,128)(2,1)} %bitcast.49), calls=%async_computation.2 | async-start | bytes 5242880 | tf_op jit(solution)/shard_map/all_to_all | solution.py:281
  47.3 8.2 %collective-permute-done.5.second_ref = bf16[320,1024]{1,0:T(8,128)(2,1)} collective-permute-done((bf16[320,1024]{1,0:T(8,128)(2,1)}, bf16[320,1024]{1,0:T(8,128)(2,1)}, u32[]{:S(2)}, u32[]{:S(2)}) %collective-permute-start.5) | collective-permute-done | bytes 655392 | tf_op jit(solution)/shard_map/ppermute | solution.py:285
  55.5 0.0 copy-done.1
  55.5 0.0 copy-start.2
  55.5 1.6 copy-done.2
  57.1 8.6 %shard_map.157 = (bf16[4,320,1024]{2,1,0:T(8,128)(2,1)}, f32[4,320,1024]{2,1,0:T(8,128)}, f32[4,320,1024]{2,1,0:T(8,128)}, bf16[4,320,1024]{2,1,0:T(8,128)(2,1)}, bf16[4,1280,256]{2,1,0:T(8,128)(2,1)}) custom-call(s32[1]{0:T(128)} %bitcast.z_ref, bf16[320,1024]{1,0:T(8,128)(2,1)} %get-tuple-element.36.first_ref, ...), custom_call_target="tpu_custom_call" | custom-call | flops 32212254720 | bytes 18087936 | tf_op jit(solution)/shard_map/pallas_call | solution.py:369
  65.7 5.6 %collective-permute-done.4.second_ref = bf16[320,1024]{1,0:T(8,128)(2,1)S(1)} collective-permute-done((bf16[320,1024]{1,0:T(8,128)(2,1)}, bf16[320,1024]{1,0:T(8,128)(2,1)S(1)}, u32[]{:S(2)}, u32[]{:S(2)}) %collective-permute-start.4) | collective-permute-done | bytes 655392 | tf_op jit(solution)/shard_map/ppermute | solution.py:285
  71.3 2.7 %collective-permute-done.3.first_ref = bf16[320,1024]{1,0:T(8,128)(2,1)} collective-permute-done((bf16[320,1024]{1,0:T(8,128)(2,1)}, bf16[320,1024]{1,0:T(8,128)(2,1)}, u32[]{:S(2)}, u32[]{:S(2)}) %collective-permute-start.3) | collective-permute-done | bytes 655392 | tf_op jit(solution)/shard_map/ppermute | solution.py:285
  74.0 8.4 %shard_map.158 = (bf16[4,320,1024]{2,1,0:T(8,128)(2,1)}, f32[4,320,1024]{2,1,0:T(8,128)}, f32[4,320,1024]{2,1,0:T(8,128)}, bf16[4,320,1024]{2,1,0:T(8,128)(2,1)}, bf16[4,1280,256]{2,1,0:T(8,128)(2,1)}) custom-call(s32[1]{0:T(128)} %bitcast.z_ref, ...), custom_call_target="tpu_custom_call", output_to_operand_aliasing={{0}: (7, {}), {1}: (8, {}), {2}: (9, {}), {3}: (10, {}), {4... | custom-call | flops 32212254720 | bytes 18087936 | tf_op jit(solution)/shard_map/pallas_call | solution.py:369
  82.4 0.0 all-to-all-done.2
  82.4 0.0 copy-start.6
  82.4 0.0 copy-start.7
  82.4 6.3 %all-to-all-start.1 = ((bf16[128,40,256]{2,1,0:T(8,128)(2,1)}), bf16[128,40,256]{2,1,0:T(8,128)(2,1)}, u32[]{:S(2)}, u32[]{:S(2)}) async-start(bf16[128,40,256]{2,1,0:T(8,128)(2,1)} %bitcast.51), calls=%async_computation.1 | async-start | bytes 5242880 | tf_op jit(solution)/shard_map/all_to_all | solution.py:281
  88.8 0.0 copy-done.6
  88.8 0.0 copy-done.7
  88.8 0.0 copy-start.3
  88.8 1.6 copy-done.3
  90.4 16.5 %shard_map.160 = (bf16[4,320,1024]{2,1,0:T(8,128)(2,1)}, bf16[4,320,1024]{2,1,0:T(8,128)(2,1)}, bf16[4,320,1024]{2,1,0:T(8,128)(2,1)}, bf16[4,4,320,256]{3,2,1,0:T(8,128)(2,1)}) custom-call(s32[1]{0:T(128)} %bitcast.z_ref, bf16[1280,1024]{1,0:T(8,128)(2,1)} %bitcast.11.moved_ref, f32[4,320,1024]{2,1,0:T(8,128)} %get-tuple-element.46.active_ref, ...), custom_call_target="tpu_custom_call" | custom-call | flops 64424509440 | bytes 29884416 | tf_op jit(solution)/shard_map/pallas_call | solution.py:384
  106.9 17.4 %all-to-all-done.1 = bf16[128,40,256]{2,1,0:T(8,128)(2,1)} async-done(((bf16[128,40,256]{2,1,0:T(8,128)(2,1)}), bf16[128,40,256]{2,1,0:T(8,128)(2,1)}, u32[]{:S(2)}, u32[]{:S(2)}) %all-to-all-start.1) | async-done | bytes 2621472 | tf_op jit(solution)/shard_map/all_to_all | solution.py:281
  124.3 4.7 %all-to-all-start.3 = ((bf16[128,40,256]{2,1,0:T(8,128)(2,1)}), bf16[128,40,256]{2,1,0:T(8,128)(2,1)S(1)}, u32[]{:S(2)}, u32[]{:S(2)}) async-start(bf16[128,40,256]{2,1,0:T(8,128)(2,1)} %bitcast.50), calls=%async_computation.3 | async-start | bytes 5242880 | tf_op jit(solution)/shard_map/all_to_all | solution.py:281
  128.9 0.0 copy-start.9
  128.9 0.0 copy-start.10
  129.0 6.9 %fusion = bf16[1,1024,1024]{2,1,0:T(8,128)(2,1)} fusion(bf16[4,320,1024]{2,1,0:T(8,128)(2,1)} %get-tuple-element.51, bf16[4,320,1024]{2,1,0:T(8,128)(2,1)} %get-tuple-element.52), kind=kOutput, calls=%fused_computation.3 | convolution fusion | flops 2685403136 | bytes 7340032 | tf_op jit(solution)/shard_map/dot_general | solution.py:402
  135.9 0.0 copy-done.9
  135.9 0.0 copy-done.10
  135.9 0.0 copy-start.8
  135.9 0.0 copy-start.11
  135.9 4.1 %fusion.1 = bf16[1,1024,1024]{2,1,0:T(8,128)(2,1)} fusion(bf16[4,320,1024]{2,1,0:T(8,128)(2,1)S(1)} %copy-done.10, bf16[4,320,1024]{2,1,0:T(8,128)(2,1)S(1)} %copy-done.9), kind=kOutput, calls=%fused_computation.4 | convolution fusion | flops 2685403136 | bytes 7340032 | tf_op jit(solution)/shard_map/dot_general | solution.py:403
  140.0 0.0 copy-done.8
  140.0 0.0 copy-done.11
  140.0 0.0 copy-start.4
  140.0 0.0 copy-start.5
  140.0 4.1 %fusion.2 = bf16[1,1024,1024]{2,1,0:T(8,128)(2,1)} fusion(bf16[4,320,1024]{2,1,0:T(8,128)(2,1)S(1)} %copy-done.11, bf16[4,320,1024]{2,1,0:T(8,128)(2,1)S(1)} %copy-done.8), kind=kOutput, calls=%fused_computation.5 | convolution fusion | flops 2685403136 | bytes 7340032 | tf_op jit(solution)/shard_map/dot_general | solution.py:404
  144.2 0.0 copy-done.4
  144.2 0.0 copy-done.5
  144.2 7.0 %shard_map.159 = (bf16[128,1024]{1,0:T(8,128)(2,1)}, f32[4,128]{1,0:T(4,128)}, bf16[128,1280]{1,0:T(8,128)(2,1)S(1)}) custom-call(bf16[5120,256]{1,0:T(8,128)(2,1)} %bitcast.9.back_ref, s32[4,128]{1,0:T(4,128)S(1)} %get-tuple-element.43.target_ref, f32[4,128]{1,0:T(4,128)S(1)} %bitcast.48, bf16[128,1024]{1,0:T(8,128)(2,1)S(1)} %copy-done.4, ...), custom_call_target="tpu_custom_call" | custom-call | flops 1342177280 | bytes 2621440 | tf_op jit(solution)/shard_map/pallas_call | solution.py:406
  151.2 13.8 %all-to-all-done.3 = bf16[128,40,256]{2,1,0:T(8,128)(2,1)S(1)} async-done(((bf16[128,40,256]{2,1,0:T(8,128)(2,1)}), bf16[128,40,256]{2,1,0:T(8,128)(2,1)S(1)}, u32[]{:S(2)}, u32[]{:S(2)}) %all-to-all-start.3) | async-done | bytes 2621472 | tf_op jit(solution)/shard_map/all_to_all | solution.py:281
  165.0 1.9 %shard_map.161 = bf16[128,1024]{1,0:T(8,128)(2,1)} custom-call(bf16[5120,256]{1,0:T(8,128)(2,1)S(1)} %bitcast.39, bf16[128,1280]{1,0:T(8,128)(2,1)S(1)} %get-tuple-element.49.table_ref, bf16[160,160]{1,0:T(8,128)(2,1)S(1)} %copy-done), custom_call_target="tpu_custom_call" | custom-call | flops 335544320 | bytes 2621440 | tf_op jit(solution)/shard_map/pallas_call | solution.py:420
Async XLA Ops:
  0.6 21.3 %copy-start = (bf16[160,160]{1,0:T(8,128)(2,1)S(1)}, bf16[160,160]{1,0:T(8,128)(2,1)}, u32[]{:S(2)}) copy-start(bf16[160,160]{1,0:T(8,128)(2,1)} %constant.10.clone.together.apart.refs_4_) | copy-start | bytes 153604
  3.6 17.5 %collective-permute-start.2 = (bf16[144,1024]{1,0:T(8,128)(2,1)S(1)}, bf16[144,1024]{1,0:T(8,128)(2,1)S(1)}, u32[]{:S(2)}, u32[]{:S(2)}) collective-permute-start(bf16[144,1024]{1,0:T(8,128)(2,1)S(1)} %get-tuple-element.34.refs_0_), channel_id=1, source_target_pairs={{0,3},{1,2},{2,1},{3,0},{4,7},{5,6},{6,5},{7,4},{8,11},{9,10},{10,... | collective-permute-start | bytes 884744 | tf_op jit(solution)/shard_map/ppermute | solution.py:285
  7.8 13.3 %collective-permute-start.1 = (bf16[144,1024]{1,0:T(8,128)(2,1)S(1)}, bf16[144,1024]{1,0:T(8,128)(2,1)S(1)}, u32[]{:S(2)}, u32[]{:S(2)}) collective-permute-start(bf16[144,1024]{1,0:T(8,128)(2,1)S(1)} %get-tuple-element.34.refs_0_), channel_id=1, source_target_pairs={{0,2},{1,3},{2,0},{3,1},{4,6},{5,7},{6,4},{7,5},{8,10},{9,11},{10,... | collective-permute-start | bytes 884744 | tf_op jit(solution)/shard_map/ppermute | solution.py:285
  7.8 14.0 %collective-permute-start = (bf16[144,1024]{1,0:T(8,128)(2,1)S(1)}, bf16[144,1024]{1,0:T(8,128)(2,1)S(1)}, u32[]{:S(2)}, u32[]{:S(2)}) collective-permute-start(bf16[144,1024]{1,0:T(8,128)(2,1)S(1)} %get-tuple-element.34.refs_0_), channel_id=1, source_target_pairs={{0,1},{1,0},{2,3},{3,2},{4,5},{5,4},{6,7},{7,6},{8,9},{9,8},{10,11... | collective-permute-start | bytes 884744 | tf_op jit(solution)/shard_map/ppermute | solution.py:285
  8.8 27.3 %all-to-all-start = ((bf16[32,40,512]{2,1,0:T(8,128)(2,1)}), bf16[32,40,512]{2,1,0:T(8,128)(2,1)S(1)}, u32[]{:S(2)}, u32[]{:S(2)}) async-start(bf16[32,40,512]{2,1,0:T(8,128)(2,1)} %bitcast.52), calls=%async_computation | async-start | bytes 2621440 | tf_op jit(solution)/shard_map/all_to_all | solution.py:281
  37.6 17.9 %collective-permute-start.5 = (bf16[320,1024]{1,0:T(8,128)(2,1)}, bf16[320,1024]{1,0:T(8,128)(2,1)}, u32[]{:S(2)}, u32[]{:S(2)}) collective-permute-start(bf16[320,1024]{1,0:T(8,128)(2,1)} %get-tuple-element.36.first_ref), channel_id=1, source_target_pairs={{0,1},{1,0},{2,3},{3,2},{4,5},{5,4},{6,7},{7,6},{8,9},{9,8},{10,11... | collective-permute-start | bytes 1966088 | tf_op jit(solution)/shard_map/ppermute | solution.py:285
  38.7 32.6 %collective-permute-start.4 = (bf16[320,1024]{1,0:T(8,128)(2,1)}, bf16[320,1024]{1,0:T(8,128)(2,1)S(1)}, u32[]{:S(2)}, u32[]{:S(2)}) collective-permute-start(bf16[320,1024]{1,0:T(8,128)(2,1)} %get-tuple-element.35), channel_id=1, source_target_pairs={{0,2},{1,3},{2,0},{3,1},{4,6},{5,7},{6,4},{7,5},{8,10},{9,11},{10,... | collective-permute-start | bytes 1966088 | tf_op jit(solution)/shard_map/ppermute | solution.py:285
  42.2 31.8 %collective-permute-start.3 = (bf16[320,1024]{1,0:T(8,128)(2,1)}, bf16[320,1024]{1,0:T(8,128)(2,1)}, u32[]{:S(2)}, u32[]{:S(2)}) collective-permute-start(bf16[320,1024]{1,0:T(8,128)(2,1)} %get-tuple-element.35), channel_id=1, source_target_pairs={{0,3},{1,2},{2,1},{3,0},{4,7},{5,6},{6,5},{7,4},{8,11},{9,10},{10,... | collective-permute-start | bytes 1966088 | tf_op jit(solution)/shard_map/ppermute | solution.py:285
  42.3 13.2 %copy-start.1 = (bf16[1,1024,1024]{2,1,0:T(8,128)(2,1)S(1)}, bf16[1,1024,1024]{2,1,0:T(8,128)(2,1)}, u32[]{:S(2)}) copy-start(bf16[1,1024,1024]{2,1,0:T(8,128)(2,1)} %param.14) | copy-start | bytes 6291460
  42.3 40.1 %all-to-all-start.2 = ((bf16[32,40,1024]{2,1,0:T(8,128)(2,1)}), bf16[32,40,1024]{2,1,0:T(8,128)(2,1)}, u32[]{:S(2)}, u32[]{:S(2)}) async-start(bf16[32,40,1024]{2,1,0:T(8,128)(2,1)} %bitcast.49), calls=%async_computation.2 | async-start | bytes 5242880 | tf_op jit(solution)/shard_map/all_to_all | solution.py:281
  55.5 1.6 copy-start.2
  82.4 6.4 %copy-start.6 = (bf16[320,320]{1,0:T(8,128)(2,1)S(1)}, bf16[320,320]{1,0:T(8,128)(2,1)}, u32[]{:S(2)}) copy-start(bf16[320,320]{1,0:T(8,128)(2,1)} %constant.12.clone.together) | copy-start | bytes 614404
  82.4 6.4 %copy-start.7 = (bf16[320,320]{1,0:T(8,128)(2,1)S(1)}, bf16[320,320]{1,0:T(8,128)(2,1)}, u32[]{:S(2)}) copy-start(bf16[320,320]{1,0:T(8,128)(2,1)} %constant.11.clone.apart) | copy-start | bytes 614404
  82.4 41.8 %all-to-all-start.1 = ((bf16[128,40,256]{2,1,0:T(8,128)(2,1)}), bf16[128,40,256]{2,1,0:T(8,128)(2,1)}, u32[]{:S(2)}, u32[]{:S(2)}) async-start(bf16[128,40,256]{2,1,0:T(8,128)(2,1)} %bitcast.51), calls=%async_computation.1 | async-start | bytes 5242880 | tf_op jit(solution)/shard_map/all_to_all | solution.py:281
  88.8 1.6 copy-start.3
  124.3 40.7 %all-to-all-start.3 = ((bf16[128,40,256]{2,1,0:T(8,128)(2,1)}), bf16[128,40,256]{2,1,0:T(8,128)(2,1)S(1)}, u32[]{:S(2)}, u32[]{:S(2)}) async-start(bf16[128,40,256]{2,1,0:T(8,128)(2,1)} %bitcast.50), calls=%async_computation.3 | async-start | bytes 5242880 | tf_op jit(solution)/shard_map/all_to_all | solution.py:281
  128.9 7.0 %copy-start.9 = (bf16[4,320,1024]{2,1,0:T(8,128)(2,1)S(1)}, bf16[4,320,1024]{2,1,0:T(8,128)(2,1)}, u32[]{:S(2)}) copy-start(bf16[4,320,1024]{2,1,0:T(8,128)(2,1)} %get-tuple-element.53) | copy-start | bytes 7864324
  128.9 7.0 %copy-start.10 = (bf16[4,320,1024]{2,1,0:T(8,128)(2,1)S(1)}, bf16[4,320,1024]{2,1,0:T(8,128)(2,1)}, u32[]{:S(2)}) copy-start(bf16[4,320,1024]{2,1,0:T(8,128)(2,1)} %get-tuple-element.51) | copy-start | bytes 7864324
  135.9 4.1 %copy-start.8 = (bf16[4,320,1024]{2,1,0:T(8,128)(2,1)S(1)}, bf16[4,320,1024]{2,1,0:T(8,128)(2,1)}, u32[]{:S(2)}) copy-start(bf16[4,320,1024]{2,1,0:T(8,128)(2,1)} %get-tuple-element.55) | copy-start | bytes 7864324
  135.9 4.1 %copy-start.11 = (bf16[4,320,1024]{2,1,0:T(8,128)(2,1)S(1)}, bf16[4,320,1024]{2,1,0:T(8,128)(2,1)}, u32[]{:S(2)}) copy-start(bf16[4,320,1024]{2,1,0:T(8,128)(2,1)} %get-tuple-element.54) | copy-start | bytes 7864324
  140.0 4.1 %copy-start.4 = (bf16[128,1024]{1,0:T(8,128)(2,1)S(1)}, bf16[128,1024]{1,0:T(8,128)(2,1)}, u32[]{:S(2)}) copy-start(bf16[128,1024]{1,0:T(8,128)(2,1)} %cotangent_ref.3) | copy-start | bytes 786436
  140.0 4.1 %copy-start.5 = (f32[128,4]{0,1:T(4,128)S(1)}, f32[128,4]{0,1:T(4,128)}, u32[]{:S(2)}) copy-start(f32[128,4]{0,1:T(4,128)} %param.13) | copy-start | bytes 6148
